TPU v7x, 32 devices: a whole 2x2x4 slice. The times are simulated.
32 devices in a mesh: gz: 4 (over y, x), gy: 8 (over z, core).
Axes of the slice: x: 2, y: 2, z: 4, core: 2. Of those that a mesh axis runs over, the one named last changes fastest.
Arguments:
- velocity_x: bfloat16 [8, 128, 2048], P('gz', 'gy'), may hold values from -1.5 to 1.5
- velocity_y: bfloat16 [8, 128, 2048], P('gz', 'gy'), may hold values from -1.5 to 1.5
- velocity_z: bfloat16 [8, 128, 2048], P('gz', 'gy'), may hold values from -1.5 to 1.5
- owners: int32 [64, 1], replicated, may hold values from 0 to 7; in each aligned block of 64 rows (0 to 63, 64 to 127, ...) at most 16 rows name the same one
- coupling_below: float32 [8], replicated, may hold values from 0.5 to 2
- coupling_above: float32 [8], replicated, may hold values from 0.5 to 2
- metric: float32 [8], replicated, may hold values from 0.25 to 1
Outputs:
- pressure: float32 [8, 16, 2, 8, 128], P('gy', None, None, 'gz')
Inputs may be any that keep to these rules, and one draw needn't show every extreme that they name: owners[m, 0] is the owner of retained mode kx = m; no owner has more than 16 modes, and some owner has exactly 16.
All inputs are finite; a program needn't handle non-finite values.
Results may differ from a plain program's by a relative error of at most 0.0003.
Values may be sent and summed in bfloat16 or wider, within the bound.
No kernel may reach another device: no remote copies, remote signals or barrier semaphores. Data moves between devices by JAX's collectives and lax.ppermute only.
A program may use at most 64 MiB of HBM per device.

v0:
```python
import math

import jax
import jax.numpy as jnp
from jax import lax
from jax.sharding import PartitionSpec as P

CAP = 16


SMAG_COEF = 0.12
STRAIN_FLOOR = 0.01
BASE_SHIFT = 0.004
MODE_SHIFT = 0.02


def with_halo(array, sides, width):
    for axis, dim in sides:
        size, length = (lax.axis_size(axis), array.shape[dim])
        up = [(i, (i + 1) % size) for i in range(size - 1)]
        down = [(j, i) for i, j in up]
        last = lax.slice_in_dim(array, length - width, length, axis=dim)
        leading = lax.slice_in_dim(array, 0, width, axis=dim)
        before = lax.ppermute(last, axis, up)
        after = lax.ppermute(leading, axis, down)
        array = jnp.concatenate([before, array, after], axis=dim)
    return array


def prefix(array, axis, combine, identity, reverse):
    size, here = (lax.axis_size(axis), lax.axis_index(axis))
    everything = jax.tree.map(lambda part: lax.all_gather(part, axis), array)
    start = jax.tree.map(
        lambda part, zero: jnp.broadcast_to(jnp.asarray(zero, part.dtype), part.shape),
        array,
        identity,
    )

    def turn(k, before):
        at = size - 1 - k if reverse else k
        reached = at > here if reverse else at < here
        new = combine(before, jax.tree.map(lambda part: part[at], everything))
        return jax.tree.map(lambda a, b: jnp.where(reached, a, b), new, before)

    return lax.fori_loop(0, size, turn, start)


def shrink(field):
    return field[1:-1, 1:-1]


def centred_x(field):
    return (jnp.roll(field, -1, 2) - jnp.roll(field, 1, 2)) * 0.5


def slope_x(field):
    return shrink(centred_x(field))


def slope_y(field):
    return (field[1:-1, 2:] - field[1:-1, :-2]) * 0.5


def slope_z(field):
    return (field[2:, 1:-1] - field[:-2, 1:-1]) * 0.5


def second_x(field):
    return shrink(jnp.roll(field, -1, 2) + jnp.roll(field, 1, 2) - 2.0 * field)


def second_y(field):
    return field[1:-1, 2:] + field[1:-1, :-2] - 2.0 * shrink(field)


def second_z(field):
    return field[2:, 1:-1] + field[:-2, 1:-1] - 2.0 * shrink(field)


def mixed_yz(field):
    return 0.25 * (field[2:, 2:] - field[2:, :-2] - field[:-2, 2:] + field[:-2, :-2])


def pressure_source(extended):
    slopes = (slope_x, slope_y, slope_z)
    gradient = [
        [slopes[axis_two](extended[axis_one]) for axis_two in range(3)] for axis_one in range(3)
    ]
    strain = {}
    for axis_one in range(3):
        for axis_two in range(axis_one, 3):
            strain[axis_one, axis_two] = 0.5 * (
                gradient[axis_one][axis_two] + gradient[axis_two][axis_one]
            )
    squared = 2.0 * (
        strain[0, 0] * strain[0, 0] + strain[1, 1] * strain[1, 1] + strain[2, 2] * strain[2, 2]
    )
    squared = squared + 4.0 * (
        strain[0, 1] * strain[0, 1] + strain[0, 2] * strain[0, 2] + strain[1, 2] * strain[1, 2]
    )
    viscous = 2.0 * SMAG_COEF * jnp.sqrt(squared + STRAIN_FLOOR)
    stress = {}
    for pair_key in strain:
        stress[pair_key] = viscous * strain[pair_key]
    divergence = shrink(gradient[0][0] + gradient[1][1] + gradient[2][2])
    forcing = second_x(stress[0, 0]) + second_y(stress[1, 1]) + second_z(stress[2, 2])
    crossed = (
        slope_y(centred_x(stress[0, 1])) + slope_z(centred_x(stress[0, 2])) + mixed_yz(stress[1, 2])
    )
    return divergence + forcing + 2.0 * crossed


def slot_table(owners, groups, capacity):
    owner_of = owners[:, 0]
    one_hot = (owner_of[:, None] == jnp.arange(groups, dtype=jnp.int32)[None, :]).astype(jnp.int32)
    before = jnp.cumsum(one_hot, axis=0) - one_hot
    rank_in = jnp.sum(before * one_hot, axis=1)
    slot_of = owner_of * capacity + rank_in
    matches = slot_of[None, :] == jnp.arange(groups * capacity, dtype=jnp.int32)[:, None]
    mode_ids = jnp.arange(owner_of.shape[0], dtype=jnp.int32)
    slot_mode = jnp.sum(jnp.where(matches, mode_ids[None, :], 0), axis=1)
    return (slot_mode, jnp.any(matches, axis=1))


def chain_combine(before_map, after_map):
    first, second = (after_map, before_map)
    p_aa = first[0] * second[0] + first[1] * second[2]
    p_ab = first[0] * second[1] + first[1] * second[3]
    p_ba = first[2] * second[0] + first[3] * second[2]
    p_bb = first[2] * second[1] + first[3] * second[3]
    real_a = first[4] * second[0] + first[5] * second[2] + first[8] * second[4]
    real_b = first[4] * second[1] + first[5] * second[3] + first[8] * second[5]
    imag_a = first[6] * second[0] + first[7] * second[2] + first[8] * second[6]
    imag_b = first[6] * second[1] + first[7] * second[3] + first[8] * second[7]
    factor = first[8] * second[8]
    largest = jnp.maximum(
        jnp.maximum(jnp.abs(p_aa), jnp.abs(p_ab)), jnp.maximum(jnp.abs(p_ba), jnp.abs(p_bb))
    )
    return (
        jnp.stack([p_aa, p_ab, p_ba, p_bb, real_a, real_b, imag_a, imag_b, factor]) / largest[None]
    )


def affine_combine(before_map, after_map):
    return (after_map[0] * before_map[0], after_map[0][:, None] * before_map[1] + after_map[1])


def per_device(velocity_x, velocity_y, velocity_z, owners, coupling_below, coupling_above, metric):
    groups = lax.axis_size("gy")
    depth, rows, width = velocity_x.shape
    kxr = owners.shape[0]
    kyr = 2 * kxr
    levels = coupling_below.shape[0]
    capacity = CAP
    grid_rows = rows * groups
    stacked = jnp.stack([velocity_x, velocity_y, velocity_z])
    extended = with_halo(stacked, (("gz", 1), ("gy", 2)), 2)
    source = pressure_source(extended.astype(jnp.float32))
    norm_factor = 1.0 / math.sqrt(width * grid_rows)
    kx_all = jnp.arange(kxr, dtype=jnp.int32)
    x_cells = jnp.arange(width, dtype=jnp.int32)
    x_phase = jnp.mod(kx_all[:, None] * x_cells[None, :], width).astype(jnp.float32) * (
        2.0 * math.pi / width
    )
    x_table = jnp.stack(
        [jnp.cos(x_phase) * norm_factor, -jnp.sin(x_phase) * norm_factor], axis=1
    ).reshape(2 * kxr, width)
    flat_rows = source.reshape(depth * rows, width)
    spectra = lax.dot_general(
        x_table,
        flat_rows,
        (((1,), (1,)), ((), ())),
        precision=lax.Precision.HIGHEST,
        preferred_element_type=jnp.float32,
    )
    spectra = spectra.reshape(kxr, 2, depth * rows)
    slot_mode, slot_ok = slot_table(owners, groups, capacity)
    outgoing = jnp.take(spectra, slot_mode, axis=0) * slot_ok[:, None, None].astype(jnp.float32)
    outgoing = outgoing.reshape(groups, 1, capacity, 2, depth * rows)
    block_size = min(8, groups)
    turns = groups // block_size
    ky_all = jnp.arange(kyr, dtype=jnp.int32) - kxr
    received = lax.all_to_all(outgoing, "gy", split_axis=0, concat_axis=1, tiled=True)
    items = received.shape[2]
    blocks = received.reshape(turns, block_size, items, 2, depth, rows)

    def one_turn(totals, entry):
        pieces, turn_pos = entry
        y_cells = (turn_pos * block_size + jnp.arange(block_size, dtype=jnp.int32))[
            :, None
        ] * rows + jnp.arange(rows, dtype=jnp.int32)[None, :]
        phases = jnp.mod(y_cells[:, :, None] * ky_all[None, None, :], grid_rows).astype(
            jnp.float32
        ) * (2.0 * math.pi / grid_rows)
        basis = jnp.stack([jnp.cos(phases), jnp.sin(phases)], axis=2)
        product = jnp.einsum("gmrzy,gyjk->mrzjk", pieces, basis, precision=lax.Precision.HIGHEST)
        real_part = product[:, 0, :, 0] + product[:, 1, :, 1]
        imag_part = product[:, 1, :, 0] - product[:, 0, :, 1]
        return (totals + jnp.stack([real_part, imag_part], axis=1), None)

    start = jnp.zeros((items, 2, depth, kyr), jnp.float32)
    totals, _ = lax.scan(one_turn, start, (blocks, jnp.arange(turns, dtype=jnp.int32)))
    own_index = lax.axis_index("gy")
    own_kx = lax.dynamic_slice_in_dim(slot_mode, own_index * capacity, capacity)
    own_ok = lax.dynamic_slice_in_dim(slot_ok, own_index * capacity, capacity)
    radius = own_kx[:, None] * own_kx[:, None] + ky_all[None, :] * ky_all[None, :]
    inside = (radius <= kxr * kxr) & own_ok[:, None]
    kappa = radius.astype(jnp.float32) / float(kxr * kxr)
    rhs = totals * inside[:, None, None, :].astype(jnp.float32)
    layer_ids = jnp.arange(levels, dtype=jnp.int32)
    below_eff = coupling_below * (layer_ids > 0).astype(jnp.float32)
    above_eff = coupling_above * (layer_ids < levels - 1).astype(jnp.float32)
    above_prev = jnp.concatenate([jnp.zeros((1,), jnp.float32), coupling_above[:-1]])
    base_level = lax.axis_index("gz") * depth
    below_raw_own = lax.dynamic_slice_in_dim(coupling_below, base_level, depth)
    above_raw_own = lax.dynamic_slice_in_dim(coupling_above, base_level, depth)
    below_own = lax.dynamic_slice_in_dim(below_eff, base_level, depth)
    above_own = lax.dynamic_slice_in_dim(above_eff, base_level, depth)
    prev_own = lax.dynamic_slice_in_dim(above_prev, base_level, depth)
    metric_own = lax.dynamic_slice_in_dim(metric, base_level, depth)
    diagonals = [
        -(
            below_raw_own[pos]
            + above_raw_own[pos]
            + metric_own[pos] * (BASE_SHIFT + MODE_SHIFT * kappa)
        )
        for pos in range(depth)
    ]
    ones_mode = jnp.ones((capacity, kyr), jnp.float32)
    zeros_mode = jnp.zeros((capacity, kyr), jnp.float32)
    pivots = []
    values = []
    identity = jnp.stack(
        [
            ones_mode,
            zeros_mode,
            zeros_mode,
            ones_mode,
            zeros_mode,
            zeros_mode,
            zeros_mode,
            zeros_mode,
            ones_mode,
        ]
    )
    composite = identity
    for pos in range(depth):
        coupled = below_own[pos] * prev_own[pos] * ones_mode
        level_map = jnp.stack(
            [
                diagonals[pos],
                -coupled,
                ones_mode,
                zeros_mode,
                rhs[:, 0, pos],
                zeros_mode,
                rhs[:, 1, pos],
                zeros_mode,
                -below_own[pos] * ones_mode,
            ]
        )
        composite = chain_combine(composite, level_map)
    incoming = prefix(composite, "gz", chain_combine, identity, False)
    inverse = incoming[2] / incoming[0]
    term = jnp.stack([incoming[4], incoming[6]], axis=1) / incoming[0][:, None]
    for pos in range(depth):
        pivot = diagonals[pos] - below_own[pos] * prev_own[pos] * inverse
        value = rhs[:, :, pos] - below_own[pos] * term
        inverse = 1.0 / pivot
        term = value * inverse[:, None]
        pivots.append(pivot)
        values.append(value)
    alphas = [-above_own[pos] / pivots[pos] for pos in range(depth)]
    betas = [values[pos] / pivots[pos][:, None] for pos in range(depth)]
    back_identity = (ones_mode, jnp.zeros((capacity, 2, kyr), jnp.float32))
    composite = back_identity
    for pos in range(depth - 1, -1, -1):
        composite = affine_combine(composite, (alphas[pos], betas[pos]))
    incoming = prefix(composite, "gz", affine_combine, back_identity, True)
    current = incoming[1]
    solution = [None] * depth
    for pos in range(depth - 1, -1, -1):
        current = alphas[pos][:, None] * current + betas[pos]
        solution[pos] = current
    return jnp.stack(solution, axis=2)[None]


def solution(mesh):
    placed = (P("gz", "gy", None), P("gz", "gy", None), P("gz", "gy", None), P(), P(), P(), P())
    return jax.shard_map(
        per_device,
        mesh=mesh,
        in_specs=placed,
        out_specs=P("gy", None, None, "gz", None),
        check_vma=False,
    )
```

profile of v0, /device:TPU:0, one launch (start us, length us, event | category | flops | bytes accessed | tf_op | source)
XLA Modules:
  0.0 97.2 jit_solution(4729818196758137681)
XLA Ops:
  0.0 1.1 %pad_maximum_fusion.6 = bf16[3,2,16,2048]{3,2,1,0:T(8,128)(2,1)S(1)} fusion(bf16[1,2,16,2048]{3,2,1,0:T(8,128)(2,1)} %bitcast.277, bf16[1,2,16,2048]{3,2,1,0:T(8,128)(2,1)} %bitcast.280, bf16[1,2,16,2048]{3,2,1,0:T(8,128)(2,1)} %bitcast.283), kind=kLoop, calls=%fused_computation.89 | loop fusion | flops 393216 | bytes 786432 | tf_op jit(solution)/shard_map/stack | solution.py:156
  1.1 4.9 %collective-permute-start = (bf16[3,2,16,2048]{3,2,1,0:T(8,128)(2,1)S(1)}, bf16[3,2,16,2048]{3,2,1,0:T(8,128)(2,1)S(1)}, u32[]{:S(2)}, u32[]{:S(2)}) collective-permute-start(bf16[3,2,16,2048]{3,2,1,0:T(8,128)(2,1)S(1)} %pad_maximum_fusion.6), channel_id=1, source_target_pairs={{0,8},{8,16},{16,24},{1,9},{9,17},{17,25},{2,10},{10,18},{18,26},{... | collective-permute-start | bytes 1179656 | tf_op jit(solution)/shard_map/ppermute | solution.py:24
  6.0 1.3 %collective-permute-start.1 = (bf16[3,2,16,2048]{3,2,1,0:T(8,128)(2,1)S(1)}, bf16[3,2,16,2048]{3,2,1,0:T(8,128)(2,1)S(1)}, u32[]{:S(2)}, u32[]{:S(2)}) collective-permute-start(bf16[3,2,16,2048]{3,2,1,0:T(8,128)(2,1)S(1)} %pad_maximum_fusion.6), channel_id=1, source_target_pairs={{8,0},{16,8},{24,16},{9,1},{17,9},{25,17},{10,2},{18,10},{26,18},{... | collective-permute-start | bytes 1179656 | tf_op jit(solution)/shard_map/ppermute | solution.py:25
  7.3 0.7 fusion.55
  8.2 0.8 select_reduce_fusion.1
  15.7 0.7 dynamic_slice.60
  19.0 0.8 constant_dynamic-update-slice_fusion.17
  19.7 0.8 fusion.80
  20.7 0.8 constant_dynamic-update-slice_fusion.16
  22.5 2.1 %negate_multiply_fusion = (f32[64,1,2048]{2,0,1:T(8,128)S(1)}, f32[64,1,2048]{2,0,1:T(8,128)S(1)}) fusion(), kind=kLoop, calls=%fused_computation.84 | loop fusion | flops 2228224 | bytes 1048576 | tf_op jit(solution)/shard_map/mul | solution.py:166
  25.0 1.4 %collective-permute-start.2 = (bf16[3,6,2,2048]{3,2,1,0:T(2,128)(2,1)S(1)}, bf16[3,6,2,2048]{3,2,1,0:T(2,128)(2,1)S(1)}, u32[]{:S(2)}, u32[]{:S(2)}) collective-permute-start(bf16[3,6,2,2048]{3,2,1,0:T(2,128)(2,1)S(1)} %get-tuple-element.321), channel_id=1, source_target_pairs={{0,1},{1,2},{2,3},{3,4},{4,5},{5,6},{6,7},{8,9},{9,10},{10,11},{11... | collective-permute-start | bytes 442376 | tf_op jit(solution)/shard_map/ppermute | solution.py:24
  26.4 1.3 %collective-permute-start.3 = (bf16[3,6,2,2048]{3,2,1,0:T(2,128)(2,1)S(1)}, bf16[3,6,2,2048]{3,2,1,0:T(2,128)(2,1)S(1)}, u32[]{:S(2)}, u32[]{:S(2)}) collective-permute-start(bf16[3,6,2,2048]{3,2,1,0:T(2,128)(2,1)S(1)} %get-tuple-element.322), channel_id=1, source_target_pairs={{1,0},{2,1},{3,2},{4,3},{5,4},{6,5},{7,6},{9,8},{10,9},{11,10},{12... | collective-permute-start | bytes 442376 | tf_op jit(solution)/shard_map/ppermute | solution.py:25
  32.8 0.9 maximum_convert_fusion
  34.1 0.9 fusion.111
  35.5 3.6 %fusion.24 = (f32[4,18,2048]{2,1,0:T(8,128)S(1)}, f32[4,18,2048]{2,1,0:T(8,128)S(1)}, f32[4,18,2048]{2,1,0:T(8,128)S(1)}, f32[4,18,2048]{2,1,0:T(8,128)S(1)}, f3...) fusion(f32[6,20,2048]{2,1,0:T(8,128)S(1)} %get-tuple-element.30, ...), kind=kLoop, calls=%fused_computation.78 | loop fusion | flops 7372800 | bytes 17694720 | tf_op jit(solution)/shard_map/mul | solution.py:104
  41.9 1.5 %fusion.2 = f32[64,2,32]{0,2,1:T(8,128)S(1)} fusion(f32[32,2048,1]{1,0,2:T(8,128)S(1)} %bitcast.287, f32[64,1,2048]{2,0,1:T(8,128)S(1)} %get-tuple-element.367, f32[64,1,2048]{2,0,1:T(8,128)S(1)} %get-tuple-element.368), kind=kOutput, calls=%fused_computation.35 | convolution fusion | flops 100925440 | bytes 1327104 | tf_op jit(solution)/shard_map/dot_general | solution.py:169
  43.5 0.7 gather_fusion
  44.4 0.7 reshape.1055
  45.1 7.8 %all-to-all-start = ((f32[8,1,1024]{2,1,0:T(1,128)}), f32[8,1,1024]{2,1,0:T(1,128)S(1)}, u32[]{:S(2)}, u32[]{:S(2)}) async-start(f32[8,1,1024]{2,1,0:T(1,128)} %reshape.1055), calls=%async_computation | async-start | bytes 65536 | tf_op jit(solution)/shard_map/all_to_all | solution.py:183
  52.9 5.7 %all-to-all-done = f32[8,1,1024]{2,1,0:T(1,128)S(1)} async-done(((f32[8,1,1024]{2,1,0:T(1,128)}), f32[8,1,1024]{2,1,0:T(1,128)S(1)}, u32[]{:S(2)}, u32[]{:S(2)}) %all-to-all-start) | async-done | bytes 32800 | tf_op jit(solution)/shard_map/all_to_all | solution.py:183
  60.7 0.8 constant_dynamic-update-slice_fusion.26
  61.4 0.8 maximum_bitcast_fusion.4
  62.2 0.8 constant_dynamic-update-slice_fusion.25
  63.1 11.1 %all_gather.12 = f32[4,9,16,128]{3,2,1,0:T(8,128)S(1)} all-gather(f32[1,9,16,128]{3,2,1,0:T(8,128)S(1)} %broadcast_divide_fusion), channel_id=1, replica_groups=mesh['gz'=4,'gy'=8] {'gz'}, dimensions={0}, use_global_device_ids=true | all-gather | bytes 368640 | tf_op jit(solution)/shard_map/all_gather | solution.py:32
  74.1 1.0 while.33
  75.1 0.8 broadcast_divide_fusion.4
  75.9 1.5 %slice_bitcast_fusion.10 = (f32[1,16,1,128]{3,1,2,0:T(8,128)S(1)}, f32[1,16,128]{2,1,0:T(8,128)S(1)}, f32[16,1,128]{2,0,1:T(8,128)S(1)}, f32[16,1,128]{2,0,1:T(8...) fusion(f32[9,16,128]{2,1,0:T(8,128)S(1)} %get-tuple-element.228, f32[]{:T(128)S(6)} %mul.1028, ...), kind=kLoop, calls=%fused_computation.239 | loop fusion | flops 38912 | bytes 82528 | tf_op jit(solution)/shard_map/stack | solution.py:265
  77.3 0.8 broadcast_multiply_fusion
  78.1 1.3 %fusion.68 = f32[1,16,2,128]{3,1,2,0:T(8,128)S(1)} fusion(f32[1,16,1,128]{3,1,2,0:T(8,128)S(1)} %get-tuple-element.344, f32[1,16,1,128]{3,1,2,0:T(8,128)S(1)} %get-tuple-element.340, f32[16,2,2,128]{3,0,2,1:T(8,128)S(1)} %maximum_multiply_fusion, f32[16,128]{1,0:T(8,128)S(1)} %get-tuple-element.294, f32[16,128]{1,0:T(8,128)S(1)} %get-tuple-element.297, ...), kind=kLoop, calls=%fused_computation.184 | loop fusion | flops 49152 | bytes 114696 | tf_op jit(solution)/shard_map/add | solution.py:145
  79.4 7.3 %all_gather.14 = f32[4,16,2,128]{3,1,2,0:T(8,128)S(1)} all-gather(f32[1,16,2,128]{3,1,2,0:T(8,128)S(1)} %fusion.68), channel_id=1, replica_groups=mesh['gz'=4,'gy'=8] {'gz'}, dimensions={0}, use_global_device_ids=true | all-gather | bytes 81920 | tf_op jit(solution)/shard_map/all_gather | solution.py:32
  86.8 8.1 %all_gather.13 = f32[4,16,128]{2,1,0:T(8,128)S(1)} all-gather(f32[1,16,128]{2,1,0:T(8,128)S(1)} %get-tuple-element.341), channel_id=1, replica_groups=mesh['gz'=4,'gy'=8] {'gz'}, dimensions={0}, use_global_device_ids=true | all-gather | bytes 40960 | tf_op jit(solution)/shard_map/all_gather | solution.py:32
  95.2 1.3 %add_bitcast_fusion = (f32[16,2,1,128]{3,0,1,2:T(8,128)S(1)}, f32[16,2,128]{2,0,1:T(8,128)S(1)}) fusion(f32[16,128]{1,0:T(8,128)S(1)} %get-tuple-element.294, f32[16,128]{1,0:T(8,128)S(1)} %get-tuple-element.293, f32[16,128]{1,0:T(8,128)S(1)} %get-tuple-element.345, f32[16,1,128]{2,0,1:T(8,128)S(1)} %get-tuple-element.343, ...), kind=kLoop, calls=%fused_computation.186 | loop fusion | flops 53248 | bytes 147464 | tf_op jit(solution)/shard_map/stack | solution.py:285
  (147 shorter events, 16.0 us)
Async XLA Ops:
  0.0 24.7 %copy-start.3 = (bf16[2,16,2048]{2,1,0:T(8,128)(2,1)S(1)}, bf16[2,16,2048]{2,1,0:T(8,128)(2,1)}, u32[]{:S(2)}) copy-start(bf16[2,16,2048]{2,1,0:T(8,128)(2,1)} %param.11) | copy-start | bytes 393220
  0.0 24.7 %copy-start.2 = (bf16[2,16,2048]{2,1,0:T(8,128)(2,1)S(1)}, bf16[2,16,2048]{2,1,0:T(8,128)(2,1)}, u32[]{:S(2)}) copy-start(bf16[2,16,2048]{2,1,0:T(8,128)(2,1)} %param.12) | copy-start | bytes 393220
  0.0 24.7 %copy-start.1 = (bf16[2,16,2048]{2,1,0:T(8,128)(2,1)S(1)}, bf16[2,16,2048]{2,1,0:T(8,128)(2,1)}, u32[]{:S(2)}) copy-start(bf16[2,16,2048]{2,1,0:T(8,128)(2,1)} %param.13) | copy-start | bytes 393220
  0.0 21.8 %copy-start.4 = (f32[8]{0:T(128)S(1)}, f32[8]{0:T(128)}, u32[]{:S(2)}) copy-start(f32[8]{0:T(128)} %param.16) | copy-start | bytes 100
  1.1 23.5 %collective-permute-start = (bf16[3,2,16,2048]{3,2,1,0:T(8,128)(2,1)S(1)}, bf16[3,2,16,2048]{3,2,1,0:T(8,128)(2,1)S(1)}, u32[]{:S(2)}, u32[]{:S(2)}) collective-permute-start(bf16[3,2,16,2048]{3,2,1,0:T(8,128)(2,1)S(1)} %pad_maximum_fusion.6), channel_id=1, source_target_pairs={{0,8},{8,16},{16,24},{1,9},{9,17},{17,25},{2,10},{10,18},{18,26},{... | collective-permute-start | bytes 1179656 | tf_op jit(solution)/shard_map/ppermute | solution.py:24
  6.0 18.7 %collective-permute-start.1 = (bf16[3,2,16,2048]{3,2,1,0:T(8,128)(2,1)S(1)}, bf16[3,2,16,2048]{3,2,1,0:T(8,128)(2,1)S(1)}, u32[]{:S(2)}, u32[]{:S(2)}) collective-permute-start(bf16[3,2,16,2048]{3,2,1,0:T(8,128)(2,1)S(1)} %pad_maximum_fusion.6), channel_id=1, source_target_pairs={{8,0},{16,8},{24,16},{9,1},{17,9},{25,17},{10,2},{18,10},{26,18},{... | collective-permute-start | bytes 1179656 | tf_op jit(solution)/shard_map/ppermute | solution.py:25
  25.0 7.8 %collective-permute-start.2 = (bf16[3,6,2,2048]{3,2,1,0:T(2,128)(2,1)S(1)}, bf16[3,6,2,2048]{3,2,1,0:T(2,128)(2,1)S(1)}, u32[]{:S(2)}, u32[]{:S(2)}) collective-permute-start(bf16[3,6,2,2048]{3,2,1,0:T(2,128)(2,1)S(1)} %get-tuple-element.321), channel_id=1, source_target_pairs={{0,1},{1,2},{2,3},{3,4},{4,5},{5,6},{6,7},{8,9},{9,10},{10,11},{11... | collective-permute-start | bytes 442376 | tf_op jit(solution)/shard_map/ppermute | solution.py:24
  26.4 6.5 %collective-permute-start.3 = (bf16[3,6,2,2048]{3,2,1,0:T(2,128)(2,1)S(1)}, bf16[3,6,2,2048]{3,2,1,0:T(2,128)(2,1)S(1)}, u32[]{:S(2)}, u32[]{:S(2)}) collective-permute-start(bf16[3,6,2,2048]{3,2,1,0:T(2,128)(2,1)S(1)} %get-tuple-element.322), channel_id=1, source_target_pairs={{1,0},{2,1},{3,2},{4,3},{5,4},{6,5},{7,6},{9,8},{10,9},{11,10},{12... | collective-permute-start | bytes 442376 | tf_op jit(solution)/shard_map/ppermute | solution.py:25
  45.1 13.5 %all-to-all-start = ((f32[8,1,1024]{2,1,0:T(1,128)}), f32[8,1,1024]{2,1,0:T(1,128)S(1)}, u32[]{:S(2)}, u32[]{:S(2)}) async-start(f32[8,1,1024]{2,1,0:T(1,128)} %reshape.1055), calls=%async_computation | async-start | bytes 65536 | tf_op jit(solution)/shard_map/all_to_all | solution.py:183
  52.9 21.2 %copy-start = (f32[9,16,128]{2,1,0:T(8,128)S(1)}, f32[9,16,128]{2,1,0:T(8,128)}, u32[]{:S(2)}) copy-start(f32[9,16,128]{2,1,0:T(8,128)} %constant.179.clone.1) | copy-start | bytes 221188
where the time goes:
time: 97.9 us; the launch traced here: 97.2 us
  blocking collectives  26.5 us (27%)
  other arithmetic  26 us (27%)
  starting transfers between devices  16.6 us (17%)
  local copies, waits for them, and re-layouts  11.7 us (12%)
  between operations  8.13 us (8%)
  waiting for transfers between devices  5.86 us (6%)
  matrix products  1.89 us (2%)
    all_gather x3, blocking collectives, prefix(): everything = jax.tree.map(lambda part: lax.all_gather(part, axis), array)  26.5 us
    all_to_all x1, starting transfers between devices, per_device(): lax.all_to_all(outgoing, 'gy', split_axis=0, concat_axis=1, tiled=True)  7.78 us
    ppermute x2, starting transfers between devices, with_halo(): before = lax.ppermute(last, axis, up)  6.25 us
    all_to_all x1, waiting for transfers between devices, per_device(): lax.all_to_all(outgoing, 'gy', split_axis=0, concat_axis=1, tiled=True)  5.72 us
    mul x2, other arithmetic, pressure_source(): stress[pair_key] = viscous * strain[pair_key]  4.03 us
    unnamed x16, other arithmetic  3.19 us
    ppermute x2, starting transfers between devices, with_halo(): after = lax.ppermute(leading, axis, down)  2.58 us
    slice x8, local copies, waits for them, and re-layouts, centred_x(): return (jnp.roll(field, -1, 2) - jnp.roll(field, 1, 2)) * 0.5  2.18 us
  transfers between devices with their start and end apart: 5, of which 2 were waited for; matrix products, arithmetic and copies ran while one was open for 15% of the time, Pallas kernels for 0%

commit v1 on v0

v1 whole, which is shorter than its diff:
```python
import functools
import math

import jax
import jax.numpy as jnp
import numpy as np
from jax import lax
from jax.experimental import pallas as pl
from jax.experimental.pallas import tpu as pltpu
from jax.sharding import PartitionSpec as P

CAP = 16
SMAG_COEF = 0.12
STRAIN_FLOOR = 0.01
BASE_SHIFT = 0.004
MODE_SHIFT = 0.02

CHUNK = 256
PAD_ROWS = 24
VMEM = pl.BlockSpec(memory_space=pltpu.VMEM)
SMEM = pl.BlockSpec(memory_space=pltpu.SMEM)


def split(value):
    high = value.astype(jnp.bfloat16)
    low = (value - high.astype(jnp.float32)).astype(jnp.bfloat16)
    return high, low


def split_table(table):
    high = table.astype(jnp.bfloat16)
    low = (table - high.astype(np.float64)).astype(jnp.bfloat16)
    return high, low


def matmul(left, right):
    return jnp.dot(left, right, preferred_element_type=jnp.float32)


def x_tables(width, kxr, grid_rows):
    norm = 1.0 / math.sqrt(width * grid_rows)
    phase = (np.arange(width)[:, None] * np.arange(kxr)[None, :] % width) * (2.0 * np.pi / width)
    table = np.stack([np.cos(phase) * norm, -np.sin(phase) * norm], axis=2)
    high, low = split_table(table.reshape(width, 2 * kxr))
    angle = np.arange(kxr) * (2.0 * np.pi / width)
    turn = np.stack([-np.sin(angle), np.sin(angle)], axis=1).reshape(2 * kxr) * 0.5
    second = np.repeat(-4.0 * np.sin(angle * 0.5) ** 2, 2)
    return np.concatenate([high, low], axis=1), np.stack([turn, second]).astype(np.float32)


def y_tables(rows, groups, kyr):
    grid_rows = rows * groups
    offset = np.concatenate([np.arange(rows), [-1, rows]])
    cells = (np.arange(groups)[:, None] * rows + offset[None, :]).reshape(-1)
    ky = np.arange(kyr) - kyr // 2
    phase = (ky[:, None] * cells[None, :] % grid_rows) * (2.0 * np.pi / grid_rows)
    valid = (cells >= 0) & (cells < grid_rows)
    table = np.concatenate([np.cos(phase), np.sin(phase)], axis=0) * valid[None, :]
    return split_table(table)


def mode_kernel(groups, capacity, kyr, levels, depth, own_ref, below, above, metric, pick, green):
    kxr = own_ref.shape[0]
    places, gy = lax.axis_index("gz"), lax.axis_index("gy")
    owner = jnp.broadcast_to(own_ref[...], (kxr, kxr))
    mode = lax.broadcasted_iota(jnp.int32, (kxr, kxr), 0)
    other = lax.broadcasted_iota(jnp.int32, (kxr, kxr), 1)
    owner_f = owner.astype(jnp.float32)
    same = (owner_f == owner_f.T) & (other < mode)
    rank = jnp.sum(jnp.where(same, 1.0, 0.0), axis=1, keepdims=True)
    slot = own_ref[...].astype(jnp.float32) * capacity + rank

    row = lax.broadcasted_iota(jnp.int32, (2 * kxr, groups * capacity * 2), 0)
    column = lax.broadcasted_iota(jnp.int32, (2 * kxr, groups * capacity * 2), 1)
    again = jnp.where(
        lax.broadcasted_iota(jnp.int32, (2 * kxr, kxr), 0) // 2
        == lax.broadcasted_iota(jnp.int32, (2 * kxr, kxr), 1),
        1.0,
        0.0,
    )
    slot_row = jnp.broadcast_to(slot, (kxr, kxr)).T[:1]
    slot_two = jnp.sum(again * slot_row, axis=1, keepdims=True).astype(jnp.int32)
    match = (slot_two * 2 + row % 2) == column
    pick[...] = jnp.where(match, 1.0, 0.0).astype(jnp.bfloat16)

    lane = lax.broadcasted_iota(jnp.int32, (kxr, 128), 1)
    here = gy * capacity + lane % (2 * capacity) // 2
    owned = slot.astype(jnp.int32) == here
    mode_id = lax.broadcasted_iota(jnp.int32, (kxr, 128), 0).astype(jnp.float32)
    kx = jnp.sum(jnp.where(owned, mode_id, 0.0), axis=0, keepdims=True)
    filled = jnp.sum(jnp.where(owned, 1.0, 0.0), axis=0, keepdims=True)

    at = lax.broadcasted_iota(jnp.int32, (8, 128), 1) // (2 * capacity)

    def turn(step, carry):
        start = pl.multiple_of(step * 8, 8)
        ky = (lax.broadcasted_iota(jnp.int32, (8, 128), 0) + (start - kyr // 2)).astype(jnp.float32)
        radius = kx * kx + ky * ky
        inside = jnp.where(radius <= float(kxr * kxr), filled, 0.0)
        shift = BASE_SHIFT + MODE_SHIFT * (radius / float(kxr * kxr))
        inverse = []
        for k in range(levels):
            pivot = -(below[k] + above[k] + metric[k] * shift)
            if k > 0:
                pivot = pivot - below[k] * above[k - 1] * inverse[-1]
            inverse.append(1.0 / pivot)
        for k in range(depth):
            target = places * depth + k
            forward = []
            for pos in range(levels):
                unit = jnp.where(target == pos, 1.0, 0.0)
                value = inside * unit
                if pos > 0:
                    value = value - above[pos - 1] * inverse[pos - 1] * forward[-1]
                forward.append(value)
            weights = [None] * levels
            for pos in range(levels - 1, -1, -1):
                value = forward[pos]
                if pos < levels - 1:
                    value = value - below[pos + 1] * weights[pos + 1]
                weights[pos] = value * inverse[pos]
            for block in range(levels // depth):
                total = jnp.zeros((8, 128), jnp.float32)
                for j in range(depth + 2):
                    pos = block * depth - 1 + j
                    if 0 <= pos < levels:
                        total = jnp.where(at == j, weights[pos], total)
                green[k, block, pl.ds(start, 8), :] = total
        return carry

    lax.fori_loop(0, kyr // 8, turn, 0)


def source_kernel(
    groups, planes, capacity,
    vx, vy, vz, z_low, z_high, y_low, y_high, table, factors, pick,
    out, total, lines,
):
    depth, rows, width = vx.shape
    modes = factors.shape[1]
    gz, gy = lax.axis_index("gz"), lax.axis_index("gy")
    first = jnp.where(gz == 0, 1.0, 0.0)
    last = jnp.where(gz == planes - 1, 1.0, 0.0)
    sub = lax.broadcasted_iota(jnp.int32, (8, CHUNK), 0)
    at_top, at_bottom = sub == 0, sub == 7
    ghost_rows = jnp.where(at_top & (gy == groups - 1) | at_bottom & (gy == 0), SMAG_COEF, 0.0)
    empty = jnp.zeros((8, CHUNK), jnp.float32)
    velocity = (vx, vy, vz)

    def up(field):
        return pltpu.roll(field, PAD_ROWS - 1, 0)

    def down(field):
        return pltpu.roll(field, 1, 0)

    def padded(field):
        return jnp.concatenate([field, empty], axis=0)

    def turn(step, carry):
        here = pl.multiple_of(step * CHUNK, CHUNK)
        before = pl.multiple_of(jnp.where(step == 0, width - 128, here - 128), 128)
        after = pl.multiple_of(jnp.where(step == width // CHUNK - 1, 0, here + CHUNK), 128)
        cells = pl.ds(here, CHUNK)
        rim_low = y_low[:, cells].astype(jnp.float32)
        rim_high = y_high[:, cells].astype(jnp.float32)

        own = [[velocity[i][k, :, cells].astype(jnp.float32) for k in range(depth)] for i in range(3)]
        below = [z_low[i, :, cells].astype(jnp.float32) for i in range(3)]
        above = [z_high[i, :, cells].astype(jnp.float32) for i in range(3)]

        def slope_x(i, k):
            window = jnp.concatenate(
                [
                    velocity[i][k, :, pl.ds(before, 128)].astype(jnp.float32),
                    own[i][k],
                    velocity[i][k, :, pl.ds(after, 128)].astype(jnp.float32),
                ],
                axis=1,
            )
            wide = CHUNK + 256
            difference = pltpu.roll(window, wide - 1, 1) - pltpu.roll(window, 1, 1)
            return difference[:, 128 : 128 + CHUNK]

        def slope_y(i, k):
            at = i * depth + k
            rim = jnp.where(
                at_top, rim_high[at : at + 1], jnp.where(at_bottom, rim_low[at : at + 1], 0.0)
            )
            field = jnp.concatenate([own[i][k], rim], axis=0)
            difference = up(field) - down(field)
            return difference[:rows], difference[rows:]

        def slope_z(i, k):
            lower = below[i] if k == 0 else own[i][k - 1]
            upper = above[i] if k == depth - 1 else own[i][k + 1]
            return upper - lower

        stress = []
        for k in range(depth):
            x = [slope_x(i, k) for i in range(3)]
            y, rim = zip(*[slope_y(i, k) for i in range(3)])
            z = [slope_z(i, k) for i in range(3)]
            e01, e02, e12 = y[0] + x[1], z[0] + x[2], z[1] + y[2]
            squared = 0.5 * (x[0] * x[0] + y[1] * y[1] + z[2] * z[2])
            squared = squared + 0.25 * (e01 * e01 + e02 * e02 + e12 * e12)
            viscous = SMAG_COEF * jnp.sqrt(squared + STRAIN_FLOOR)
            rim_squared = 0.5 * (rim[1] * rim[1]) + 0.25 * (rim[0] * rim[0] + rim[2] * rim[2])
            rim_viscous = ghost_rows * jnp.sqrt(rim_squared + STRAIN_FLOOR)
            s00, s11, s22 = viscous * x[0], viscous * y[1], viscous * z[2]
            t02 = viscous * e02
            t01 = jnp.concatenate([viscous * e01, rim_viscous * rim[0]], axis=0)
            p11 = jnp.concatenate([s11, rim_viscous * rim[1]], axis=0)
            t12 = jnp.concatenate([viscous * e12, rim_viscous * rim[2]], axis=0)
            divergence = 0.5 * (x[0] + y[1] + z[2])
            local = up(p11) + down(p11) + padded(divergence - 2.0 * (s11 + s22))
            cross = 0.25 * (up(t12) - down(t12))
            turned = up(t01) - down(t01)
            stress.append((s00, s22, t02, local, cross, turned))

        rim_u, rim_v, rim_w = [first * own[i][0] - last * own[i][depth - 1] for i in range(3)]
        squared = 0.5 * (rim_w * rim_w) + 0.25 * (rim_u * rim_u + rim_v * rim_v)
        viscous = SMAG_COEF * jnp.sqrt(squared + STRAIN_FLOOR)
        g22, g02, g12 = viscous * rim_w, viscous * rim_u, padded(viscous * rim_v)
        g_cross = 0.25 * (up(g12) - down(g12))
        g22 = padded(g22)

        plain = [None] * (depth + 2)
        turned = [None] * (depth + 2)
        plain[0] = padded(stress[0][1]) + stress[0][4]
        turned[0] = stress[0][2]
        for k in range(depth):
            plain[k + 1] = stress[k][3]
            turned[k + 1] = stress[k][5]
            if k > 0:
                plain[k + 1] = plain[k + 1] + padded(stress[k - 1][1]) - stress[k - 1][4]
                turned[k + 1] = turned[k + 1] - padded(stress[k - 1][2])
            if k < depth - 1:
                plain[k + 1] = plain[k + 1] + padded(stress[k + 1][1]) + stress[k + 1][4]
                turned[k + 1] = turned[k + 1] + padded(stress[k + 1][2])
        plain[1] = plain[1] + first * (g22 - g_cross)
        turned[1] = turned[1] - padded(first * g02)
        plain[depth] = plain[depth] + last * (g22 + g_cross)
        turned[depth] = turned[depth] + padded(last * g02)
        plain[depth + 1] = padded(stress[depth - 1][1]) - stress[depth - 1][4]
        turned[depth + 1] = -stress[depth - 1][2]

        fields = plain + turned + [stress[k][0] for k in range(depth)]
        half = lines.shape[0] // 2
        start = 0
        for field in fields:
            high, low = split(field)
            size = field.shape[0]
            lines[start : start + size, :] = high
            lines[half + start : half + start + size, :] = low
            start += size
        product = matmul(lines[...], table[cells, :])
        total[...] += product[:half] + product[half:]
        return carry

    total[...] = jnp.zeros_like(total)
    lax.fori_loop(0, width // CHUNK, turn, 0)

    summed = total[:, :modes] + total[:, modes:]
    even = lax.broadcasted_iota(jnp.int32, (1, modes), 1) % 2 == 0
    turn_factor, second_factor = factors[0:1], factors[1:2]

    def swapped(field):
        return jnp.where(even, pltpu.roll(field, modes - 1, 1), pltpu.roll(field, 1, 1))

    count = depth + 2
    spectrum = [summed[PAD_ROWS * j : PAD_ROWS * (j + 1)] for j in range(count)]
    start = PAD_ROWS * count
    zero_rows = jnp.zeros((PAD_ROWS - rows, modes), jnp.float32)
    for j in range(count):
        size = rows if j in (0, count - 1) else PAD_ROWS
        field = summed[start : start + size]
        if size == rows:
            field = jnp.concatenate([field, zero_rows], axis=0)
        spectrum[j] = spectrum[j] + turn_factor * swapped(field)
        start += size
    for k in range(depth):
        field = jnp.concatenate([summed[start : start + rows], zero_rows], axis=0)
        spectrum[k + 1] = spectrum[k + 1] + second_factor * field
        start += rows

    stacked = jnp.concatenate(spectrum, axis=0)
    high = stacked.astype(jnp.bfloat16)
    rest = stacked - high.astype(jnp.float32)
    middle, low = split(rest)
    selected = matmul(jnp.concatenate([high, middle, low], axis=0), pick[...])
    size = count * PAD_ROWS
    selected = selected[:size] + selected[size : 2 * size] + selected[2 * size :]

    lane = lax.broadcasted_iota(jnp.int32, (PAD_ROWS, 128), 1)
    share = 2 * capacity
    for half in range(groups * share // 128):
        pieces = [
            selected[PAD_ROWS * j : PAD_ROWS * (j + 1), 128 * half : 128 * (half + 1)]
            for j in range(count)
        ]
        for place in range(128 // share):
            block = jnp.zeros((PAD_ROWS, 128), jnp.float32)
            for j in range(count):
                distance = (share * (j - place)) % 128
                moved = pltpu.roll(pieces[j], distance, 1) if distance else pieces[j]
                block = jnp.where(lane // share == j, moved, block)
            rim = pltpu.roll(block[rows:], 1, 0)
            for plane in range(planes):
                base = (plane * groups + half * (128 // share) + place) * (rows + 2)
                out[base : base + rows, :] = block[:rows]
                out[base + rows : base + rows + 2, :] = rim[:2]


def solve_kernel(kyr, depth, capacity, received, basis_high, basis_low, green, out):
    planes = green.shape[1]
    reach = received.shape[0] // planes
    cosine = [jnp.zeros((kyr, 128), jnp.float32) for _ in range(depth)]
    sine = [jnp.zeros((kyr, 128), jnp.float32) for _ in range(depth)]
    for block in range(planes):
        high, low = split(received[block * reach : (block + 1) * reach, :])
        product = matmul(basis_high[...], high) + matmul(basis_high[...], low)
        product = product + matmul(basis_low[...], high)
        for k in range(depth):
            cosine[k] = cosine[k] + green[k, block] * product[:kyr]
            sine[k] = sine[k] + green[k, block] * product[kyr:]
    lane = lax.broadcasted_iota(jnp.int32, (kyr, 128), 1)
    share = 2 * capacity

    def gathered(field):
        distance = 64
        while distance >= share:
            field = field + pltpu.roll(field, distance, 1)
            distance //= 2
        return field

    result = jnp.zeros((kyr, 128), jnp.float32)
    for k in range(depth):
        real = gathered(cosine[k])
        turned = gathered(sine[k])
        turned = jnp.where(lane % 2 == 0, pltpu.roll(turned, 127, 1), -pltpu.roll(turned, 1, 1))
        result = jnp.where(lane // share == k, real + turned, result)
    flipped = result.T
    for k in range(depth):
        out[:, k, :] = flipped[k * share : (k + 1) * share]


def per_device(groups, planes, velocity_x, velocity_y, velocity_z, owners, below, above, metric):
    depth, rows, width = velocity_x.shape
    kxr = owners.shape[0]
    kyr = 2 * kxr
    levels = below.shape[0]
    limit = pltpu.CompilerParams(vmem_limit_bytes=32 * 1024 * 1024)
    fields = (velocity_x, velocity_y, velocity_z)

    upward = [(i, i + 1) for i in range(planes - 1)]
    sideways = [(i, i + 1) for i in range(groups - 1)]
    back = lambda pairs: [(j, i) for i, j in pairs]
    top = jnp.stack([field[depth - 1] for field in fields])
    bottom = jnp.stack([field[0] for field in fields])
    z_low = lax.ppermute(top, "gz", upward)
    z_high = lax.ppermute(bottom, "gz", back(upward))
    far = jnp.stack([field[:, rows - 1] for field in fields]).reshape(3 * depth, width)
    near = jnp.stack([field[:, 0] for field in fields]).reshape(3 * depth, width)
    y_low = lax.ppermute(far, "gy", sideways)
    y_high = lax.ppermute(near, "gy", back(sideways))

    columns = groups * CAP * 2
    pick, green = pl.pallas_call(
        functools.partial(mode_kernel, groups, CAP, kyr, levels, depth),
        out_shape=(
            jax.ShapeDtypeStruct((2 * kxr, columns), jnp.bfloat16),
            jax.ShapeDtypeStruct((depth, planes, kyr, 128), jnp.float32),
        ),
        in_specs=[VMEM, SMEM, SMEM, SMEM],
        out_specs=(VMEM, VMEM),
        compiler_params=limit,
    )(owners, below, above, metric)

    table, factors = x_tables(width, kxr, rows * groups)
    count = (depth + 2) * PAD_ROWS + depth * PAD_ROWS + (2 + depth) * rows
    reach = rows + 2
    outgoing = pl.pallas_call(
        functools.partial(source_kernel, groups, planes, CAP),
        out_shape=jax.ShapeDtypeStruct((planes * groups * reach, 128), jnp.float32),
        in_specs=[VMEM] * 10,
        out_specs=VMEM,
        scratch_shapes=[
            pltpu.VMEM((count, table.shape[1]), jnp.float32),
            pltpu.VMEM((2 * count, CHUNK), jnp.bfloat16),
        ],
        compiler_params=limit,
    )(*fields, z_low, z_high, y_low, y_high, jnp.asarray(table), jnp.asarray(factors), pick)

    outgoing = outgoing.reshape(planes * groups, reach // 2, 2, 128)
    received = lax.all_to_all(outgoing, ("gz", "gy"), split_axis=0, concat_axis=0, tiled=True)
    received = received.reshape(planes * groups * reach, 128)

    basis_high, basis_low = y_tables(rows, groups, kyr)
    solved = pl.pallas_call(
        functools.partial(solve_kernel, kyr, depth, CAP),
        out_shape=jax.ShapeDtypeStruct((CAP * 2, depth, kyr), jnp.float32),
        in_specs=[VMEM] * 4,
        out_specs=VMEM,
        compiler_params=limit,
    )(received, jnp.asarray(basis_high), jnp.asarray(basis_low), green)
    return solved.reshape(1, CAP, 2, depth, kyr)


def solution(mesh):
    placed = (P("gz", "gy", None), P("gz", "gy", None), P("gz", "gy", None), P(), P(), P(), P())
    return jax.shard_map(
        functools.partial(per_device, mesh.shape["gy"], mesh.shape["gz"]),
        mesh=mesh,
        in_specs=placed,
        out_specs=P("gy", None, None, "gz", None),
        check_vma=False,
    )
```

time: 97.9 us -> 41.5 us (0.42)
  other arithmetic: 26 us -> 0.13 us
  blocking collectives: 26.5 us -> 16 us
  local copies, waits for them, and re-layouts: 11.7 us -> 3.13 us
  between operations: 8.13 us -> 0.28 us
  Pallas kernels: 0 us -> 7.47 us
  starting transfers between devices: 16.6 us -> 9.31 us
  matrix products: 1.89 us -> 0 us
    all_gather x3 -> x0, blocking collectives: 26.5 us -> none  [prefix(): everything = jax.tree.map(lambda part: lax.all_gather(part, axis), array)]
    all_to_all x0 -> x1, blocking collectives: none -> 16 us  [per_device(): lax.all_to_all(outgoing, ('gz', 'gy'), split_axis=0, concat_axis=0, tiled...]
    mul x12 -> x0, other arithmetic: 8.2 us -> none  [the longest x2 4.03 us: pressure_source(): stress[pair_key] = viscous * strain[pair_key]]
    all_to_all x1 -> x0, starting transfers between devices: 7.78 us -> none  [per_device(): lax.all_to_all(outgoing, 'gy', split_axis=0, concat_axis=1, tiled=True)]
    pallas_call x0 -> x3, Pallas kernels: none -> 7.47 us  [the longest x1 3.35 us: per_device(): pl.pallas_call(functools.partial(source_kernel, groups, planes, CAP), out...]
    all_to_all x1 -> x0, waiting for transfers between devices: 5.72 us -> none  [per_device(): lax.all_to_all(outgoing, 'gy', split_axis=0, concat_axis=1, tiled=True)]
    ppermute x4, waiting for transfers between devices: 0.13 us -> 4.9 us  [the longest x1 4.78 us: per_device(): z_high = lax.ppermute(bottom, 'gz', back(upward))]
    another operation x9 -> x4, other arithmetic: 4.07 us -> 0.13 us  [the longest x1 0.04 us: per_device(): jnp.stack([field[:, 0] for field in fields]).reshape(3 * depth, width)]
  transfers between devices with their start and end apart: 5 -> 4, of which waited for: 2 -> 2; matrix products, arithmetic and copies ran while one was open for 15% -> 1% of each run, Pallas kernels for 0% -> 6%
where the time goes in v1:
time: 41.5 us; the launch traced here: 41.2 us
  blocking collectives  16 us (39%)
  starting transfers between devices  9.31 us (22%)
  Pallas kernels  7.47 us (18%)
  waiting for transfers between devices  4.9 us (12%)
  local copies, waits for them, and re-layouts  3.13 us (8%)
    all_to_all x1, blocking collectives, per_device(): lax.all_to_all(outgoing, ('gz', 'gy'), split_axis=0, concat_axis=0, tiled...  16 us
    ppermute x1, waiting for transfers between devices, per_device(): z_high = lax.ppermute(bottom, 'gz', back(upward))  4.78 us
    ppermute x1, starting transfers between devices, per_device(): z_low = lax.ppermute(top, 'gz', upward)  4.24 us
    pallas_call x1, Pallas kernels, per_device(): pl.pallas_call(functools.partial(source_kernel, groups, planes, CAP), out...  3.35 us
    slice x3, local copies, waits for them, and re-layouts, per_device(): field[:, 0]  2.84 us
    pallas_call x1, Pallas kernels, per_device(): pl.pallas_call(functools.partial(mode_kernel, groups, CAP, kyr, levels, d...  2.61 us
    ppermute x1, starting transfers between devices, per_device(): y_low = lax.ppermute(far, 'gy', sideways)  2.36 us
    pallas_call x1, Pallas kernels, per_device(): pl.pallas_call(functools.partial(solve_kernel, kyr, depth, CAP), out_shap...  1.5 us
  transfers between devices with their start and end apart: 4, of which 2 were waited for; matrix products, arithmetic and copies ran while one was open for 1% of the time, Pallas kernels for 6%

profile of v1, /device:TPU:0, one launch (start us, length us, event | category | flops | bytes accessed | tf_op | source)
XLA Modules:
  0.0 41.2 jit_solution(6593797403726486890)
XLA Ops:
  0.0 0.9 %fusion = (bf16[2,1,2048]{2,1,0:T(2,128)(2,1)S(1)}, bf16[2,1,2048]{2,1,0:T(2,128)(2,1)S(1)}) fusion(bf16[2,16,2048]{2,1,0:T(8,128)(2,1)} %vx.1), kind=kLoop, calls=%fused_computation.10 | loop fusion | bytes 32768 | tf_op jit(solution)/shard_map/slice | solution.py:363
  0.9 0.0 copy-start.1
  0.9 0.0 copy-start.2
  0.9 0.0 copy-start.3
  0.9 1.0 %fusion.1 = (bf16[2,1,2048]{2,1,0:T(2,128)(2,1)S(1)}, bf16[2,1,2048]{2,1,0:T(2,128)(2,1)S(1)}) fusion(bf16[2,16,2048]{2,1,0:T(8,128)(2,1)} %vy.1), kind=kLoop, calls=%fused_computation.11 | loop fusion | bytes 32768 | tf_op jit(solution)/shard_map/slice | solution.py:363
  1.9 0.0 copy-start
  1.9 1.0 %fusion.2 = (bf16[2,1,2048]{2,1,0:T(2,128)(2,1)S(1)}, bf16[2,1,2048]{2,1,0:T(2,128)(2,1)S(1)}) fusion(bf16[2,16,2048]{2,1,0:T(8,128)(2,1)} %vz.1), kind=kLoop, calls=%fused_computation.12 | loop fusion | bytes 32768 | tf_op jit(solution)/shard_map/slice | solution.py:363
  3.0 2.4 %collective-permute-start.2 = (bf16[6,2048]{1,0:T(8,128)(2,1)S(1)}, bf16[6,2048]{1,0:T(8,128)(2,1)S(1)}, u32[]{:S(2)}, u32[]{:S(2)}) collective-permute-start(bf16[6,2048]{1,0:T(8,128)(2,1)S(1)} %reshape.15), channel_id=1, source_target_pairs={{0,1},{1,2},{2,3},{3,4},{4,5},{5,6},{6,7},{8,9},{9,10},{10,11},{11... | collective-permute-start | bytes 73736 | tf_op jit(solution)/shard_map/ppermute | solution.py:364
  5.4 0.0 copy-done.1
  5.4 0.0 copy-done.2
  5.5 0.0 copy-done.3
  5.5 4.2 %collective-permute-start = (bf16[3,16,2048]{2,1,0:T(8,128)(2,1)S(1)}, bf16[3,16,2048]{2,1,0:T(8,128)(2,1)S(1)}, u32[]{:S(2)}, u32[]{:S(2)}) collective-permute-start(bf16[3,16,2048]{2,1,0:T(8,128)(2,1)S(1)} %pad_maximum_fusion), channel_id=1, source_target_pairs={{0,8},{8,16},{16,24},{1,9},{9,17},{17,25},{2,10},{10,18},{18,26},{... | collective-permute-start | bytes 589832 | tf_op jit(solution)/shard_map/ppermute | solution.py:360
  9.8 1.3 %collective-permute-start.1 = (bf16[3,16,2048]{2,1,0:T(8,128)(2,1)S(1)}, bf16[3,16,2048]{2,1,0:T(8,128)(2,1)S(1)}, u32[]{:S(2)}, u32[]{:S(2)}) collective-permute-start(bf16[3,16,2048]{2,1,0:T(8,128)(2,1)S(1)} %pad_maximum_fusion.1), channel_id=1, source_target_pairs={{8,0},{16,8},{24,16},{9,1},{17,9},{25,17},{10,2},{18,10},{26,18},{... | collective-permute-start | bytes 589832 | tf_op jit(solution)/shard_map/ppermute | solution.py:361
  11.2 0.0 copy-start.10
  11.2 0.0 copy-start.7
  11.2 0.0 copy-start.8
  11.2 0.0 copy-start.9
  11.2 1.4 %collective-permute-start.3 = (bf16[6,2048]{1,0:T(8,128)(2,1)S(1)}, bf16[6,2048]{1,0:T(8,128)(2,1)S(1)}, u32[]{:S(2)}, u32[]{:S(2)}) collective-permute-start(bf16[6,2048]{1,0:T(8,128)(2,1)S(1)} %reshape.16), channel_id=1, source_target_pairs={{1,0},{2,1},{3,2},{4,3},{5,4},{6,5},{7,6},{9,8},{10,9},{11,10},{12... | collective-permute-start | bytes 73736 | tf_op jit(solution)/shard_map/ppermute | solution.py:365
  12.7 0.0 copy-done.10
  12.7 0.1 copy.21.own_ref
  12.8 2.6 %shard_map.109 = (bf16[128,256]{1,0:T(8,128)(2,1)S(1)}, f32[2,4,128,128]{3,2,1,0:T(8,128)S(1)}) custom-call(s32[64,1]{1,0:T(8,128)S(1)} %copy.21.own_ref, f32[8]{0:T(128)S(1)} %copy-done.7, f32[8]{0:T(128)S(1)} %copy-done.8, f32[8]{0:T(128)S(1)} %copy-done.9), custom_call_target="tpu_custom_call" | custom-call | tf_op jit(solution)/shard_map/pallas_call | solution.py:368
  15.4 0.0 copy-start.6
  15.4 0.0 collective-permute-done.2.y_low
  15.4 0.1 collective-permute-done.3.y_high
  15.5 0.0 collective-permute-done.z_low
  15.5 4.8 %collective-permute-done.1.z_high = bf16[3,16,2048]{2,1,0:T(8,128)(2,1)S(1)} collective-permute-done((bf16[3,16,2048]{2,1,0:T(8,128)(2,1)S(1)}, bf16[3,16,2048]{2,1,0:T(8,128)(2,1)S(1)}, u32[]{:S(2)}, u32[]{:S(2)}) %collective-permute-start.1) | collective-permute-done | bytes 196640 | tf_op jit(solution)/shard_map/ppermute | solution.py:361
  20.3 3.4 %shard_map.110 = f32[576,128]{1,0:T(8,128)S(1)} custom-call(bf16[2,16,2048]{2,1,0:T(8,128)(2,1)S(1)} %copy-done.2, bf16[2,16,2048]{2,1,0:T(8,128)(2,1)S(1)} %copy-done.3, bf16[2,16,2048]{2,1,0:T(8,128)(2,1)S(1)} %copy-done.1, bf16[3,16,2048]{2,1,0:T(8,128)(2,1)S(1)} %collective-permute-done.z_low, bf16[3,16,2048]{2,1,0:T(8,128)(2,1)S(1)} %collective-permute-done.1.z_high, ...), custom_call_target="tpu_custom_call" | custom-call | tf_op jit(solution)/shard_map/pallas_call | solution.py:382
  23.7 0.0 copy-start.4
  23.7 0.0 copy-start.5
  23.7 16.0 %all_to_all.5 = f32[32,9,2,128]{3,2,1,0:T(2,128)S(1)} all-to-all(f32[32,9,2,128]{3,2,1,0:T(2,128)S(1)} %bitcast.15), channel_id=1, replica_groups=mesh['gz'=4,'gy'=8] {'gz','gy'}, dimensions={0} | all-to-all | bytes 589824 | tf_op jit(solution)/shard_map/all_to_all | solution.py:395
  39.7 0.0 copy-done.4
  39.7 1.5 %shard_map.111 = f32[32,2,128]{2,1,0:T(2,128)} custom-call(f32[576,128]{1,0:T(8,128)S(1)} %bitcast.16, bf16[256,144]{1,0:T(8,128)(2,1)S(1)} %copy-done.5, bf16[256,144]{1,0:T(8,128)(2,1)S(1)} %copy-done.4, f32[2,4,128,128]{3,2,1,0:T(8,128)S(1)} %get-tuple-element.8.green), custom_call_target="tpu_custom_call" | custom-call | tf_op jit(solution)/shard_map/pallas_call | solution.py:399
  (17 shorter events, 0.3 us)
Async XLA Ops:
  0.9 4.5 %copy-start.1 = (bf16[2,16,2048]{2,1,0:T(8,128)(2,1)S(1)}, bf16[2,16,2048]{2,1,0:T(8,128)(2,1)}, u32[]{:S(2)}) copy-start(bf16[2,16,2048]{2,1,0:T(8,128)(2,1)} %vz.1) | copy-start | bytes 393220
  0.9 4.5 %copy-start.2 = (bf16[2,16,2048]{2,1,0:T(8,128)(2,1)S(1)}, bf16[2,16,2048]{2,1,0:T(8,128)(2,1)}, u32[]{:S(2)}) copy-start(bf16[2,16,2048]{2,1,0:T(8,128)(2,1)} %vx.1) | copy-start | bytes 393220
  0.9 4.5 %copy-start.3 = (bf16[2,16,2048]{2,1,0:T(8,128)(2,1)S(1)}, bf16[2,16,2048]{2,1,0:T(8,128)(2,1)}, u32[]{:S(2)}) copy-start(bf16[2,16,2048]{2,1,0:T(8,128)(2,1)} %vy.1) | copy-start | bytes 393220
  1.9 18.4 %copy-start = (bf16[2048,256]{1,0:T(8,128)(2,1)S(1)}, bf16[2048,256]{1,0:T(8,128)(2,1)}, u32[]{:S(2)}) copy-start(bf16[2048,256]{1,0:T(8,128)(2,1)} %constant.8.clone.table) | copy-start | bytes 3145732
  3.0 12.4 %collective-permute-start.2 = (bf16[6,2048]{1,0:T(8,128)(2,1)S(1)}, bf16[6,2048]{1,0:T(8,128)(2,1)S(1)}, u32[]{:S(2)}, u32[]{:S(2)}) collective-permute-start(bf16[6,2048]{1,0:T(8,128)(2,1)S(1)} %reshape.15), channel_id=1, source_target_pairs={{0,1},{1,2},{2,3},{3,4},{4,5},{5,6},{6,7},{8,9},{9,10},{10,11},{11... | collective-permute-start | bytes 73736 | tf_op jit(solution)/shard_map/ppermute | solution.py:364
  5.5 10.0 %collective-permute-start = (bf16[3,16,2048]{2,1,0:T(8,128)(2,1)S(1)}, bf16[3,16,2048]{2,1,0:T(8,128)(2,1)S(1)}, u32[]{:S(2)}, u32[]{:S(2)}) collective-permute-start(bf16[3,16,2048]{2,1,0:T(8,128)(2,1)S(1)} %pad_maximum_fusion), channel_id=1, source_target_pairs={{0,8},{8,16},{16,24},{1,9},{9,17},{17,25},{2,10},{10,18},{18,26},{... | collective-permute-start | bytes 589832 | tf_op jit(solution)/shard_map/ppermute | solution.py:360
  9.8 10.5 %collective-permute-start.1 = (bf16[3,16,2048]{2,1,0:T(8,128)(2,1)S(1)}, bf16[3,16,2048]{2,1,0:T(8,128)(2,1)S(1)}, u32[]{:S(2)}, u32[]{:S(2)}) collective-permute-start(bf16[3,16,2048]{2,1,0:T(8,128)(2,1)S(1)} %pad_maximum_fusion.1), channel_id=1, source_target_pairs={{8,0},{16,8},{24,16},{9,1},{17,9},{25,17},{10,2},{18,10},{26,18},{... | collective-permute-start | bytes 589832 | tf_op jit(solution)/shard_map/ppermute | solution.py:361
  11.2 1.5 %copy-start.10 = (s32[64,1]{0,1:T(1,128)S(1)}, s32[64,1]{0,1:T(1,128)}, u32[]{:S(2)}) copy-start(s32[64,1]{0,1:T(1,128)} %param.14) | copy-start | bytes 772
  11.2 1.6 %copy-start.7 = (f32[8]{0:T(128)S(1)}, f32[8]{0:T(128)}, u32[]{:S(2)}) copy-start(f32[8]{0:T(128)} %below.1) | copy-start | bytes 100
  11.2 1.6 %copy-start.8 = (f32[8]{0:T(128)S(1)}, f32[8]{0:T(128)}, u32[]{:S(2)}) copy-start(f32[8]{0:T(128)} %above.1) | copy-start | bytes 100
  11.2 1.6 %copy-start.9 = (f32[8]{0:T(128)S(1)}, f32[8]{0:T(128)}, u32[]{:S(2)}) copy-start(f32[8]{0:T(128)} %metric.1) | copy-start | bytes 100
  11.2 4.3 %collective-permute-start.3 = (bf16[6,2048]{1,0:T(8,128)(2,1)S(1)}, bf16[6,2048]{1,0:T(8,128)(2,1)S(1)}, u32[]{:S(2)}, u32[]{:S(2)}) collective-permute-start(bf16[6,2048]{1,0:T(8,128)(2,1)S(1)} %reshape.16), channel_id=1, source_target_pairs={{1,0},{2,1},{3,2},{4,3},{5,4},{6,5},{7,6},{9,8},{10,9},{11,10},{12... | collective-permute-start | bytes 73736 | tf_op jit(solution)/shard_map/ppermute | solution.py:365
  15.4 4.9 %copy-start.6 = (f32[2,128]{1,0:T(2,128)S(1)}, f32[2,128]{1,0:T(2,128)}, u32[]{:S(2)}) copy-start(f32[2,128]{1,0:T(2,128)} %constant.9.clone.factors) | copy-start | bytes 3076
  23.7 16.0 %copy-start.4 = (bf16[256,144]{1,0:T(8,128)(2,1)S(1)}, bf16[256,144]{1,0:T(8,128)(2,1)}, u32[]{:S(2)}) copy-start(bf16[256,144]{1,0:T(8,128)(2,1)} %constant.11.clone.basis_low) | copy-start | bytes 221188
  23.7 16.0 %copy-start.5 = (bf16[256,144]{1,0:T(8,128)(2,1)S(1)}, bf16[256,144]{1,0:T(8,128)(2,1)}, u32[]{:S(2)}) copy-start(bf16[256,144]{1,0:T(8,128)(2,1)} %constant.10.clone.basis_high) | copy-start | bytes 221188

commit v2 on v1

v2 whole, which is shorter than its diff:
```python
import functools
import math

import jax
import jax.numpy as jnp
import numpy as np
from jax import lax
from jax.experimental import pallas as pl
from jax.experimental.pallas import tpu as pltpu
from jax.sharding import PartitionSpec as P

CAP = 16
SMAG_COEF = 0.12
STRAIN_FLOOR = 0.01
BASE_SHIFT = 0.004
MODE_SHIFT = 0.02

CHUNK = 256
PAD_ROWS = 24
VMEM = pl.BlockSpec(memory_space=pltpu.VMEM)
SMEM = pl.BlockSpec(memory_space=pltpu.SMEM)


def split(value):
    high = value.astype(jnp.bfloat16)
    low = (value - high.astype(jnp.float32)).astype(jnp.bfloat16)
    return high, low


def split_table(table):
    high = table.astype(jnp.bfloat16)
    low = (table - high.astype(np.float64)).astype(jnp.bfloat16)
    return high, low


def matmul(left, right):
    return jnp.dot(left, right, preferred_element_type=jnp.float32)


def x_tables(width, kxr, grid_rows):
    norm = 1.0 / math.sqrt(width * grid_rows)
    phase = (np.arange(width)[:, None] * np.arange(kxr)[None, :] % width) * (2.0 * np.pi / width)
    table = np.stack([np.cos(phase) * norm, -np.sin(phase) * norm], axis=2)
    high, low = split_table(table.reshape(width, 2 * kxr))
    angle = np.arange(kxr) * (2.0 * np.pi / width)
    turn = np.stack([-np.sin(angle), np.sin(angle)], axis=1).reshape(2 * kxr) * 0.5
    second = np.repeat(-4.0 * np.sin(angle * 0.5) ** 2, 2)
    return np.concatenate([high, low], axis=1), np.stack([turn, second]).astype(np.float32)


def y_tables(rows, groups, kyr):
    grid_rows = rows * groups
    offset = np.concatenate([np.arange(rows), [-1, rows]])
    cells = (np.arange(groups)[:, None] * rows + offset[None, :]).reshape(-1)
    ky = np.arange(kyr) - kyr // 2
    phase = (ky[:, None] * cells[None, :] % grid_rows) * (2.0 * np.pi / grid_rows)
    valid = (cells >= 0) & (cells < grid_rows)
    table = np.concatenate([np.cos(phase), np.sin(phase)], axis=0) * valid[None, :]
    return split_table(table)


def mode_kernel(
    groups, capacity, kyr, levels, depth,
    own_ref, below, above, metric, table, pick, green, held, arrived,
):
    copies = []
    part = table.shape[0] // arrived.shape[0]
    for i in range(arrived.shape[0]):
        at = pl.ds(i * part, part)
        copies.append(pltpu.make_async_copy(table.at[at], held.at[at], arrived.at[i]))
        copies[i].start()
    kxr = own_ref.shape[0]
    places, gy = lax.axis_index("gz"), lax.axis_index("gy")
    owner = jnp.broadcast_to(own_ref[...], (kxr, kxr))
    mode = lax.broadcasted_iota(jnp.int32, (kxr, kxr), 0)
    other = lax.broadcasted_iota(jnp.int32, (kxr, kxr), 1)
    owner_f = owner.astype(jnp.float32)
    same = (owner_f == owner_f.T) & (other < mode)
    rank = jnp.sum(jnp.where(same, 1.0, 0.0), axis=1, keepdims=True)
    slot = own_ref[...].astype(jnp.float32) * capacity + rank

    row = lax.broadcasted_iota(jnp.int32, (2 * kxr, groups * capacity * 2), 0)
    column = lax.broadcasted_iota(jnp.int32, (2 * kxr, groups * capacity * 2), 1)
    again = jnp.where(
        lax.broadcasted_iota(jnp.int32, (2 * kxr, kxr), 0) // 2
        == lax.broadcasted_iota(jnp.int32, (2 * kxr, kxr), 1),
        1.0,
        0.0,
    )
    slot_row = jnp.broadcast_to(slot, (kxr, kxr)).T[:1]
    slot_two = jnp.sum(again * slot_row, axis=1, keepdims=True).astype(jnp.int32)
    match = (slot_two * 2 + row % 2) == column
    pick[...] = jnp.where(match, 1.0, 0.0).astype(jnp.bfloat16)

    lane = lax.broadcasted_iota(jnp.int32, (kxr, 128), 1)
    here = gy * capacity + lane % (2 * capacity) // 2
    owned = slot.astype(jnp.int32) == here
    mode_id = lax.broadcasted_iota(jnp.int32, (kxr, 128), 0).astype(jnp.float32)
    kx = jnp.sum(jnp.where(owned, mode_id, 0.0), axis=0, keepdims=True)
    filled = jnp.sum(jnp.where(owned, 1.0, 0.0), axis=0, keepdims=True)

    size = 64
    at = lax.broadcasted_iota(jnp.int32, (size, 128), 1) // (2 * capacity)

    def turn(step, carry):
        start = pl.multiple_of(step * size, size)
        ky = lax.broadcasted_iota(jnp.int32, (size, 128), 0) + (start - kyr // 2)
        ky = ky.astype(jnp.float32)
        radius = kx * kx + ky * ky
        inside = jnp.where(radius <= float(kxr * kxr), filled, 0.0)
        shift = BASE_SHIFT + MODE_SHIFT * (radius / float(kxr * kxr))
        inverse = []
        for k in range(levels):
            pivot = -(below[k] + above[k] + metric[k] * shift)
            if k > 0:
                pivot = pivot - below[k] * above[k - 1] * inverse[-1]
            inverse.append(1.0 / pivot)
        for k in range(depth):
            target = places * depth + k
            forward = []
            for pos in range(levels):
                unit = jnp.where(target == pos, 1.0, 0.0)
                value = inside * unit
                if pos > 0:
                    value = value - above[pos - 1] * inverse[pos - 1] * forward[-1]
                forward.append(value)
            weights = [None] * levels
            for pos in range(levels - 1, -1, -1):
                value = forward[pos]
                if pos < levels - 1:
                    value = value - below[pos + 1] * weights[pos + 1]
                weights[pos] = value * inverse[pos]
            for block in range(levels // depth):
                total = jnp.zeros((size, 128), jnp.float32)
                for j in range(depth + 2):
                    pos = block * depth - 1 + j
                    if 0 <= pos < levels:
                        total = jnp.where(at == j, weights[pos], total)
                green[k, block, pl.ds(start, size), :] = total
        return carry

    lax.fori_loop(0, kyr // size, turn, 0)
    for copy in copies:
        copy.wait()


def pack_kernel(vx, vy, vz, plane_one, plane_two, row_one, row_two, held, arrived):
    rows = vx.shape[1]
    odd, odd_row = lax.axis_index("gz") % 2, lax.axis_index("gy") % 2
    copies = []
    for i, field in enumerate((vx, vy, vz)):
        for k in range(2):
            copies.append(pltpu.make_async_copy(field.at[k], held.at[i, k], arrived.at[i, k]))
    for copy in copies:
        copy.start()
    sub = lax.broadcasted_iota(jnp.int32, (8, vx.shape[2]), 0)
    bottom = jnp.zeros((8, vx.shape[2]), jnp.float32)
    top = bottom
    for i in range(3):
        copies[2 * i].wait()
        copies[2 * i + 1].wait()
        plane_one[i] = held[i, 1 - odd]
        plane_two[i] = held[i, odd]
        for k, level in enumerate((1 - odd, odd)):
            field = held[i, level].astype(jnp.float32)
            bottom = jnp.where(sub == 2 * i + k, field[0:1], bottom)
            top = jnp.where(sub == 2 * i + k, field[rows - 1 : rows], top)
    row_one[...] = jnp.where(odd_row == 0, top, bottom).astype(jnp.bfloat16)
    row_two[...] = jnp.where(odd_row == 0, bottom, top).astype(jnp.bfloat16)


def level_kernel(
    groups, planes, capacity, second,
    vx, vy, vz, plane, row_one, row_two, table, factors, *rest,
):
    if second:
        earlier, pick, out, lines = rest
    else:
        out, lines = rest
    depth, rows, width = vx.shape
    modes = factors.shape[1]
    gz, gy = lax.axis_index("gz"), lax.axis_index("gy")
    first = jnp.where(gz == 0, 1.0, 0.0)
    last = jnp.where(gz == planes - 1, 1.0, 0.0)
    odd, odd_row = gz % 2, gy % 2
    level = odd if second else 1 - odd
    upward = jnp.where(level == 1, 1.0, -1.0)
    sub = lax.broadcasted_iota(jnp.int32, (8, CHUNK), 0)
    at_top, at_bottom = sub == 0, sub == 7
    rim_one = at_top & (odd_row == 0) | at_bottom & (odd_row == 1)
    rim_two = at_top & (odd_row == 1) | at_bottom & (odd_row == 0)
    ghost_rows = jnp.where(at_top & (gy == groups - 1) | at_bottom & (gy == 0), SMAG_COEF, 0.0)
    empty = jnp.zeros((8, CHUNK), jnp.float32)
    velocity = (vx, vy, vz)

    def up(field):
        return pltpu.roll(field, PAD_ROWS - 1, 0)

    def down(field):
        return pltpu.roll(field, 1, 0)

    def padded(field):
        return jnp.concatenate([field, empty], axis=0)

    def turn(step):
        here = step * CHUNK
        before, after = (here - 128) % width, (here + CHUNK) % width
        cells = pl.ds(here, CHUNK)
        rows_one = row_one[:, cells].astype(jnp.float32)
        rows_two = row_two[:, cells].astype(jnp.float32)
        own = [velocity[i][level, :, cells].astype(jnp.float32) for i in range(3)]
        other = [velocity[i][1 - level, :, cells].astype(jnp.float32) for i in range(3)]

        def slope_x(i):
            window = jnp.concatenate(
                [
                    velocity[i][level, :, pl.ds(before, 128)].astype(jnp.float32),
                    own[i],
                    velocity[i][level, :, pl.ds(after, 128)].astype(jnp.float32),
                ],
                axis=1,
            )
            wide = CHUNK + 256
            difference = pltpu.roll(window, wide - 1, 1) - pltpu.roll(window, 1, 1)
            return difference[:, 128 : 128 + CHUNK]

        def slope_y(i):
            at = 2 * i + (1 if second else 0)
            rim = jnp.where(
                rim_one, rows_one[at : at + 1], jnp.where(rim_two, rows_two[at : at + 1], 0.0)
            )
            field = jnp.concatenate([own[i], rim], axis=0)
            difference = up(field) - down(field)
            return difference[:rows], difference[rows:]

        x = [slope_x(i) for i in range(3)]
        y, rim = zip(*[slope_y(i) for i in range(3)])
        z = [upward * (plane[i, :, cells].astype(jnp.float32) - other[i]) for i in range(3)]
        e01, e02, e12 = y[0] + x[1], z[0] + x[2], z[1] + y[2]
        squared = 0.5 * (x[0] * x[0] + y[1] * y[1] + z[2] * z[2])
        squared = squared + 0.25 * (e01 * e01 + e02 * e02 + e12 * e12)
        viscous = SMAG_COEF * jnp.sqrt(squared + STRAIN_FLOOR)
        rim_squared = 0.5 * (rim[1] * rim[1]) + 0.25 * (rim[0] * rim[0] + rim[2] * rim[2])
        rim_viscous = ghost_rows * jnp.sqrt(rim_squared + STRAIN_FLOOR)
        s00, s11, s22 = viscous * x[0], viscous * y[1], viscous * z[2]
        t02 = viscous * e02
        t01 = jnp.concatenate([viscous * e01, rim_viscous * rim[0]], axis=0)
        p11 = jnp.concatenate([s11, rim_viscous * rim[1]], axis=0)
        t12 = jnp.concatenate([viscous * e12, rim_viscous * rim[2]], axis=0)
        divergence = 0.5 * (x[0] + y[1] + z[2])
        local = up(p11) + down(p11) + padded(divergence - 2.0 * (s11 + s22))
        cross = 0.25 * (up(t12) - down(t12))
        turned = up(t01) - down(t01)
        fields = [local, cross, turned, s22, t02, s00]

        if not second:
            edge = first - last
            ghost = [edge * other[i] for i in range(3)]
            squared = 0.5 * (ghost[2] * ghost[2])
            squared = squared + 0.25 * (ghost[0] * ghost[0] + ghost[1] * ghost[1])
            viscous = SMAG_COEF * jnp.sqrt(squared + STRAIN_FLOOR)
            t12 = padded(viscous * ghost[1])
            cross = 0.25 * (up(t12) - down(t12))
            fields = fields + [cross, viscous * ghost[2], viscous * ghost[0]]

        half = lines.shape[0] // 2
        start = 0
        for field in fields:
            high, low = split(field)
            size = field.shape[0]
            lines[start : start + size, cells] = high
            lines[half + start : half + start + size, cells] = low
            start += size

    for step in range(width // CHUNK):
        turn(step)
    half = lines.shape[0] // 2
    product = matmul(lines[...], table[...])
    product = product[:half] + product[half:]
    summed = product[:, :modes] + product[:, modes:]
    even = lax.broadcasted_iota(jnp.int32, (1, modes), 1) % 2 == 0
    zero_rows = jnp.zeros((PAD_ROWS - rows, modes), jnp.float32)

    def slope(field):
        moved = jnp.where(even, pltpu.roll(field, modes - 1, 1), pltpu.roll(field, 1, 1))
        return factors[0:1] * moved

    def taken(start, size):
        field = summed[start : start + size]
        return jnp.concatenate([field, zero_rows], axis=0) if size == rows else field

    local, cross, turned = [taken(PAD_ROWS * i, PAD_ROWS) for i in range(3)]
    s22, t02, s00 = [taken(3 * PAD_ROWS + rows * i, rows) for i in range(3)]
    middle = local + slope(turned) + factors[1:2] * s00
    cross = cross + slope(t02)
    parts = [s22 + cross, middle, s22 - cross]
    if not second:
        start = 3 * PAD_ROWS + 3 * rows
        cross = taken(start, PAD_ROWS) + slope(taken(start + PAD_ROWS + rows, rows))
        parts.append(taken(start + PAD_ROWS, rows) + (last - first) * cross)
        for i, part in enumerate(parts):
            out[PAD_ROWS * i : PAD_ROWS * (i + 1), :] = part
        return

    before = [earlier[PAD_ROWS * i : PAD_ROWS * (i + 1), :] for i in range(4)]
    ghost = before.pop()
    lower = [jnp.where(odd == 1, p, q) for p, q in zip(before, parts)]
    upper = [jnp.where(odd == 1, q, p) for p, q in zip(before, parts)]
    spectrum = [
        lower[0],
        lower[1] + upper[0] + first * ghost,
        lower[2] + upper[1] + last * ghost,
        upper[2],
    ]
    count = len(spectrum)

    stacked = jnp.concatenate(spectrum, axis=0)
    high = stacked.astype(jnp.bfloat16)
    middle, low = split(stacked - high.astype(jnp.float32))
    selected = matmul(jnp.concatenate([high, middle, low], axis=0), pick[...])
    size = count * PAD_ROWS
    selected = selected[:size] + selected[size : 2 * size] + selected[2 * size :]

    lane = lax.broadcasted_iota(jnp.int32, (PAD_ROWS, 128), 1)
    share = 2 * capacity
    for half in range(groups * share // 128):
        pieces = [
            selected[PAD_ROWS * j : PAD_ROWS * (j + 1), 128 * half : 128 * (half + 1)]
            for j in range(count)
        ]
        for place in range(128 // share):
            block = jnp.zeros((PAD_ROWS, 128), jnp.float32)
            for j in range(count):
                distance = (share * (j - place)) % 128
                moved = pltpu.roll(pieces[j], distance, 1) if distance else pieces[j]
                block = jnp.where(lane // share == j, moved, block)
            rim = pltpu.roll(block[rows:], 1, 0)
            for side in range(planes):
                base = (side * groups + half * (128 // share) + place) * (rows + 2)
                out[base : base + rows, :] = block[:rows]
                out[base + rows : base + rows + 2, :] = rim[:2]


def solve_kernel(kyr, depth, capacity, received, basis_high, basis_low, green, out):
    planes = green.shape[1]
    reach = received.shape[0] // planes
    cosine = [jnp.zeros((kyr, 128), jnp.float32) for _ in range(depth)]
    sine = [jnp.zeros((kyr, 128), jnp.float32) for _ in range(depth)]
    for block in range(planes):
        high, low = split(received[block * reach : (block + 1) * reach, :])
        product = matmul(basis_high[...], high) + matmul(basis_high[...], low)
        product = product + matmul(basis_low[...], high)
        for k in range(depth):
            cosine[k] = cosine[k] + green[k, block] * product[:kyr]
            sine[k] = sine[k] + green[k, block] * product[kyr:]
    lane = lax.broadcasted_iota(jnp.int32, (kyr, 128), 1)
    share = 2 * capacity

    def gathered(field):
        distance = 64
        while distance >= share:
            field = field + pltpu.roll(field, distance, 1)
            distance //= 2
        return field

    result = jnp.zeros((kyr, 128), jnp.float32)
    for k in range(depth):
        real = gathered(cosine[k])
        turned = gathered(sine[k])
        turned = jnp.where(lane % 2 == 0, pltpu.roll(turned, 127, 1), -pltpu.roll(turned, 1, 1))
        result = jnp.where(lane // share == k, real + turned, result)
    flipped = result.T
    for k in range(depth):
        out[:, k, :] = flipped[k * share : (k + 1) * share]


def exchange(array, axis, size, shifted):
    pairs = [(i, i + 1) for i in range(shifted, size - 1, 2)]
    return lax.ppermute(array, axis, pairs + [(j, i) for i, j in pairs])


def per_device(groups, planes, velocity_x, velocity_y, velocity_z, owners, below, above, metric):
    depth, rows, width = velocity_x.shape
    kxr = owners.shape[0]
    kyr = 2 * kxr
    levels = below.shape[0]
    limit = pltpu.CompilerParams(vmem_limit_bytes=32 * 1024 * 1024)
    fields = (velocity_x, velocity_y, velocity_z)

    plane_shape = jax.ShapeDtypeStruct((3, rows, width), jnp.bfloat16)
    row_shape = jax.ShapeDtypeStruct((8, width), jnp.bfloat16)
    plane_one, plane_two, row_one, row_two = pl.pallas_call(
        pack_kernel,
        out_shape=(plane_shape, plane_shape, row_shape, row_shape),
        in_specs=[pl.BlockSpec(memory_space=pltpu.HBM)] * 3,
        out_specs=(VMEM,) * 4,
        scratch_shapes=[
            pltpu.VMEM((3, depth, rows, width), jnp.bfloat16),
            pltpu.SemaphoreType.DMA((3, depth)),
        ],
        compiler_params=limit,
    )(*[pltpu.with_memory_space_constraint(field, pltpu.HBM) for field in fields])
    plane_one = exchange(plane_one, "gz", planes, 0)
    plane_two = exchange(plane_two, "gz", planes, 1)
    row_one = exchange(row_one, "gy", groups, 0)
    row_two = exchange(row_two, "gy", groups, 1)

    columns = groups * CAP * 2
    table, factors = [jnp.asarray(array) for array in x_tables(width, kxr, rows * groups)]
    pick, green, table = pl.pallas_call(
        functools.partial(mode_kernel, groups, CAP, kyr, levels, depth),
        out_shape=(
            jax.ShapeDtypeStruct((2 * kxr, columns), jnp.bfloat16),
            jax.ShapeDtypeStruct((depth, planes, kyr, 128), jnp.float32),
            jax.ShapeDtypeStruct(table.shape, table.dtype),
        ),
        in_specs=[VMEM, SMEM, SMEM, SMEM, pl.BlockSpec(memory_space=pltpu.HBM)],
        out_specs=(VMEM, VMEM, VMEM),
        scratch_shapes=[pltpu.SemaphoreType.DMA((4,))],
        compiler_params=limit,
    )(owners, below, above, metric, pltpu.with_memory_space_constraint(table, pltpu.HBM))

    reach = rows + 2

    def level(second, plane, *rest):
        count = 3 * (PAD_ROWS + rows) + (0 if second else PAD_ROWS + 2 * rows)
        out_rows = planes * groups * reach if second else 4 * PAD_ROWS
        return pl.pallas_call(
            functools.partial(level_kernel, groups, planes, CAP, second),
            out_shape=jax.ShapeDtypeStruct((out_rows, 128 if second else 2 * kxr), jnp.float32),
            in_specs=[VMEM] * (8 + len(rest)),
            out_specs=VMEM,
            scratch_shapes=[
                pltpu.VMEM((2 * count, width), jnp.bfloat16),
            ],
            compiler_params=limit,
            cost_estimate=pl.CostEstimate(flops=10**8, bytes_accessed=10**6, transcendentals=0),
        )(*fields, plane, row_one, row_two, table, factors, *rest)

    earlier = level(False, plane_one)
    outgoing = level(True, plane_two, earlier, pick)
    outgoing = outgoing.reshape(planes * groups, reach // 2, 2, 128)
    received = lax.all_to_all(outgoing, ("gz", "gy"), split_axis=0, concat_axis=0, tiled=True)
    received = received.reshape(planes * groups * reach, 128)

    basis_high, basis_low = y_tables(rows, groups, kyr)
    solved = pl.pallas_call(
        functools.partial(solve_kernel, kyr, depth, CAP),
        out_shape=jax.ShapeDtypeStruct((CAP * 2, depth, kyr), jnp.float32),
        in_specs=[VMEM] * 4,
        out_specs=VMEM,
        compiler_params=limit,
    )(received, jnp.asarray(basis_high), jnp.asarray(basis_low), green)
    return solved.reshape(1, CAP, 2, depth, kyr)


def solution(mesh):
    placed = (P("gz", "gy", None), P("gz", "gy", None), P("gz", "gy", None), P(), P(), P(), P())
    return jax.shard_map(
        functools.partial(per_device, mesh.shape["gy"], mesh.shape["gz"]),
        mesh=mesh,
        in_specs=placed,
        out_specs=P("gy", None, None, "gz", None),
        check_vma=False,
    )
```

time: 41.5 us -> 33.7 us (0.81)
  starting transfers between devices: 9.31 us -> 4.53 us
  blocking collectives: 16 us -> 20.1 us
  waiting for transfers between devices: 4.9 us -> 1.28 us
  local copies, waits for them, and re-layouts: 3.13 us -> 0.16 us
    ppermute x4, starting transfers between devices: 9.31 us -> 4.53 us  [exchange(): return lax.ppermute(array, axis, pairs + [(j, i) for i, j in pairs])]
    all_to_all x1, blocking collectives: 16 us -> 20.1 us  [per_device(): lax.all_to_all(outgoing, ('gz', 'gy'), split_axis=0, concat_axis=0, tiled...]
    ppermute x4, waiting for transfers between devices: 4.9 us -> 1.28 us  [exchange(): return lax.ppermute(array, axis, pairs + [(j, i) for i, j in pairs])]
    slice x5 -> x0, local copies, waits for them, and re-layouts: 2.87 us -> none  [the longest x3 2.84 us: per_device(): field[:, 0]]
    pallas_call x1, Pallas kernels: 2.61 us -> 1.83 us  [per_device(): pl.pallas_call(functools.partial(mode_kernel, groups, CAP, kyr, levels, d...]
    pallas_call x1 -> x3, Pallas kernels: 3.35 us -> 3.83 us  [the longest x2 2.74 us: level(): pl.pallas_call(functools.partial(level_kernel, groups, planes, CAP, secon...]
  transfers between devices with their start and end apart: 4 -> 4, of which waited for: 2 -> 1; matrix products, arithmetic and copies ran while one was open for 1% -> 0% of each run, Pallas kernels for 6% -> 10%
where the time goes in v2:
time: 33.7 us; the launch traced here: 33.5 us
  blocking collectives  20.1 us (60%)
  Pallas kernels  7.16 us (21%)
  starting transfers between devices  4.53 us (13%)
  waiting for transfers between devices  1.28 us (4%)
    all_to_all x1, blocking collectives, per_device(): lax.all_to_all(outgoing, ('gz', 'gy'), split_axis=0, concat_axis=0, tiled...  20.1 us
    ppermute x4, starting transfers between devices, exchange(): return lax.ppermute(array, axis, pairs + [(j, i) for i, j in pairs])  4.53 us
    pallas_call x2, Pallas kernels, level(): pl.pallas_call(functools.partial(level_kernel, groups, planes, CAP, secon...  2.74 us
    pallas_call x1, Pallas kernels, per_device(): pl.pallas_call(functools.partial(mode_kernel, groups, CAP, kyr, levels, d...  1.83 us
    pallas_call x1, Pallas kernels, per_device(): pl.pallas_call(functools.partial(solve_kernel, kyr, depth, CAP), out_shap...  1.51 us
    ppermute x4, waiting for transfers between devices, exchange(): return lax.ppermute(array, axis, pairs + [(j, i) for i, j in pairs])  1.28 us
    pallas_call x1, Pallas kernels, per_device(): pl.pallas_call(pack_kernel, out_shape=(plane_shape, plane_shape, row_shap...  1.09 us
  transfers between devices with their start and end apart: 4, of which 1 were waited for; matrix products, arithmetic and copies ran while one was open for 0% of the time, Pallas kernels for 10%

profile of v2, /device:TPU:0, one launch (start us, length us, event | category | flops | bytes accessed | tf_op | source)
XLA Modules:
  0.0 33.5 jit_solution(12263315982586218018)
XLA Ops:
  0.0 1.1 %shard_map.109 = (bf16[3,16,2048]{2,1,0:T(8,128)(2,1)S(1)}, bf16[3,16,2048]{2,1,0:T(8,128)(2,1)S(1)}, bf16[8,2048]{1,0:T(8,128)(2,1)S(1)}, bf16[8,2048]{1,0:T(8,128)(2,1)S(1)}) custom-call(bf16[2,16,2048]{2,1,0:T(8,128)(2,1)} %vx.5, bf16[2,16,2048]{2,1,0:T(8,128)(2,1)} %vy.5, bf16[2,16,2048]{2,1,0:T(8,128)(2,1)} %vz.5), custom_call_target="tpu_custom_call" | custom-call | tf_op jit(solution)/shard_map/pallas_call | solution.py:392
  1.1 3.0 %collective-permute-start.3 = (bf16[3,16,2048]{2,1,0:T(8,128)(2,1)S(1)}, bf16[3,16,2048]{2,1,0:T(8,128)(2,1)S(1)}, u32[]{:S(2)}, u32[]{:S(2)}) collective-permute-start(bf16[3,16,2048]{2,1,0:T(8,128)(2,1)S(1)} %get-tuple-element.16), channel_id=1, source_target_pairs={{0,8},{16,24},{8,0},{24,16},{1,9},{17,25},{9,1},{25,17},{2,10},{18... | collective-permute-start | bytes 589832 | tf_op jit(solution)/shard_map/ppermute | solution.py:379
  4.1 0.7 %collective-permute-start = (bf16[3,16,2048]{2,1,0:T(8,128)(2,1)S(1)}, bf16[3,16,2048]{2,1,0:T(8,128)(2,1)S(1)}, u32[]{:S(2)}, u32[]{:S(2)}) collective-permute-start(bf16[3,16,2048]{2,1,0:T(8,128)(2,1)S(1)} %get-tuple-element.12), channel_id=1, source_target_pairs={{8,16},{16,8},{9,17},{17,9},{10,18},{18,10},{11,19},{19,11},{12,20... | collective-permute-start | bytes 589832 | tf_op jit(solution)/shard_map/ppermute | solution.py:379
  4.8 0.0 copy-start.9
  4.8 0.1 collective-permute-start.1
  4.9 0.0 copy-start.6
  4.9 0.0 copy-start.7
  4.9 0.0 copy-start.8
  4.9 0.8 %collective-permute-start.2 = (bf16[8,2048]{1,0:T(8,128)(2,1)S(1)}, bf16[8,2048]{1,0:T(8,128)(2,1)S(1)}, u32[]{:S(2)}, u32[]{:S(2)}) collective-permute-start(bf16[8,2048]{1,0:T(8,128)(2,1)S(1)} %get-tuple-element.14), channel_id=1, source_target_pairs={{1,2},{3,4},{5,6},{2,1},{4,3},{6,5},{9,10},{11,12},{13,14},{10,9},... | collective-permute-start | bytes 98312 | tf_op jit(solution)/shard_map/ppermute | solution.py:379
  5.7 0.0 copy-done.9
  5.7 0.1 copy.12.own_ref
  5.8 0.0 copy-done.6
  5.8 0.0 copy-done.7
  5.8 0.0 copy-done.8
  5.8 0.0 copy-start
  5.8 0.0 copy-start.1
  5.8 0.0 copy-start.2
  5.9 1.8 %shard_map.110 = (bf16[128,256]{1,0:T(8,128)(2,1)S(1)}, f32[2,4,128,128]{3,2,1,0:T(8,128)S(1)}, bf16[2048,256]{1,0:T(8,128)(2,1)S(1)}) custom-call(s32[64,1]{1,0:T(8,128)S(1)} %copy.12.own_ref, f32[8]{0:T(128)S(1)} %copy-done.6, f32[8]{0:T(128)S(1)} %copy-done.7, f32[8]{0:T(128)S(1)} %copy-done.8, bf16[2048,256]{1,0:T(8,128)(2,1)} %constant.8.clone.table), custom_call_target="tpu_custom_call" | custom-call | tf_op jit(solution)/shard_map/pallas_call | solution.py:410
  7.7 0.0 copy-start.5
  7.7 0.0 collective-permute-done.1.row_one
  7.7 0.0 collective-permute-done.2.row_two
  7.7 1.3 %collective-permute-done.3.plane = bf16[3,16,2048]{2,1,0:T(8,128)(2,1)S(1)} collective-permute-done((bf16[3,16,2048]{2,1,0:T(8,128)(2,1)S(1)}, bf16[3,16,2048]{2,1,0:T(8,128)(2,1)S(1)}, u32[]{:S(2)}, u32[]{:S(2)}) %collective-permute-start.3) | collective-permute-done | bytes 196640 | tf_op jit(solution)/shard_map/ppermute | solution.py:379
  9.0 0.0 copy-done
  9.0 0.0 copy-done.1
  9.0 0.0 copy-done.2
  9.0 1.4 %shard_map.111.rest_0_ = f32[96,128]{1,0:T(8,128)S(1)} custom-call(bf16[2,16,2048]{2,1,0:T(8,128)(2,1)S(1)} %copy-done, bf16[2,16,2048]{2,1,0:T(8,128)(2,1)S(1)} %copy-done.1, bf16[2,16,2048]{2,1,0:T(8,128)(2,1)S(1)} %copy-done.2, bf16[3,16,2048]{2,1,0:T(8,128)(2,1)S(1)} %collective-permute-done.3.plane, bf16[8,2048]{1,0:T(8,128)(2,1)S(1)} %collective-permute-done.1.row_one, ...), custom_call_target="tpu_custom_call" | custom-call | flops 100000000 | bytes 1000000 | tf_op jit(solution)/shard_map/pallas_call | solution.py:428
  10.4 0.0 collective-permute-done.plane
  10.4 1.4 %shard_map.112 = f32[576,128]{1,0:T(8,128)S(1)} custom-call(bf16[2,16,2048]{2,1,0:T(8,128)(2,1)S(1)} %copy-done, bf16[2,16,2048]{2,1,0:T(8,128)(2,1)S(1)} %copy-done.1, bf16[2,16,2048]{2,1,0:T(8,128)(2,1)S(1)} %copy-done.2, bf16[3,16,2048]{2,1,0:T(8,128)(2,1)S(1)} %collective-permute-done.plane, bf16[8,2048]{1,0:T(8,128)(2,1)S(1)} %collective-permute-done.1.row_one, ...), custom_call_target="tpu_custom_call" | custom-call | flops 100000000 | bytes 1000000 | tf_op jit(solution)/shard_map/pallas_call | solution.py:428
  11.8 0.0 copy-start.3
  11.8 0.0 copy-start.4
  11.8 20.1 %all_to_all.5 = f32[32,9,2,128]{3,2,1,0:T(2,128)S(1)} all-to-all(f32[32,9,2,128]{3,2,1,0:T(2,128)S(1)} %bitcast.3), channel_id=1, replica_groups=mesh['gz'=4,'gy'=8] {'gz','gy'}, dimensions={0} | all-to-all | bytes 589824 | tf_op jit(solution)/shard_map/all_to_all | solution.py:443
  32.0 1.5 %shard_map.113 = f32[32,2,128]{2,1,0:T(2,128)} custom-call(f32[576,128]{1,0:T(8,128)S(1)} %bitcast.4, bf16[256,144]{1,0:T(8,128)(2,1)S(1)} %copy-done.4, bf16[256,144]{1,0:T(8,128)(2,1)S(1)} %copy-done.3, f32[2,4,128,128]{3,2,1,0:T(8,128)S(1)} %get-tuple-element.18.green), custom_call_target="tpu_custom_call" | custom-call | tf_op jit(solution)/shard_map/pallas_call | solution.py:447
  (3 shorter events, 0.0 us)
Async XLA Ops:
  1.1 7.9 %collective-permute-start.3 = (bf16[3,16,2048]{2,1,0:T(8,128)(2,1)S(1)}, bf16[3,16,2048]{2,1,0:T(8,128)(2,1)S(1)}, u32[]{:S(2)}, u32[]{:S(2)}) collective-permute-start(bf16[3,16,2048]{2,1,0:T(8,128)(2,1)S(1)} %get-tuple-element.16), channel_id=1, source_target_pairs={{0,8},{16,24},{8,0},{24,16},{1,9},{17,25},{9,1},{25,17},{2,10},{18... | collective-permute-start | bytes 589832 | tf_op jit(solution)/shard_map/ppermute | solution.py:379
  4.1 6.3 %collective-permute-start = (bf16[3,16,2048]{2,1,0:T(8,128)(2,1)S(1)}, bf16[3,16,2048]{2,1,0:T(8,128)(2,1)S(1)}, u32[]{:S(2)}, u32[]{:S(2)}) collective-permute-start(bf16[3,16,2048]{2,1,0:T(8,128)(2,1)S(1)} %get-tuple-element.12), channel_id=1, source_target_pairs={{8,16},{16,8},{9,17},{17,9},{10,18},{18,10},{11,19},{19,11},{12,20... | collective-permute-start | bytes 589832 | tf_op jit(solution)/shard_map/ppermute | solution.py:379
  4.8 0.9 %copy-start.9 = (s32[64,1]{0,1:T(1,128)S(1)}, s32[64,1]{0,1:T(1,128)}, u32[]{:S(2)}) copy-start(s32[64,1]{0,1:T(1,128)} %param.14) | copy-start | bytes 772
  4.8 2.9 %collective-permute-start.1 = (bf16[8,2048]{1,0:T(8,128)(2,1)S(1)}, bf16[8,2048]{1,0:T(8,128)(2,1)S(1)}, u32[]{:S(2)}, u32[]{:S(2)}) collective-permute-start(bf16[8,2048]{1,0:T(8,128)(2,1)S(1)} %get-tuple-element.13), channel_id=1, source_target_pairs={{0,1},{2,3},{4,5},{6,7},{1,0},{3,2},{5,4},{7,6},{8,9},{10,11},{12,... | collective-permute-start | bytes 98312 | tf_op jit(solution)/shard_map/ppermute | solution.py:379
  4.9 0.9 %copy-start.6 = (f32[8]{0:T(128)S(1)}, f32[8]{0:T(128)}, u32[]{:S(2)}) copy-start(f32[8]{0:T(128)} %below.1) | copy-start | bytes 100
  4.9 0.9 %copy-start.7 = (f32[8]{0:T(128)S(1)}, f32[8]{0:T(128)}, u32[]{:S(2)}) copy-start(f32[8]{0:T(128)} %above.1) | copy-start | bytes 100
  4.9 0.9 %copy-start.8 = (f32[8]{0:T(128)S(1)}, f32[8]{0:T(128)}, u32[]{:S(2)}) copy-start(f32[8]{0:T(128)} %metric.1) | copy-start | bytes 100
  4.9 2.8 %collective-permute-start.2 = (bf16[8,2048]{1,0:T(8,128)(2,1)S(1)}, bf16[8,2048]{1,0:T(8,128)(2,1)S(1)}, u32[]{:S(2)}, u32[]{:S(2)}) collective-permute-start(bf16[8,2048]{1,0:T(8,128)(2,1)S(1)} %get-tuple-element.14), channel_id=1, source_target_pairs={{1,2},{3,4},{5,6},{2,1},{4,3},{6,5},{9,10},{11,12},{13,14},{10,9},... | collective-permute-start | bytes 98312 | tf_op jit(solution)/shard_map/ppermute | solution.py:379
  5.8 3.2 %copy-start = (bf16[2,16,2048]{2,1,0:T(8,128)(2,1)S(1)}, bf16[2,16,2048]{2,1,0:T(8,128)(2,1)}, u32[]{:S(2)}) copy-start(bf16[2,16,2048]{2,1,0:T(8,128)(2,1)} %vx.5) | copy-start | bytes 393220
  5.8 3.2 %copy-start.1 = (bf16[2,16,2048]{2,1,0:T(8,128)(2,1)S(1)}, bf16[2,16,2048]{2,1,0:T(8,128)(2,1)}, u32[]{:S(2)}) copy-start(bf16[2,16,2048]{2,1,0:T(8,128)(2,1)} %vy.5) | copy-start | bytes 393220
  5.8 3.2 %copy-start.2 = (bf16[2,16,2048]{2,1,0:T(8,128)(2,1)S(1)}, bf16[2,16,2048]{2,1,0:T(8,128)(2,1)}, u32[]{:S(2)}) copy-start(bf16[2,16,2048]{2,1,0:T(8,128)(2,1)} %vz.5) | copy-start | bytes 393220
  7.7 1.3 %copy-start.5 = (f32[2,128]{1,0:T(2,128)S(1)}, f32[2,128]{1,0:T(2,128)}, u32[]{:S(2)}) copy-start(f32[2,128]{1,0:T(2,128)} %constant.9.clone.factors) | copy-start | bytes 3076
  11.8 20.2 %copy-start.3 = (bf16[256,144]{1,0:T(8,128)(2,1)S(1)}, bf16[256,144]{1,0:T(8,128)(2,1)}, u32[]{:S(2)}) copy-start(bf16[256,144]{1,0:T(8,128)(2,1)} %constant.11.clone.basis_low) | copy-start | bytes 221188
  11.8 20.2 %copy-start.4 = (bf16[256,144]{1,0:T(8,128)(2,1)S(1)}, bf16[256,144]{1,0:T(8,128)(2,1)}, u32[]{:S(2)}) copy-start(bf16[256,144]{1,0:T(8,128)(2,1)} %constant.10.clone.basis_high) | copy-start | bytes 221188

commit v3 on v2

--- a/solution.py
+++ b/solution.py
@@ -17,6 +17,8 @@
 
 CHUNK = 256
 PAD_ROWS = 24
+CODES = 32000.0
+STEPS = 32.0
 VMEM = pl.BlockSpec(memory_space=pltpu.VMEM)
 SMEM = pl.BlockSpec(memory_space=pltpu.SMEM)
 
@@ -50,13 +52,14 @@
 
 def y_tables(rows, groups, kyr):
     grid_rows = rows * groups
-    offset = np.concatenate([np.arange(rows), [-1, rows]])
+    nowhere = -grid_rows
+    offset = np.concatenate([np.arange(rows), [-1, rows, nowhere, nowhere]])
     cells = (np.arange(groups)[:, None] * rows + offset[None, :]).reshape(-1)
     ky = np.arange(kyr) - kyr // 2
     phase = (ky[:, None] * cells[None, :] % grid_rows) * (2.0 * np.pi / grid_rows)
     valid = (cells >= 0) & (cells < grid_rows)
     table = np.concatenate([np.cos(phase), np.sin(phase)], axis=0) * valid[None, :]
-    return split_table(table)
+    return np.concatenate(split_table(table), axis=0)
 
 
 def mode_kernel(
@@ -174,7 +177,7 @@
     vx, vy, vz, plane, row_one, row_two, table, factors, *rest,
 ):
     if second:
-        earlier, pick, out, lines = rest
+        earlier, pick, out, lines, codes = rest
     else:
         out, lines = rest
     depth, rows, width = vx.shape
@@ -322,6 +325,8 @@
     selected = selected[:size] + selected[size : 2 * size] + selected[2 * size :]
 
     lane = lax.broadcasted_iota(jnp.int32, (PAD_ROWS, 128), 1)
+    empty_block = jnp.zeros((PAD_ROWS, 128), jnp.float32)
+    sub_lanes = lax.broadcasted_iota(jnp.int32, (8, 128), 0)
     share = 2 * capacity
     for half in range(groups * share // 128):
         pieces = [
@@ -329,30 +334,46 @@
             for j in range(count)
         ]
         for place in range(128 // share):
-            block = jnp.zeros((PAD_ROWS, 128), jnp.float32)
+            block = empty_block
             for j in range(count):
                 distance = (share * (j - place)) % 128
                 moved = pltpu.roll(pieces[j], distance, 1) if distance else pieces[j]
                 block = jnp.where(lane // share == j, moved, block)
+            largest = jnp.max(jnp.abs(block), axis=0, keepdims=True)
+            power = jnp.floor(jnp.log2(jnp.maximum(largest, 1e-35)) * STEPS) + 1.0
+            block = jnp.floor(block * (CODES * jnp.exp2(power * (-1.0 / STEPS))) + 0.5)
             rim = pltpu.roll(block[rows:], 1, 0)
+            rim = jnp.where(sub_lanes < 2, rim, jnp.where(sub_lanes == 2, power, 0.0))
             for side in range(planes):
-                base = (side * groups + half * (128 // share) + place) * (rows + 2)
-                out[base : base + rows, :] = block[:rows]
-                out[base + rows : base + rows + 2, :] = rim[:2]
-
-
-def solve_kernel(kyr, depth, capacity, received, basis_high, basis_low, green, out):
+                base = (side * groups + half * (128 // share) + place) * (rows + 4)
+                codes[base : base + rows, :] = block[:rows]
+                codes[base + rows : base + rows + 4, :] = rim[:4]
+    out[...] = codes[...].astype(jnp.int32).astype(jnp.int16)
+
+
+def solve_kernel(kyr, depth, capacity, reach, received, basis, green, out, codes):
     planes = green.shape[1]
-    reach = received.shape[0] // planes
+    sources = received.shape[0] // reach
+    codes[...] = received[...].astype(jnp.int32).astype(jnp.float32)
+    power = codes[pl.ds(reach - 2, sources, stride=reach), :]
+    scale = jnp.exp2(power * (1.0 / STEPS)) * (1.0 / CODES)
+    row = lax.broadcasted_iota(jnp.int32, (2 * reach, 128), 0)
+    values = []
+    for pair in range(0, sources, 2):
+        factor = jnp.where(row < reach, scale[pair : pair + 1], scale[pair + 1 : pair + 2])
+        values.append(codes[pair * reach : (pair + 2) * reach, :] * factor)
+    each = sources // planes // 2
+    blocks = [jnp.concatenate(values[i * each : (i + 1) * each], axis=0) for i in range(planes)]
+    high, low = split(jnp.concatenate(blocks, axis=1))
+    product = matmul(basis[...], high)
+    product = product[: 2 * kyr] + product[2 * kyr :] + matmul(basis[: 2 * kyr, :], low)
     cosine = [jnp.zeros((kyr, 128), jnp.float32) for _ in range(depth)]
     sine = [jnp.zeros((kyr, 128), jnp.float32) for _ in range(depth)]
     for block in range(planes):
-        high, low = split(received[block * reach : (block + 1) * reach, :])
-        product = matmul(basis_high[...], high) + matmul(basis_high[...], low)
-        product = product + matmul(basis_low[...], high)
+        lanes = slice(block * 128, (block + 1) * 128)
         for k in range(depth):
-            cosine[k] = cosine[k] + green[k, block] * product[:kyr]
-            sine[k] = sine[k] + green[k, block] * product[kyr:]
+            cosine[k] = cosine[k] + green[k, block] * product[:kyr, lanes]
+            sine[k] = sine[k] + green[k, block] * product[kyr:, lanes]
     lane = lax.broadcasted_iota(jnp.int32, (kyr, 128), 1)
     share = 2 * capacity
 
@@ -420,19 +441,20 @@
         compiler_params=limit,
     )(owners, below, above, metric, pltpu.with_memory_space_constraint(table, pltpu.HBM))
 
-    reach = rows + 2
+    reach = rows + 4
 
     def level(second, plane, *rest):
         count = 3 * (PAD_ROWS + rows) + (0 if second else PAD_ROWS + 2 * rows)
         out_rows = planes * groups * reach if second else 4 * PAD_ROWS
         return pl.pallas_call(
             functools.partial(level_kernel, groups, planes, CAP, second),
-            out_shape=jax.ShapeDtypeStruct((out_rows, 128 if second else 2 * kxr), jnp.float32),
+            out_shape=jax.ShapeDtypeStruct(
+                (out_rows, 128 if second else 2 * kxr), jnp.int16 if second else jnp.float32
+            ),
             in_specs=[VMEM] * (8 + len(rest)),
             out_specs=VMEM,
-            scratch_shapes=[
-                pltpu.VMEM((2 * count, width), jnp.bfloat16),
-            ],
+            scratch_shapes=[pltpu.VMEM((2 * count, width), jnp.bfloat16)]
+            + ([pltpu.VMEM((out_rows, 128), jnp.float32)] if second else []),
             compiler_params=limit,
             cost_estimate=pl.CostEstimate(flops=10**8, bytes_accessed=10**6, transcendentals=0),
         )(*fields, plane, row_one, row_two, table, factors, *rest)
@@ -443,14 +465,15 @@
     received = lax.all_to_all(outgoing, ("gz", "gy"), split_axis=0, concat_axis=0, tiled=True)
     received = received.reshape(planes * groups * reach, 128)
 
-    basis_high, basis_low = y_tables(rows, groups, kyr)
+    basis = jnp.asarray(y_tables(rows, groups, kyr))
     solved = pl.pallas_call(
-        functools.partial(solve_kernel, kyr, depth, CAP),
+        functools.partial(solve_kernel, kyr, depth, CAP, reach),
         out_shape=jax.ShapeDtypeStruct((CAP * 2, depth, kyr), jnp.float32),
-        in_specs=[VMEM] * 4,
+        in_specs=[VMEM] * 3,
         out_specs=VMEM,
+        scratch_shapes=[pltpu.VMEM(received.shape, jnp.float32)],
         compiler_params=limit,
-    )(received, jnp.asarray(basis_high), jnp.asarray(basis_low), green)
+    )(received, basis, green)
     return solved.reshape(1, CAP, 2, depth, kyr)
 
 

time: 33.7 us -> 30.7 us (0.911)
  blocking collectives: 20.1 us -> 17.2 us
    all_to_all x1, blocking collectives: 20.1 us -> 17.2 us  [per_device(): lax.all_to_all(outgoing, ('gz', 'gy'), split_axis=0, concat_axis=0, tiled...]
where the time goes in v3:
time: 30.7 us; the launch traced here: 30.4 us
  blocking collectives  17.2 us (56%)
  Pallas kernels  7.08 us (23%)
  starting transfers between devices  4.53 us (15%)
  waiting for transfers between devices  1.28 us (4%)
    all_to_all x1, blocking collectives, per_device(): lax.all_to_all(outgoing, ('gz', 'gy'), split_axis=0, concat_axis=0, tiled...  17.2 us
    ppermute x4, starting transfers between devices, exchange(): return lax.ppermute(array, axis, pairs + [(j, i) for i, j in pairs])  4.53 us
    pallas_call x2, Pallas kernels, level(): pl.pallas_call(functools.partial(level_kernel, groups, planes, CAP, secon...  2.81 us
    pallas_call x1, Pallas kernels, per_device(): pl.pallas_call(functools.partial(mode_kernel, groups, CAP, kyr, levels, d...  1.83 us
    pallas_call x1, Pallas kernels, per_device(): pl.pallas_call(functools.partial(solve_kernel, kyr, depth, CAP, reach), o...  1.35 us
    ppermute x4, waiting for transfers between devices, exchange(): return lax.ppermute(array, axis, pairs + [(j, i) for i, j in pairs])  1.28 us
    pallas_call x1, Pallas kernels, per_device(): pl.pallas_call(pack_kernel, out_shape=(plane_shape, plane_shape, row_shap...  1.09 us
  transfers between devices with their start and end apart: 4, of which 1 were waited for; matrix products, arithmetic and copies ran while one was open for 0% of the time, Pallas kernels for 10%

profile of v3, /device:TPU:0, one launch (start us, length us, event | category | flops | bytes accessed | tf_op | source)
XLA Modules:
  0.0 30.4 jit_solution(13140384570502588472)
XLA Ops:
  0.0 1.1 %shard_map.100 = (bf16[3,16,2048]{2,1,0:T(8,128)(2,1)S(1)}, bf16[3,16,2048]{2,1,0:T(8,128)(2,1)S(1)}, bf16[8,2048]{1,0:T(8,128)(2,1)S(1)}, bf16[8,2048]{1,0:T(8,128)(2,1)S(1)}) custom-call(bf16[2,16,2048]{2,1,0:T(8,128)(2,1)} %vx.5, bf16[2,16,2048]{2,1,0:T(8,128)(2,1)} %vy.5, bf16[2,16,2048]{2,1,0:T(8,128)(2,1)} %vz.5), custom_call_target="tpu_custom_call" | custom-call | tf_op jit(solution)/shard_map/pallas_call | solution.py:413
  1.1 3.0 %collective-permute-start.3 = (bf16[3,16,2048]{2,1,0:T(8,128)(2,1)S(1)}, bf16[3,16,2048]{2,1,0:T(8,128)(2,1)S(1)}, u32[]{:S(2)}, u32[]{:S(2)}) collective-permute-start(bf16[3,16,2048]{2,1,0:T(8,128)(2,1)S(1)} %get-tuple-element.16), channel_id=1, source_target_pairs={{0,8},{16,24},{8,0},{24,16},{1,9},{17,25},{9,1},{25,17},{2,10},{18... | collective-permute-start | bytes 589832 | tf_op jit(solution)/shard_map/ppermute | solution.py:400
  4.1 0.7 %collective-permute-start = (bf16[3,16,2048]{2,1,0:T(8,128)(2,1)S(1)}, bf16[3,16,2048]{2,1,0:T(8,128)(2,1)S(1)}, u32[]{:S(2)}, u32[]{:S(2)}) collective-permute-start(bf16[3,16,2048]{2,1,0:T(8,128)(2,1)S(1)} %get-tuple-element.12), channel_id=1, source_target_pairs={{8,16},{16,8},{9,17},{17,9},{10,18},{18,10},{11,19},{19,11},{12,20... | collective-permute-start | bytes 589832 | tf_op jit(solution)/shard_map/ppermute | solution.py:400
  4.8 0.0 copy-start.8
  4.8 0.1 collective-permute-start.1
  4.9 0.0 copy-start.5
  4.9 0.0 copy-start.6
  4.9 0.0 copy-start.7
  4.9 0.8 %collective-permute-start.2 = (bf16[8,2048]{1,0:T(8,128)(2,1)S(1)}, bf16[8,2048]{1,0:T(8,128)(2,1)S(1)}, u32[]{:S(2)}, u32[]{:S(2)}) collective-permute-start(bf16[8,2048]{1,0:T(8,128)(2,1)S(1)} %get-tuple-element.14), channel_id=1, source_target_pairs={{1,2},{3,4},{5,6},{2,1},{4,3},{6,5},{9,10},{11,12},{13,14},{10,9},... | collective-permute-start | bytes 98312 | tf_op jit(solution)/shard_map/ppermute | solution.py:400
  5.7 0.0 copy-done.8
  5.7 0.1 copy.11.own_ref
  5.8 0.0 copy-done.5
  5.8 0.0 copy-done.6
  5.8 0.0 copy-done.7
  5.8 0.0 copy-start
  5.8 0.0 copy-start.1
  5.8 0.0 copy-start.2
  5.9 1.8 %shard_map.101 = (bf16[128,256]{1,0:T(8,128)(2,1)S(1)}, f32[2,4,128,128]{3,2,1,0:T(8,128)S(1)}, bf16[2048,256]{1,0:T(8,128)(2,1)S(1)}) custom-call(s32[64,1]{1,0:T(8,128)S(1)} %copy.11.own_ref, f32[8]{0:T(128)S(1)} %copy-done.5, f32[8]{0:T(128)S(1)} %copy-done.6, f32[8]{0:T(128)S(1)} %copy-done.7, bf16[2048,256]{1,0:T(8,128)(2,1)} %constant.6.clone.table), custom_call_target="tpu_custom_call" | custom-call | tf_op jit(solution)/shard_map/pallas_call | solution.py:431
  7.7 0.0 copy-start.4
  7.7 0.0 collective-permute-done.1.row_one
  7.7 0.0 collective-permute-done.2.row_two
  7.7 1.3 %collective-permute-done.3.plane = bf16[3,16,2048]{2,1,0:T(8,128)(2,1)S(1)} collective-permute-done((bf16[3,16,2048]{2,1,0:T(8,128)(2,1)S(1)}, bf16[3,16,2048]{2,1,0:T(8,128)(2,1)S(1)}, u32[]{:S(2)}, u32[]{:S(2)}) %collective-permute-start.3) | collective-permute-done | bytes 196640 | tf_op jit(solution)/shard_map/ppermute | solution.py:400
  9.0 0.0 copy-done
  9.0 0.0 copy-done.1
  9.0 0.0 copy-done.2
  9.0 0.0 copy-done.4
  9.0 1.4 %shard_map.102.rest_0_ = f32[96,128]{1,0:T(8,128)S(1)} custom-call(bf16[2,16,2048]{2,1,0:T(8,128)(2,1)S(1)} %copy-done, bf16[2,16,2048]{2,1,0:T(8,128)(2,1)S(1)} %copy-done.1, bf16[2,16,2048]{2,1,0:T(8,128)(2,1)S(1)} %copy-done.2, bf16[3,16,2048]{2,1,0:T(8,128)(2,1)S(1)} %collective-permute-done.3.plane, bf16[8,2048]{1,0:T(8,128)(2,1)S(1)} %collective-permute-done.1.row_one, ...), custom_call_target="tpu_custom_call" | custom-call | flops 100000000 | bytes 1000000 | tf_op jit(solution)/shard_map/pallas_call | solution.py:449
  10.4 0.0 collective-permute-done.plane
  10.4 1.4 %shard_map.103 = s16[640,128]{1,0:T(8,128)(2,1)S(1)} custom-call(bf16[2,16,2048]{2,1,0:T(8,128)(2,1)S(1)} %copy-done, bf16[2,16,2048]{2,1,0:T(8,128)(2,1)S(1)} %copy-done.1, bf16[2,16,2048]{2,1,0:T(8,128)(2,1)S(1)} %copy-done.2, bf16[3,16,2048]{2,1,0:T(8,128)(2,1)S(1)} %collective-permute-done.plane, bf16[8,2048]{1,0:T(8,128)(2,1)S(1)} %collective-permute-done.1.row_one, ...), custom_call_target="tpu_custom_call" | custom-call | flops 100000000 | bytes 1000000 | tf_op jit(solution)/shard_map/pallas_call | solution.py:449
  11.9 0.0 copy-start.3
  11.9 17.2 %all_to_all.5 = s16[32,10,2,128]{3,2,1,0:T(2,128)(2,1)S(1)} all-to-all(s16[32,10,2,128]{3,2,1,0:T(2,128)(2,1)S(1)} %bitcast.3), channel_id=1, replica_groups=mesh['gz'=4,'gy'=8] {'gz','gy'}, dimensions={0} | all-to-all | bytes 327680 | tf_op jit(solution)/shard_map/all_to_all | solution.py:465
  29.0 1.4 %shard_map.104 = f32[32,2,128]{2,1,0:T(2,128)} custom-call(s16[640,128]{1,0:T(8,128)(2,1)S(1)} %bitcast.4, bf16[512,160]{1,0:T(8,128)(2,1)S(1)} %copy-done.3, f32[2,4,128,128]{3,2,1,0:T(8,128)S(1)} %get-tuple-element.18.green), custom_call_target="tpu_custom_call" | custom-call | tf_op jit(solution)/shard_map/pallas_call | solution.py:469
  (1 shorter events, 0.0 us)
Async XLA Ops:
  1.1 7.9 %collective-permute-start.3 = (bf16[3,16,2048]{2,1,0:T(8,128)(2,1)S(1)}, bf16[3,16,2048]{2,1,0:T(8,128)(2,1)S(1)}, u32[]{:S(2)}, u32[]{:S(2)}) collective-permute-start(bf16[3,16,2048]{2,1,0:T(8,128)(2,1)S(1)} %get-tuple-element.16), channel_id=1, source_target_pairs={{0,8},{16,24},{8,0},{24,16},{1,9},{17,25},{9,1},{25,17},{2,10},{18... | collective-permute-start | bytes 589832 | tf_op jit(solution)/shard_map/ppermute | solution.py:400
  4.1 6.3 %collective-permute-start = (bf16[3,16,2048]{2,1,0:T(8,128)(2,1)S(1)}, bf16[3,16,2048]{2,1,0:T(8,128)(2,1)S(1)}, u32[]{:S(2)}, u32[]{:S(2)}) collective-permute-start(bf16[3,16,2048]{2,1,0:T(8,128)(2,1)S(1)} %get-tuple-element.12), channel_id=1, source_target_pairs={{8,16},{16,8},{9,17},{17,9},{10,18},{18,10},{11,19},{19,11},{12,20... | collective-permute-start | bytes 589832 | tf_op jit(solution)/shard_map/ppermute | solution.py:400
  4.8 0.9 %copy-start.8 = (s32[64,1]{0,1:T(1,128)S(1)}, s32[64,1]{0,1:T(1,128)}, u32[]{:S(2)}) copy-start(s32[64,1]{0,1:T(1,128)} %param.13) | copy-start | bytes 772
  4.8 2.9 %collective-permute-start.1 = (bf16[8,2048]{1,0:T(8,128)(2,1)S(1)}, bf16[8,2048]{1,0:T(8,128)(2,1)S(1)}, u32[]{:S(2)}, u32[]{:S(2)}) collective-permute-start(bf16[8,2048]{1,0:T(8,128)(2,1)S(1)} %get-tuple-element.13), channel_id=1, source_target_pairs={{0,1},{2,3},{4,5},{6,7},{1,0},{3,2},{5,4},{7,6},{8,9},{10,11},{12,... | collective-permute-start | bytes 98312 | tf_op jit(solution)/shard_map/ppermute | solution.py:400
  4.9 0.9 %copy-start.5 = (f32[8]{0:T(128)S(1)}, f32[8]{0:T(128)}, u32[]{:S(2)}) copy-start(f32[8]{0:T(128)} %below.1) | copy-start | bytes 100
  4.9 0.9 %copy-start.6 = (f32[8]{0:T(128)S(1)}, f32[8]{0:T(128)}, u32[]{:S(2)}) copy-start(f32[8]{0:T(128)} %above.1) | copy-start | bytes 100
  4.9 0.9 %copy-start.7 = (f32[8]{0:T(128)S(1)}, f32[8]{0:T(128)}, u32[]{:S(2)}) copy-start(f32[8]{0:T(128)} %metric.1) | copy-start | bytes 100
  4.9 2.8 %collective-permute-start.2 = (bf16[8,2048]{1,0:T(8,128)(2,1)S(1)}, bf16[8,2048]{1,0:T(8,128)(2,1)S(1)}, u32[]{:S(2)}, u32[]{:S(2)}) collective-permute-start(bf16[8,2048]{1,0:T(8,128)(2,1)S(1)} %get-tuple-element.14), channel_id=1, source_target_pairs={{1,2},{3,4},{5,6},{2,1},{4,3},{6,5},{9,10},{11,12},{13,14},{10,9},... | collective-permute-start | bytes 98312 | tf_op jit(solution)/shard_map/ppermute | solution.py:400
  5.8 3.2 %copy-start = (bf16[2,16,2048]{2,1,0:T(8,128)(2,1)S(1)}, bf16[2,16,2048]{2,1,0:T(8,128)(2,1)}, u32[]{:S(2)}) copy-start(bf16[2,16,2048]{2,1,0:T(8,128)(2,1)} %vx.5) | copy-start | bytes 393220
  5.8 3.2 %copy-start.1 = (bf16[2,16,2048]{2,1,0:T(8,128)(2,1)S(1)}, bf16[2,16,2048]{2,1,0:T(8,128)(2,1)}, u32[]{:S(2)}) copy-start(bf16[2,16,2048]{2,1,0:T(8,128)(2,1)} %vy.5) | copy-start | bytes 393220
  5.8 3.2 %copy-start.2 = (bf16[2,16,2048]{2,1,0:T(8,128)(2,1)S(1)}, bf16[2,16,2048]{2,1,0:T(8,128)(2,1)}, u32[]{:S(2)}) copy-start(bf16[2,16,2048]{2,1,0:T(8,128)(2,1)} %vz.5) | copy-start | bytes 393220
  7.7 1.3 %copy-start.4 = (f32[2,128]{1,0:T(2,128)S(1)}, f32[2,128]{1,0:T(2,128)}, u32[]{:S(2)}) copy-start(f32[2,128]{1,0:T(2,128)} %constant.7.clone.factors) | copy-start | bytes 3076
  11.9 17.2 %copy-start.3 = (bf16[512,160]{1,0:T(8,128)(2,1)S(1)}, bf16[512,160]{1,0:T(8,128)(2,1)}, u32[]{:S(2)}) copy-start(bf16[512,160]{1,0:T(8,128)(2,1)} %constant.8.clone.basis) | copy-start | bytes 491524

commit v4 on v3

v4 whole, which is shorter than its diff:
```python
import functools
import math

import jax
import jax.numpy as jnp
import numpy as np
from jax import lax
from jax.experimental import pallas as pl
from jax.experimental.pallas import tpu as pltpu
from jax.sharding import PartitionSpec as P

CAP = 16
SMAG_COEF = 0.12
STRAIN_FLOOR = 0.01
BASE_SHIFT = 0.004
MODE_SHIFT = 0.02

CHUNK = 256
PAD_ROWS = 24
COST = pl.CostEstimate(flops=10**9, bytes_accessed=10**7, transcendentals=0)
CODES = 32000.0
STEPS = 32.0
VMEM = pl.BlockSpec(memory_space=pltpu.VMEM)
HBM = pl.BlockSpec(memory_space=pltpu.HBM)
SMEM = pl.BlockSpec(memory_space=pltpu.SMEM)


def split(value):
    high = value.astype(jnp.bfloat16)
    low = (value - high.astype(jnp.float32)).astype(jnp.bfloat16)
    return high, low


def split_table(table, parts):
    pieces = []
    for _ in range(parts):
        pieces.append(table.astype(jnp.bfloat16))
        table = table - pieces[-1].astype(np.float64)
    return pieces


def matmul(left, right):
    return jnp.dot(left, right, preferred_element_type=jnp.float32)


def x_tables(width, kxr, grid_rows):
    norm = 1.0 / math.sqrt(width * grid_rows)
    phase = (np.arange(width)[:, None] * np.arange(kxr)[None, :] % width) * (2.0 * np.pi / width)
    table = np.stack([np.cos(phase) * norm, -np.sin(phase) * norm], axis=2)
    pieces = split_table(table.reshape(width, 2 * kxr), 2)
    angle = np.arange(kxr) * (2.0 * np.pi / width)
    turn = np.stack([-np.sin(angle), np.sin(angle)], axis=1).reshape(2 * kxr) * 0.5
    second = np.repeat(-4.0 * np.sin(angle * 0.5) ** 2, 2)
    return np.concatenate(pieces, axis=1), np.stack([turn, second]).astype(np.float32)


def y_tables(rows, groups, kyr):
    grid_rows = rows * groups
    nowhere = -grid_rows
    offset = np.concatenate([np.arange(rows), [-1, rows, nowhere, nowhere]])
    cells = (np.arange(groups)[:, None] * rows + offset[None, :]).reshape(-1)
    ky = np.arange(kyr) - kyr // 2
    phase = (ky[:, None] * cells[None, :] % grid_rows) * (2.0 * np.pi / grid_rows)
    valid = (cells >= 0) & (cells < grid_rows)
    table = np.concatenate([np.cos(phase), np.sin(phase)], axis=0) * valid[None, :]
    return np.concatenate(split_table(table, 2), axis=0)


def mode_kernel(
    groups, capacity, kyr, levels, depth,
    owners, columns, table_hbm, factors_hbm,
    pick, green, table, factors, arrived,
):
    copies = [pltpu.make_async_copy(factors_hbm, factors, arrived.at[0])]
    share = table.shape[0] // (arrived.shape[0] - 1)
    for i in range(1, arrived.shape[0]):
        at = pl.ds((i - 1) * share, share)
        copies.append(pltpu.make_async_copy(table_hbm.at[at], table.at[at], arrived.at[i]))
    for copy in copies:
        copy.start()
    kxr = owners.shape[1]
    below, above, metric = [
        [columns[i * levels + k : i * levels + k + 1, :] for k in range(levels)] for i in range(3)
    ]
    places, gy = lax.axis_index("gz"), lax.axis_index("gy")
    shape = (2 * kxr, kxr)
    mode = lax.broadcasted_iota(jnp.int32, shape, 0) // 2
    other = lax.broadcasted_iota(jnp.int32, shape, 1)
    named = owners[...].astype(jnp.float32)
    owner = jnp.sum(jnp.where(mode == other, named, 0.0), axis=1, keepdims=True)
    rank = jnp.sum(
        jnp.where((named == owner) & (other < mode), 1.0, 0.0), axis=1, keepdims=True
    )
    slot = (owner * capacity + rank).astype(jnp.int32)
    part = lax.broadcasted_iota(jnp.int32, (2 * kxr, 1), 0) % 2
    column = lax.broadcasted_iota(jnp.int32, (2 * kxr, groups * capacity * 2), 1)
    pick[...] = jnp.where(slot * 2 + part == column, 1.0, 0.0).astype(jnp.bfloat16)

    lane = lax.broadcasted_iota(jnp.int32, (2 * kxr, 128), 1)
    here = gy * capacity + lane % (2 * capacity) // 2
    owned = (slot == here) & (part == 0)
    mode_id = (lax.broadcasted_iota(jnp.int32, (2 * kxr, 128), 0) // 2).astype(jnp.float32)
    kx = jnp.sum(jnp.where(owned, mode_id, 0.0), axis=0, keepdims=True)
    filled = jnp.sum(jnp.where(owned, 1.0, 0.0), axis=0, keepdims=True)

    size = 64
    at = lax.broadcasted_iota(jnp.int32, (size, 128), 1) // (2 * capacity)

    def turn(step, carry):
        start = pl.multiple_of(step * size, size)
        ky = lax.broadcasted_iota(jnp.int32, (size, 128), 0) + (start - kyr // 2)
        ky = ky.astype(jnp.float32)
        radius = kx * kx + ky * ky
        inside = jnp.where(radius <= float(kxr * kxr), filled, 0.0)
        shift = BASE_SHIFT + MODE_SHIFT * (radius / float(kxr * kxr))
        inverse = []
        for k in range(levels):
            pivot = -(below[k] + above[k] + metric[k] * shift)
            if k > 0:
                pivot = pivot - below[k] * above[k - 1] * inverse[-1]
            inverse.append(1.0 / pivot)
        for k in range(depth):
            target = places * depth + k
            forward = []
            for pos in range(levels):
                unit = jnp.where(target == pos, 1.0, 0.0)
                value = inside * unit
                if pos > 0:
                    value = value - above[pos - 1] * inverse[pos - 1] * forward[-1]
                forward.append(value)
            weights = [None] * levels
            for pos in range(levels - 1, -1, -1):
                value = forward[pos]
                if pos < levels - 1:
                    value = value - below[pos + 1] * weights[pos + 1]
                weights[pos] = value * inverse[pos]
            for block in range(levels // depth):
                total = jnp.zeros((size, 128), jnp.float32)
                for j in range(depth + 2):
                    pos = block * depth - 1 + j
                    if 0 <= pos < levels:
                        total = jnp.where(at == j, weights[pos], total)
                green[k, block, pl.ds(start, size), :] = total
        return carry

    lax.fori_loop(0, kyr // size, turn, 0)
    for copy in copies:
        copy.wait()


def pack_kernel(
    vx, vy, vz, owners_hbm, below_hbm, above_hbm, metric_hbm,
    own_one, own_two, row_one, row_two, owners, columns, scalars, arrived, small,
):
    rows = vx.shape[1]
    odd, odd_row = lax.axis_index("gz") % 2, lax.axis_index("gy") % 2
    copies = []
    for i, field in enumerate((vx, vy, vz)):
        for k, plane in enumerate((own_one, own_two)):
            level = odd if k else 1 - odd
            copies.append(pltpu.make_async_copy(field.at[level], plane.at[i], arrived.at[i, k]))
    others = [pltpu.make_async_copy(owners_hbm, owners, small.at[3])]
    for i, array in enumerate((below_hbm, above_hbm, metric_hbm)):
        others.append(pltpu.make_async_copy(array, scalars.at[i], small.at[i]))
    for copy in copies + others:
        copy.start()
    sub = lax.broadcasted_iota(jnp.int32, (8, vx.shape[2]), 0)
    bottom = jnp.zeros((8, vx.shape[2]), jnp.float32)
    top = bottom
    for copy in others:
        copy.wait()
    levels = scalars.shape[1]
    for i in range(3):
        for k in range(levels):
            at = i * levels + k
            columns[at : at + 1, :] = jnp.full((1, 128), scalars[i, k], jnp.float32)
    for i in range(3):
        for k, plane in enumerate((own_one, own_two)):
            copies[2 * i + k].wait()
            field = plane[i].astype(jnp.float32)
            bottom = jnp.where(sub == 2 * i + k, field[0:1], bottom)
            top = jnp.where(sub == 2 * i + k, field[rows - 1 : rows], top)
    row_one[...] = jnp.where(odd_row == 0, top, bottom).astype(jnp.bfloat16)
    row_two[...] = jnp.where(odd_row == 0, bottom, top).astype(jnp.bfloat16)


def up(field):
    return pltpu.roll(field, PAD_ROWS - 1, 0)


def down(field):
    return pltpu.roll(field, 1, 0)


def padded(field):
    empty = jnp.zeros((PAD_ROWS - field.shape[0], field.shape[1]), field.dtype)
    return jnp.concatenate([field, empty], axis=0)


def magnitude(squared):
    return SMAG_COEF * (squared * lax.rsqrt(squared))


def put_lines(lines, cells, fields):
    count = lines.shape[0] // 2
    start = 0
    for field in fields:
        high, low = split(field)
        size = field.shape[0]
        lines[start : start + size, cells] = high
        lines[count + start : count + start + size, cells] = low
        start += size


def transformed(lines, table):
    count, modes = lines.shape[0] // 2, table.shape[1] // 2
    product = matmul(lines[...], table[...])
    product = product[:count] + product[count:]
    return product[:, :modes] + product[:, modes:]


def slope_of(factors, field):
    modes = field.shape[1]
    even = lax.broadcasted_iota(jnp.int32, (1, modes), 1) % 2 == 0
    moved = jnp.where(even, pltpu.roll(field, modes - 1, 1), pltpu.roll(field, 1, 1))
    return factors[0:1] * moved


def early_kernel(
    groups, planes,
    own_one, own_two, row_one, row_two, table, factors,
    strain, spectra, lines,
):
    rows, width = own_one.shape[1:]
    gz, gy = lax.axis_index("gz"), lax.axis_index("gy")
    first = jnp.where(gz == 0, 1.0, 0.0)
    last = jnp.where(gz == planes - 1, 1.0, 0.0)
    odd, odd_row = gz % 2, gy % 2
    sub = lax.broadcasted_iota(jnp.int32, (8, CHUNK), 0)
    at_top, at_bottom = sub == 0, sub == 7
    rim_one = at_top & (odd_row == 0) | at_bottom & (odd_row == 1)
    rim_two = at_top & (odd_row == 1) | at_bottom & (odd_row == 0)
    ghost_rows = jnp.where(at_top & (gy == groups - 1) | at_bottom & (gy == 0), 1.0, 0.0)

    for step in range(width // CHUNK):
        here = step * CHUNK
        before, after = (here - 128) % width, (here + CHUNK) % width
        cells = pl.ds(here, CHUNK)
        rows_one = row_one[:, cells].astype(jnp.float32)
        rows_two = row_two[:, cells].astype(jnp.float32)
        flat, rims = [], []
        for k, source in enumerate((own_one, own_two)):
            sign = jnp.where(odd == k, 1.0, -1.0)
            own = [source[i, :, cells].astype(jnp.float32) for i in range(3)]
            x, y, rim = [], [], []
            for i in range(3):
                window = jnp.concatenate(
                    [
                        source[i, :, pl.ds(before, 128)].astype(jnp.float32),
                        own[i],
                        source[i, :, pl.ds(after, 128)].astype(jnp.float32),
                    ],
                    axis=1,
                )
                difference = pltpu.roll(window, CHUNK + 255, 1) - pltpu.roll(window, 1, 1)
                x.append(difference[:, 128 : 128 + CHUNK])
                at = 2 * i + k
                edge = jnp.where(
                    rim_one, rows_one[at : at + 1], jnp.where(rim_two, rows_two[at : at + 1], 0.0)
                )
                field = jnp.concatenate([own[i], edge], axis=0)
                difference = up(field) - down(field)
                y.append(difference[:rows])
                rim.append(difference[rows:])
            e01 = y[0] + x[1]
            strain[k, 0, :, cells] = x[0]
            strain[k, 1, :, cells] = y[1]
            strain[k, 2, :, cells] = e01
            strain[k, 3, :, cells] = sign * x[2]
            strain[k, 4, :, cells] = sign * y[2]
            strain[k, 5, :, cells] = (
                0.5 * (x[0] * x[0] + y[1] * y[1]) + 0.25 * (e01 * e01) + STRAIN_FLOOR
            )
            squared = 0.5 * (rim[1] * rim[1]) + 0.25 * (rim[0] * rim[0] + rim[2] * rim[2])
            viscous = ghost_rows * magnitude(squared + STRAIN_FLOOR)
            rims += [viscous * rim[0], viscous * rim[1], viscous * (sign * rim[2])]
            flat.append(x[0] + y[1])

        ghost = [(first - last) * own_two[i, :, cells].astype(jnp.float32) for i in range(3)]
        squared = 0.5 * (ghost[2] * ghost[2])
        squared = squared + 0.25 * (ghost[0] * ghost[0] + ghost[1] * ghost[1])
        viscous = magnitude(squared + STRAIN_FLOOR)
        put_lines(lines, cells, flat + [viscous * ghost[i] for i in range(3)] + rims)

    total = transformed(lines, table)
    pieces = [padded(total[rows * i : rows * (i + 1)]) for i in range(5)]
    t02, t12, s22 = pieces[2:]
    cross = 0.25 * (up(t12) - down(t12)) + slope_of(factors, t02)
    pieces = pieces[:2] + [s22 + (last - first) * cross]
    for i, piece in enumerate(pieces + [total[5 * rows :]]):
        spectra[PAD_ROWS * i : PAD_ROWS * i + piece.shape[0], :] = piece


def late_kernel(
    planes, groups, capacity,
    own_one, own_two, plane_one, plane_two, strain, spectra, table, factors, pick,
    out, lines, codes,
):
    rows, width = own_one.shape[1:]
    gz = lax.axis_index("gz")
    first = jnp.where(gz == 0, 1.0, 0.0)
    last = jnp.where(gz == planes - 1, 1.0, 0.0)
    odd = gz % 2

    for step in range(width // CHUNK):
        cells = pl.ds(step * CHUNK, CHUNK)
        fields = []
        for k, plane, other in ((0, plane_one, own_two), (1, plane_two, own_one)):
            z = [
                plane[i, :, cells].astype(jnp.float32) - other[i, :, cells].astype(jnp.float32)
                for i in range(3)
            ]
            e02 = z[0] + strain[k, 3, :, cells]
            e12 = z[1] + strain[k, 4, :, cells]
            squared = strain[k, 5, :, cells] + 0.5 * (z[2] * z[2])
            squared = squared + 0.25 * (e02 * e02 + e12 * e12)
            viscous = magnitude(squared)
            fields += [viscous * strain[k, i, :, cells] for i in (2, 1)]
            fields += [viscous * e12, viscous * z[2], viscous * e02]
            fields += [viscous * strain[k, 0, :, cells], z[2]]
        put_lines(lines, cells, fields)

    total = transformed(lines, table)
    parts = []
    for k in range(2):
        sign = jnp.where(odd == k, 1.0, -1.0)
        pieces = [total[rows * i : rows * (i + 1)] for i in range(7 * k, 7 * k + 7)]
        for i in range(3):
            start = 3 * PAD_ROWS + 8 * (3 * k + i)
            pieces[i] = jnp.concatenate([pieces[i], spectra[start : start + 8, :]], axis=0)
        t01, p11, t12 = pieces[:3]
        s22, t02, s00, rise = [padded(piece) for piece in pieces[3:]]
        p11 = up(p11) + down(p11) - 2.0 * p11
        t01 = up(t01) - down(t01)
        t12 = 0.25 * (up(t12) - down(t12))
        flat = spectra[k * PAD_ROWS : (k + 1) * PAD_ROWS, :]
        s22, rise = sign * s22, sign * rise
        middle = p11 - 2.0 * s22 + 0.5 * (flat + rise)
        middle = middle + slope_of(factors, t01) + factors[1:2] * s00
        cross = sign * (t12 + slope_of(factors, t02))
        parts.append([s22 + cross, middle, s22 - cross])

    ghost = spectra[2 * PAD_ROWS : 3 * PAD_ROWS, :]
    lower = [jnp.where(odd == 1, p, q) for p, q in zip(*parts)]
    upper = [jnp.where(odd == 1, q, p) for p, q in zip(*parts)]
    spectrum = [
        lower[0],
        lower[1] + upper[0] + first * ghost,
        lower[2] + upper[1] + last * ghost,
        upper[2],
    ]
    count = len(spectrum)

    stacked = jnp.concatenate(spectrum, axis=0)
    selected = matmul(jnp.concatenate(split(stacked), axis=0), pick[...])
    size = count * PAD_ROWS
    selected = selected[:size] + selected[size:]

    lane = lax.broadcasted_iota(jnp.int32, (PAD_ROWS, 128), 1)
    empty_block = jnp.zeros((PAD_ROWS, 128), jnp.float32)
    sub_lanes = lax.broadcasted_iota(jnp.int32, (8, 128), 0)
    share = 2 * capacity
    for half in range(groups * share // 128):
        pieces = [
            selected[PAD_ROWS * j : PAD_ROWS * (j + 1), 128 * half : 128 * (half + 1)]
            for j in range(count)
        ]
        for place in range(128 // share):
            block = empty_block
            for j in range(count):
                distance = (share * (j - place)) % 128
                moved = pltpu.roll(pieces[j], distance, 1) if distance else pieces[j]
                block = jnp.where(lane // share == j, moved, block)
            largest = jnp.max(jnp.abs(block), axis=0, keepdims=True)
            power = jnp.floor(jnp.log2(jnp.maximum(largest, 1e-35)) * STEPS) + 1.0
            block = jnp.floor(block * (CODES * jnp.exp2(power * (-1.0 / STEPS))) + 0.5)
            rim = pltpu.roll(block[rows:], 1, 0)
            rim = jnp.where(sub_lanes < 2, rim, jnp.where(sub_lanes == 2, power, 0.0))
            base = (half * (128 // share) + place) * (rows + 4)
            codes[base : base + rows, :] = block[:rows]
            codes[base + rows : base + rows + 4, :] = rim[:4]
    packed = codes[...].astype(jnp.int32).astype(jnp.int16)
    for side in range(planes):
        out[side * packed.shape[0] : (side + 1) * packed.shape[0], :] = packed


def solve_kernel(kyr, depth, capacity, reach, received, basis, green, out, codes):
    planes = green.shape[1]
    sources = received.shape[0] // reach
    codes[...] = received[...].astype(jnp.int32).astype(jnp.float32)
    power = codes[pl.ds(reach - 2, sources, stride=reach), :]
    scale = jnp.exp2(power * (1.0 / STEPS)) * (1.0 / CODES)
    row = lax.broadcasted_iota(jnp.int32, (2 * reach, 128), 0)
    values = []
    for pair in range(0, sources, 2):
        factor = jnp.where(row < reach, scale[pair : pair + 1], scale[pair + 1 : pair + 2])
        values.append(codes[pair * reach : (pair + 2) * reach, :] * factor)
    each = sources // planes // 2
    blocks = [jnp.concatenate(values[i * each : (i + 1) * each], axis=0) for i in range(planes)]
    high, low = split(jnp.concatenate(blocks, axis=1))
    product = matmul(basis[...], high)
    product = product[: 2 * kyr] + product[2 * kyr :] + matmul(basis[: 2 * kyr, :], low)
    cosine = [jnp.zeros((kyr, 128), jnp.float32) for _ in range(depth)]
    sine = [jnp.zeros((kyr, 128), jnp.float32) for _ in range(depth)]
    for block in range(planes):
        lanes = slice(block * 128, (block + 1) * 128)
        for k in range(depth):
            cosine[k] = cosine[k] + green[k, block] * product[:kyr, lanes]
            sine[k] = sine[k] + green[k, block] * product[kyr:, lanes]
    lane = lax.broadcasted_iota(jnp.int32, (kyr, 128), 1)
    share = 2 * capacity

    def gathered(field):
        distance = 64
        while distance >= share:
            field = field + pltpu.roll(field, distance, 1)
            distance //= 2
        return field

    result = jnp.zeros((kyr, 128), jnp.float32)
    for k in range(depth):
        real = gathered(cosine[k])
        turned = gathered(sine[k])
        turned = jnp.where(lane % 2 == 0, pltpu.roll(turned, 127, 1), -pltpu.roll(turned, 1, 1))
        result = jnp.where(lane // share == k, real + turned, result)
    flipped = result.T
    for k in range(depth):
        out[:, k, :] = flipped[k * share : (k + 1) * share]


def exchange(array, axis, size, shifted):
    pairs = [(i, i + 1) for i in range(shifted, size - 1, 2)]
    return lax.ppermute(array, axis, pairs + [(j, i) for i, j in pairs])


def in_hbm(array):
    return pltpu.with_memory_space_constraint(array, pltpu.HBM)


def per_device(groups, planes, velocity_x, velocity_y, velocity_z, owners, below, above, metric):
    depth, rows, width = velocity_x.shape
    kxr = owners.shape[0]
    kyr = 2 * kxr
    levels = below.shape[0]
    limit = pltpu.CompilerParams(vmem_limit_bytes=32 * 1024 * 1024)
    fields = (velocity_x, velocity_y, velocity_z)

    plane_shape = jax.ShapeDtypeStruct((3, rows, width), jnp.bfloat16)
    row_shape = jax.ShapeDtypeStruct((8, width), jnp.bfloat16)
    own_one, own_two, row_one, row_two, owners, columns = pl.pallas_call(
        pack_kernel,
        out_shape=(plane_shape, plane_shape, row_shape, row_shape)
        + (
            jax.ShapeDtypeStruct((1, kxr), jnp.int32),
            jax.ShapeDtypeStruct((3 * levels, 128), jnp.float32),
        ),
        in_specs=[HBM] * 7,
        out_specs=(VMEM,) * 6,
        scratch_shapes=[
            pltpu.SMEM((3, levels), jnp.float32),
            pltpu.SemaphoreType.DMA((3, 2)),
            pltpu.SemaphoreType.DMA((4,)),
        ],
        compiler_params=limit,
    )(*[in_hbm(array) for array in (*fields, owners.reshape(1, kxr), below, above, metric)])
    plane_one = exchange(own_one, "gz", planes, 0)
    plane_two = exchange(own_two, "gz", planes, 1)
    row_one = exchange(row_one, "gy", groups, 0)
    row_two = exchange(row_two, "gy", groups, 1)

    table, factors = [jnp.asarray(array) for array in x_tables(width, kxr, rows * groups)]
    pick, green, table, factors = pl.pallas_call(
        functools.partial(mode_kernel, groups, CAP, kyr, levels, depth),
        out_shape=(
            jax.ShapeDtypeStruct((2 * kxr, groups * CAP * 2), jnp.bfloat16),
            jax.ShapeDtypeStruct((depth, planes, kyr, 128), jnp.float32),
            jax.ShapeDtypeStruct(table.shape, table.dtype),
            jax.ShapeDtypeStruct(factors.shape, factors.dtype),
        ),
        in_specs=[VMEM, VMEM, HBM, HBM],
        out_specs=(VMEM,) * 4,
        scratch_shapes=[pltpu.SemaphoreType.DMA((5,))],
        compiler_params=limit,
        cost_estimate=COST,
    )(owners, columns, in_hbm(table), in_hbm(factors))

    strain, spectra = pl.pallas_call(
        functools.partial(early_kernel, groups, planes),
        out_shape=(
            jax.ShapeDtypeStruct((depth, 6, rows, width), jnp.float32),
            jax.ShapeDtypeStruct((3 * PAD_ROWS + 6 * 8, 2 * kxr), jnp.float32),
        ),
        in_specs=[VMEM] * 6,
        out_specs=(VMEM,) * 2,
        scratch_shapes=[pltpu.VMEM((2 * (5 * rows + 6 * 8), width), jnp.bfloat16)],
        compiler_params=limit,
        cost_estimate=COST,
    )(own_one, own_two, row_one, row_two, table, factors)

    reach = rows + 4
    count = depth * 7 * rows
    outgoing = pl.pallas_call(
        functools.partial(late_kernel, planes, groups, CAP),
        out_shape=jax.ShapeDtypeStruct((planes * groups * reach, 128), jnp.int16),
        in_specs=[VMEM] * 9,
        out_specs=VMEM,
        scratch_shapes=[
            pltpu.VMEM((2 * count, width), jnp.bfloat16),
            pltpu.VMEM((groups * reach, 128), jnp.float32),
        ],
        compiler_params=limit,
    )(own_one, own_two, plane_one, plane_two, strain, spectra, table, factors, pick)
    outgoing = outgoing.reshape(planes * groups, reach // 2, 2, 128)
    received = lax.all_to_all(outgoing, ("gz", "gy"), split_axis=0, concat_axis=0, tiled=True)
    received = received.reshape(planes * groups * reach, 128)

    basis = jnp.asarray(y_tables(rows, groups, kyr))
    solved = pl.pallas_call(
        functools.partial(solve_kernel, kyr, depth, CAP, reach),
        out_shape=jax.ShapeDtypeStruct((CAP * 2, depth, kyr), jnp.float32),
        in_specs=[VMEM] * 3,
        out_specs=VMEM,
        scratch_shapes=[pltpu.VMEM(received.shape, jnp.float32)],
        compiler_params=limit,
    )(received, basis, green)
    return solved.reshape(1, CAP, 2, depth, kyr)


def solution(mesh):
    placed = (P("gz", "gy", None), P("gz", "gy", None), P("gz", "gy", None), P(), P(), P(), P())
    return jax.shard_map(
        functools.partial(per_device, mesh.shape["gy"], mesh.shape["gz"]),
        mesh=mesh,
        in_specs=placed,
        out_specs=P("gy", None, None, "gz", None),
        check_vma=False,
    )
```

time: 30.7 us -> 30.5 us (level)
  blocking collectives: 17.2 us -> 18.6 us
  Pallas kernels: 7.08 us -> 6.06 us
    all_to_all x1, blocking collectives: 17.2 us -> 18.6 us  [per_device(): lax.all_to_all(outgoing, ('gz', 'gy'), split_axis=0, concat_axis=0, tiled...]
    pallas_call x1, Pallas kernels: 1.83 us -> 1.25 us  [per_device(): pl.pallas_call(functools.partial(mode_kernel, groups, CAP, kyr, levels, d...]
    pallas_call x2, Pallas kernels: 2.81 us -> 2.33 us  [the longest x1 1.17 us: per_device(): pl.pallas_call(functools.partial(late_kernel, planes, groups, CAP), out_s...]
  transfers between devices with their start and end apart: 4 -> 4, of which waited for: 1 -> 1; matrix products, arithmetic and copies ran while one was open for 0% -> 0% of each run, Pallas kernels for 10% -> 8%
where the time goes in v4:
time: 30.5 us; the launch traced here: 30.2 us
  blocking collectives  18.6 us (61%)
  Pallas kernels  6.06 us (20%)
  starting transfers between devices  4.4 us (14%)
  waiting for transfers between devices  1.05 us (3%)
    all_to_all x1, blocking collectives, per_device(): lax.all_to_all(outgoing, ('gz', 'gy'), split_axis=0, concat_axis=0, tiled...  18.6 us
    ppermute x4, starting transfers between devices, exchange(): return lax.ppermute(array, axis, pairs + [(j, i) for i, j in pairs])  4.4 us
    pallas_call x1, Pallas kernels, per_device(): pl.pallas_call(functools.partial(solve_kernel, kyr, depth, CAP, reach), o...  1.35 us
    pallas_call x1, Pallas kernels, per_device(): pl.pallas_call(functools.partial(mode_kernel, groups, CAP, kyr, levels, d...  1.25 us
    pallas_call x1, Pallas kernels, per_device(): pl.pallas_call(functools.partial(late_kernel, planes, groups, CAP), out_s...  1.17 us
    pallas_call x1, Pallas kernels, per_device(): pl.pallas_call(functools.partial(early_kernel, groups, planes), out_shape...  1.16 us
    pallas_call x1, Pallas kernels, per_device(): pl.pallas_call(pack_kernel, out_shape=(plane_shape, plane_shape, row_shap...  1.12 us
    ppermute x4, waiting for transfers between devices, exchange(): return lax.ppermute(array, axis, pairs + [(j, i) for i, j in pairs])  1.05 us
  transfers between devices with their start and end apart: 4, of which 1 were waited for; matrix products, arithmetic and copies ran while one was open for 0% of the time, Pallas kernels for 8%

profile of v4, /device:TPU:0, one launch (start us, length us, event | category | flops | bytes accessed | tf_op | source)
XLA Modules:
  0.0 30.2 jit_solution(7154887936983534612)
XLA Ops:
  0.0 1.1 %shard_map.100 = (bf16[3,16,2048]{2,1,0:T(8,128)(2,1)S(1)}, bf16[3,16,2048]{2,1,0:T(8,128)(2,1)S(1)}, bf16[8,2048]{1,0:T(8,128)(2,1)S(1)}, bf16[8,2048]{1,0:T(8,...) custom-call(bf16[2,16,2048]{2,1,0:T(8,128)(2,1)} %vx.1, bf16[2,16,2048]{2,1,0:T(8,128)(2,1)} %vy.1, ...), custom_call_target="tpu_custom_call" | custom-call | tf_op jit(solution)/shard_map/pallas_call | solution.py:460
  1.1 3.0 %collective-permute-start = (bf16[3,16,2048]{2,1,0:T(8,128)(2,1)S(1)}, bf16[3,16,2048]{2,1,0:T(8,128)(2,1)S(1)}, u32[]{:S(2)}, u32[]{:S(2)}) collective-permute-start(bf16[3,16,2048]{2,1,0:T(8,128)(2,1)S(1)} %get-tuple-element.17.own_one), channel_id=1, source_target_pairs={{0,8},{16,24},{8,0},{24,16},{1,9},{17,25},{9,1},{25,17},{2,10},{18... | collective-permute-start | bytes 589832 | tf_op jit(solution)/shard_map/ppermute | solution.py:443
  4.1 0.7 %collective-permute-start.1 = (bf16[3,16,2048]{2,1,0:T(8,128)(2,1)S(1)}, bf16[3,16,2048]{2,1,0:T(8,128)(2,1)S(1)}, u32[]{:S(2)}, u32[]{:S(2)}) collective-permute-start(bf16[3,16,2048]{2,1,0:T(8,128)(2,1)S(1)} %get-tuple-element.18.own_two), channel_id=1, source_target_pairs={{8,16},{16,8},{9,17},{17,9},{10,18},{18,10},{11,19},{19,11},{12,20... | collective-permute-start | bytes 589832 | tf_op jit(solution)/shard_map/ppermute | solution.py:443
  4.8 0.1 collective-permute-start.2
  4.9 0.7 %collective-permute-start.3 = (bf16[8,2048]{1,0:T(8,128)(2,1)S(1)}, bf16[8,2048]{1,0:T(8,128)(2,1)S(1)}, u32[]{:S(2)}, u32[]{:S(2)}) collective-permute-start(bf16[8,2048]{1,0:T(8,128)(2,1)S(1)} %get-tuple-element.20), channel_id=1, source_target_pairs={{1,2},{3,4},{5,6},{2,1},{4,3},{6,5},{9,10},{11,12},{13,14},{10,9},... | collective-permute-start | bytes 98312 | tf_op jit(solution)/shard_map/ppermute | solution.py:443
  5.6 1.2 %shard_map.101 = (bf16[128,256]{1,0:T(8,128)(2,1)S(1)}, f32[2,4,128,128]{3,2,1,0:T(8,128)S(1)}, bf16[2048,256]{1,0:T(8,128)(2,1)S(1)}, f32[2,128]{1,0:T(2,128)S(1)}) custom-call(s32[1,64]{1,0:T(1,128)S(1)} %get-tuple-element.21.owners, f32[24,128]{1,0:T(8,128)S(1)} %get-tuple-element.22.columns, bf16[2048,256]{1,0:T(8,128)(2,1)} %constant.6.clone.table_hbm, ...), custom_call_target="tpu_custom_call" | custom-call | flops 1000000000 | bytes 10000000 | tf_op jit(solution)/shard_map/pallas_call | solution.py:482
  6.8 0.0 collective-permute-done.2.row_one
  6.8 0.0 collective-permute-done.3.row_two
  6.8 1.2 %shard_map.102 = (f32[2,6,16,2048]{3,2,1,0:T(8,128)S(1)}, f32[120,128]{1,0:T(8,128)S(1)}) custom-call(bf16[3,16,2048]{2,1,0:T(8,128)(2,1)S(1)} %get-tuple-element.17.own_one, bf16[3,16,2048]{2,1,0:T(8,128)(2,1)S(1)} %get-tuple-element.18.own_two, bf16[8,2048]{1,0:T(8,128)(2,1)S(1)} %collective-permute-done.2.row_one, ...), custom_call_target="tpu_custom_call" | custom-call | flops 1000000000 | bytes 10000000 | tf_op jit(solution)/shard_map/pallas_call | solution.py:497
  8.0 1.0 %collective-permute-done.plane_one = bf16[3,16,2048]{2,1,0:T(8,128)(2,1)S(1)} collective-permute-done((bf16[3,16,2048]{2,1,0:T(8,128)(2,1)S(1)}, bf16[3,16,2048]{2,1,0:T(8,128)(2,1)S(1)}, u32[]{:S(2)}, u32[]{:S(2)}) %collective-permute-start) | collective-permute-done | bytes 196640 | tf_op jit(solution)/shard_map/ppermute | solution.py:443
  9.0 0.0 collective-permute-done.1.plane_two
  9.0 0.0 copy-start
  9.0 1.2 %shard_map.103 = s16[640,128]{1,0:T(8,128)(2,1)S(1)} custom-call(bf16[3,16,2048]{2,1,0:T(8,128)(2,1)S(1)} %get-tuple-element.17.own_one, bf16[3,16,2048]{2,1,0:T(8,128)(2,1)S(1)} %get-tuple-element.18.own_two, bf16[3,16,2048]{2,1,0:T(8,128)(2,1)S(1)} %collective-permute-done.plane_one, bf16[3,16,2048]{2,1,0:T(8,128)(2,1)S(1)} %collective-permute-done.1.plane_two, ...), custom_call_target="tpu_custom_call" | custom-call | tf_op jit(solution)/shard_map/pallas_call | solution.py:512
  10.2 18.6 %all_to_all.5 = s16[32,10,2,128]{3,2,1,0:T(2,128)(2,1)S(1)} all-to-all(s16[32,10,2,128]{3,2,1,0:T(2,128)(2,1)S(1)} %bitcast.4), channel_id=1, replica_groups=mesh['gz'=4,'gy'=8] {'gz','gy'}, dimensions={0} | all-to-all | bytes 327680 | tf_op jit(solution)/shard_map/all_to_all | solution.py:524
  28.8 0.0 copy-done
  28.8 1.4 %shard_map.104 = f32[32,2,128]{2,1,0:T(2,128)} custom-call(s16[640,128]{1,0:T(8,128)(2,1)S(1)} %bitcast.5, bf16[512,160]{1,0:T(8,128)(2,1)S(1)} %copy-done, f32[2,4,128,128]{3,2,1,0:T(8,128)S(1)} %get-tuple-element.28.green), custom_call_target="tpu_custom_call" | custom-call | tf_op jit(solution)/shard_map/pallas_call | solution.py:528
Async XLA Ops:
  1.1 7.9 %collective-permute-start = (bf16[3,16,2048]{2,1,0:T(8,128)(2,1)S(1)}, bf16[3,16,2048]{2,1,0:T(8,128)(2,1)S(1)}, u32[]{:S(2)}, u32[]{:S(2)}) collective-permute-start(bf16[3,16,2048]{2,1,0:T(8,128)(2,1)S(1)} %get-tuple-element.17.own_one), channel_id=1, source_target_pairs={{0,8},{16,24},{8,0},{24,16},{1,9},{17,25},{9,1},{25,17},{2,10},{18... | collective-permute-start | bytes 589832 | tf_op jit(solution)/shard_map/ppermute | solution.py:443
  4.1 4.9 %collective-permute-start.1 = (bf16[3,16,2048]{2,1,0:T(8,128)(2,1)S(1)}, bf16[3,16,2048]{2,1,0:T(8,128)(2,1)S(1)}, u32[]{:S(2)}, u32[]{:S(2)}) collective-permute-start(bf16[3,16,2048]{2,1,0:T(8,128)(2,1)S(1)} %get-tuple-element.18.own_two), channel_id=1, source_target_pairs={{8,16},{16,8},{9,17},{17,9},{10,18},{18,10},{11,19},{19,11},{12,20... | collective-permute-start | bytes 589832 | tf_op jit(solution)/shard_map/ppermute | solution.py:443
  4.8 2.0 %collective-permute-start.2 = (bf16[8,2048]{1,0:T(8,128)(2,1)S(1)}, bf16[8,2048]{1,0:T(8,128)(2,1)S(1)}, u32[]{:S(2)}, u32[]{:S(2)}) collective-permute-start(bf16[8,2048]{1,0:T(8,128)(2,1)S(1)} %get-tuple-element.19), channel_id=1, source_target_pairs={{0,1},{2,3},{4,5},{6,7},{1,0},{3,2},{5,4},{7,6},{8,9},{10,11},{12,... | collective-permute-start | bytes 98312 | tf_op jit(solution)/shard_map/ppermute | solution.py:443
  4.9 1.9 %collective-permute-start.3 = (bf16[8,2048]{1,0:T(8,128)(2,1)S(1)}, bf16[8,2048]{1,0:T(8,128)(2,1)S(1)}, u32[]{:S(2)}, u32[]{:S(2)}) collective-permute-start(bf16[8,2048]{1,0:T(8,128)(2,1)S(1)} %get-tuple-element.20), channel_id=1, source_target_pairs={{1,2},{3,4},{5,6},{2,1},{4,3},{6,5},{9,10},{11,12},{13,14},{10,9},... | collective-permute-start | bytes 98312 | tf_op jit(solution)/shard_map/ppermute | solution.py:443
  9.0 19.8 %copy-start = (bf16[512,160]{1,0:T(8,128)(2,1)S(1)}, bf16[512,160]{1,0:T(8,128)(2,1)}, u32[]{:S(2)}) copy-start(bf16[512,160]{1,0:T(8,128)(2,1)} %constant.8.clone.basis) | copy-start | bytes 491524

commit v5 on v4

--- a/solution.py
+++ b/solution.py
@@ -17,7 +17,6 @@
 
 CHUNK = 256
 PAD_ROWS = 24
-COST = pl.CostEstimate(flops=10**9, bytes_accessed=10**7, transcendentals=0)
 CODES = 32000.0
 STEPS = 32.0
 VMEM = pl.BlockSpec(memory_space=pltpu.VMEM)
@@ -228,26 +227,21 @@
 
 def early_kernel(
     groups, planes,
-    own_one, own_two, row_one, row_two, table, factors,
+    own_one, own_two, table, factors,
     strain, spectra, lines,
 ):
     rows, width = own_one.shape[1:]
     gz, gy = lax.axis_index("gz"), lax.axis_index("gy")
     first = jnp.where(gz == 0, 1.0, 0.0)
     last = jnp.where(gz == planes - 1, 1.0, 0.0)
-    odd, odd_row = gz % 2, gy % 2
+    odd = gz % 2
     sub = lax.broadcasted_iota(jnp.int32, (8, CHUNK), 0)
-    at_top, at_bottom = sub == 0, sub == 7
-    rim_one = at_top & (odd_row == 0) | at_bottom & (odd_row == 1)
-    rim_two = at_top & (odd_row == 1) | at_bottom & (odd_row == 0)
-    ghost_rows = jnp.where(at_top & (gy == groups - 1) | at_bottom & (gy == 0), 1.0, 0.0)
+    ghost_rows = jnp.where((sub == 0) & (gy == groups - 1) | (sub == 7) & (gy == 0), 1.0, 0.0)
 
     for step in range(width // CHUNK):
         here = step * CHUNK
         before, after = (here - 128) % width, (here + CHUNK) % width
         cells = pl.ds(here, CHUNK)
-        rows_one = row_one[:, cells].astype(jnp.float32)
-        rows_two = row_two[:, cells].astype(jnp.float32)
         flat, rims = [], []
         for k, source in enumerate((own_one, own_two)):
             sign = jnp.where(odd == k, 1.0, -1.0)
@@ -264,11 +258,7 @@
                 )
                 difference = pltpu.roll(window, CHUNK + 255, 1) - pltpu.roll(window, 1, 1)
                 x.append(difference[:, 128 : 128 + CHUNK])
-                at = 2 * i + k
-                edge = jnp.where(
-                    rim_one, rows_one[at : at + 1], jnp.where(rim_two, rows_two[at : at + 1], 0.0)
-                )
-                field = jnp.concatenate([own[i], edge], axis=0)
+                field = padded(own[i])
                 difference = up(field) - down(field)
                 y.append(difference[:rows])
                 rim.append(difference[rows:])
@@ -278,9 +268,6 @@
             strain[k, 2, :, cells] = e01
             strain[k, 3, :, cells] = sign * x[2]
             strain[k, 4, :, cells] = sign * y[2]
-            strain[k, 5, :, cells] = (
-                0.5 * (x[0] * x[0] + y[1] * y[1]) + 0.25 * (e01 * e01) + STRAIN_FLOOR
-            )
             squared = 0.5 * (rim[1] * rim[1]) + 0.25 * (rim[0] * rim[0] + rim[2] * rim[2])
             viscous = ghost_rows * magnitude(squared + STRAIN_FLOOR)
             rims += [viscous * rim[0], viscous * rim[1], viscous * (sign * rim[2])]
@@ -301,40 +288,60 @@
         spectra[PAD_ROWS * i : PAD_ROWS * i + piece.shape[0], :] = piece
 
 
-def late_kernel(
+def stress_lines(k, other, plane, row_one, row_two, strain, table, lines):
+    rows, width = other.shape[1:]
+    odd_row = lax.axis_index("gy") % 2
+    sign = jnp.where(lax.axis_index("gz") % 2 == k, 1.0, -1.0)
+    row = lax.broadcasted_iota(jnp.int32, (rows, CHUNK), 0)
+    for step in range(width // CHUNK):
+        cells = pl.ds(step * CHUNK, CHUNK)
+        ones = row_one[:, cells].astype(jnp.float32)
+        twos = row_two[:, cells].astype(jnp.float32)
+        lows = jnp.where(odd_row == 0, twos, ones)
+        highs = jnp.where(odd_row == 0, ones, twos)
+        z, beyond = [], []
+        for i in range(3):
+            at = 2 * i + k
+            z.append(plane[i, :, cells].astype(jnp.float32) - other[i, :, cells].astype(jnp.float32))
+            beyond.append(
+                jnp.where(
+                    row == rows - 1,
+                    highs[at : at + 1],
+                    jnp.where(row == 0, -lows[at : at + 1], 0.0),
+                )
+            )
+        x0 = strain[k, 0, :, cells]
+        y1 = strain[k, 1, :, cells] + beyond[1]
+        e01 = strain[k, 2, :, cells] + beyond[0]
+        e02 = z[0] + strain[k, 3, :, cells]
+        e12 = z[1] + strain[k, 4, :, cells] + sign * beyond[2]
+        squared = 0.5 * (x0 * x0 + y1 * y1 + z[2] * z[2]) + STRAIN_FLOOR
+        squared = squared + 0.25 * (e01 * e01 + e02 * e02 + e12 * e12)
+        viscous = magnitude(squared)
+        fields = [viscous * field for field in (e01, y1, e12, z[2], e02, x0)]
+        put_lines(lines, cells, fields + [z[2] + sign * beyond[1]])
+    return transformed(lines, table)
+
+
+def late_kernel(other, plane, row_one, row_two, strain, table, out, lines):
+    out[...] = stress_lines(0, other, plane, row_one, row_two, strain, table, lines)
+
+
+def last_kernel(
     planes, groups, capacity,
-    own_one, own_two, plane_one, plane_two, strain, spectra, table, factors, pick,
+    other, plane, row_one, row_two, strain, table, earlier, spectra, factors, pick,
     out, lines, codes,
 ):
-    rows, width = own_one.shape[1:]
+    rows = other.shape[1]
     gz = lax.axis_index("gz")
     first = jnp.where(gz == 0, 1.0, 0.0)
     last = jnp.where(gz == planes - 1, 1.0, 0.0)
     odd = gz % 2
-
-    for step in range(width // CHUNK):
-        cells = pl.ds(step * CHUNK, CHUNK)
-        fields = []
-        for k, plane, other in ((0, plane_one, own_two), (1, plane_two, own_one)):
-            z = [
-                plane[i, :, cells].astype(jnp.float32) - other[i, :, cells].astype(jnp.float32)
-                for i in range(3)
-            ]
-            e02 = z[0] + strain[k, 3, :, cells]
-            e12 = z[1] + strain[k, 4, :, cells]
-            squared = strain[k, 5, :, cells] + 0.5 * (z[2] * z[2])
-            squared = squared + 0.25 * (e02 * e02 + e12 * e12)
-            viscous = magnitude(squared)
-            fields += [viscous * strain[k, i, :, cells] for i in (2, 1)]
-            fields += [viscous * e12, viscous * z[2], viscous * e02]
-            fields += [viscous * strain[k, 0, :, cells], z[2]]
-        put_lines(lines, cells, fields)
-
-    total = transformed(lines, table)
+    totals = (earlier, stress_lines(1, other, plane, row_one, row_two, strain, table, lines))
     parts = []
     for k in range(2):
         sign = jnp.where(odd == k, 1.0, -1.0)
-        pieces = [total[rows * i : rows * (i + 1)] for i in range(7 * k, 7 * k + 7)]
+        pieces = [totals[k][rows * i : rows * (i + 1)] for i in range(7)]
         for i in range(3):
             start = 3 * PAD_ROWS + 8 * (3 * k + i)
             pieces[i] = jnp.concatenate([pieces[i], spectra[start : start + 8, :]], axis=0)
@@ -491,35 +498,38 @@
         out_specs=(VMEM,) * 4,
         scratch_shapes=[pltpu.SemaphoreType.DMA((5,))],
         compiler_params=limit,
-        cost_estimate=COST,
     )(owners, columns, in_hbm(table), in_hbm(factors))
 
     strain, spectra = pl.pallas_call(
         functools.partial(early_kernel, groups, planes),
         out_shape=(
-            jax.ShapeDtypeStruct((depth, 6, rows, width), jnp.float32),
+            jax.ShapeDtypeStruct((depth, 5, rows, width), jnp.float32),
             jax.ShapeDtypeStruct((3 * PAD_ROWS + 6 * 8, 2 * kxr), jnp.float32),
         ),
-        in_specs=[VMEM] * 6,
+        in_specs=[VMEM] * 4,
         out_specs=(VMEM,) * 2,
         scratch_shapes=[pltpu.VMEM((2 * (5 * rows + 6 * 8), width), jnp.bfloat16)],
         compiler_params=limit,
-        cost_estimate=COST,
-    )(own_one, own_two, row_one, row_two, table, factors)
+    )(own_one, own_two, table, factors)
 
     reach = rows + 4
-    count = depth * 7 * rows
+    held = pltpu.VMEM((2 * 7 * rows, width), jnp.bfloat16)
+    earlier = pl.pallas_call(
+        late_kernel,
+        out_shape=jax.ShapeDtypeStruct((7 * rows, 2 * kxr), jnp.float32),
+        in_specs=[VMEM] * 6,
+        out_specs=VMEM,
+        scratch_shapes=[held],
+        compiler_params=limit,
+    )(own_two, plane_one, row_one, row_two, strain, table)
     outgoing = pl.pallas_call(
-        functools.partial(late_kernel, planes, groups, CAP),
+        functools.partial(last_kernel, planes, groups, CAP),
         out_shape=jax.ShapeDtypeStruct((planes * groups * reach, 128), jnp.int16),
-        in_specs=[VMEM] * 9,
+        in_specs=[VMEM] * 10,
         out_specs=VMEM,
-        scratch_shapes=[
-            pltpu.VMEM((2 * count, width), jnp.bfloat16),
-            pltpu.VMEM((groups * reach, 128), jnp.float32),
-        ],
+        scratch_shapes=[held, pltpu.VMEM((groups * reach, 128), jnp.float32)],
         compiler_params=limit,
-    )(own_one, own_two, plane_one, plane_two, strain, spectra, table, factors, pick)
+    )(own_one, plane_two, row_one, row_two, strain, table, earlier, spectra, factors, pick)
     outgoing = outgoing.reshape(planes * groups, reach // 2, 2, 128)
     received = lax.all_to_all(outgoing, ("gz", "gy"), split_axis=0, concat_axis=0, tiled=True)
     received = received.reshape(planes * groups * reach, 128)

time: 30.5 us -> 30.3 us (level)
  blocking collectives: 18.6 us -> 18 us
    all_to_all x1, blocking collectives: 18.6 us -> 18 us  [per_device(): lax.all_to_all(outgoing, ('gz', 'gy'), split_axis=0, concat_axis=0, tiled...]
    pallas_call x1 -> x2, Pallas kernels: 1.17 us -> 1.55 us  [the longest x1 0.98 us: per_device(): pl.pallas_call(functools.partial(last_kernel, planes, groups, CAP), out_s...]
  transfers between devices with their start and end apart: 4 -> 4, of which waited for: 1 -> 1; matrix products, arithmetic and copies ran while one was open for 0% -> 0% of each run, Pallas kernels for 8% -> 9%
where the time goes in v5:
time: 30.3 us; the launch traced here: 30 us
  blocking collectives  18 us (59%)
  Pallas kernels  6.14 us (20%)
  starting transfers between devices  4.4 us (15%)
  waiting for transfers between devices  1.33 us (4%)
    all_to_all x1, blocking collectives, per_device(): lax.all_to_all(outgoing, ('gz', 'gy'), split_axis=0, concat_axis=0, tiled...  18 us
    ppermute x4, starting transfers between devices, exchange(): return lax.ppermute(array, axis, pairs + [(j, i) for i, j in pairs])  4.4 us
    pallas_call x1, Pallas kernels, per_device(): pl.pallas_call(functools.partial(solve_kernel, kyr, depth, CAP, reach), o...  1.35 us
    ppermute x4, waiting for transfers between devices, exchange(): return lax.ppermute(array, axis, pairs + [(j, i) for i, j in pairs])  1.33 us
    pallas_call x1, Pallas kernels, per_device(): pl.pallas_call(functools.partial(mode_kernel, groups, CAP, kyr, levels, d...  1.25 us
    pallas_call x1, Pallas kernels, per_device(): pl.pallas_call(pack_kernel, out_shape=(plane_shape, plane_shape, row_shap...  1.12 us
    pallas_call x1, Pallas kernels, per_device(): pl.pallas_call(functools.partial(last_kernel, planes, groups, CAP), out_s...  0.98 us
    pallas_call x1, Pallas kernels, per_device(): pl.pallas_call(functools.partial(early_kernel, groups, planes), out_shape...  0.88 us
  transfers between devices with their start and end apart: 4, of which 1 were waited for; matrix products, arithmetic and copies ran while one was open for 0% of the time, Pallas kernels for 9%

profile of v5, /device:TPU:0, one launch (start us, length us, event | category | flops | bytes accessed | tf_op | source)
XLA Modules:
  0.0 30.0 jit_solution(17714108586527689977)
XLA Ops:
  0.0 1.1 %shard_map.100 = (bf16[3,16,2048]{2,1,0:T(8,128)(2,1)S(1)}, bf16[3,16,2048]{2,1,0:T(8,128)(2,1)S(1)}, bf16[8,2048]{1,0:T(8,128)(2,1)S(1)}, bf16[8,2048]{1,0:T(8,...) custom-call(bf16[2,16,2048]{2,1,0:T(8,128)(2,1)} %vx.1, bf16[2,16,2048]{2,1,0:T(8,128)(2,1)} %vy.1, ...), custom_call_target="tpu_custom_call" | custom-call | tf_op jit(solution)/shard_map/pallas_call | solution.py:467
  1.1 3.0 %collective-permute-start.3 = (bf16[3,16,2048]{2,1,0:T(8,128)(2,1)S(1)}, bf16[3,16,2048]{2,1,0:T(8,128)(2,1)S(1)}, u32[]{:S(2)}, u32[]{:S(2)}) collective-permute-start(bf16[3,16,2048]{2,1,0:T(8,128)(2,1)S(1)} %get-tuple-element.17.own_one.other), channel_id=1, source_target_pairs={{0,8},{16,24},{8,0},{24,16},{1,9},{17,25},{9,1},{25,17},{2,10},{18... | collective-permute-start | bytes 589832 | tf_op jit(solution)/shard_map/ppermute | solution.py:450
  4.1 0.7 %collective-permute-start = (bf16[3,16,2048]{2,1,0:T(8,128)(2,1)S(1)}, bf16[3,16,2048]{2,1,0:T(8,128)(2,1)S(1)}, u32[]{:S(2)}, u32[]{:S(2)}) collective-permute-start(bf16[3,16,2048]{2,1,0:T(8,128)(2,1)S(1)} %get-tuple-element.18.own_two.other), channel_id=1, source_target_pairs={{8,16},{16,8},{9,17},{17,9},{10,18},{18,10},{11,19},{19,11},{12,20... | collective-permute-start | bytes 589832 | tf_op jit(solution)/shard_map/ppermute | solution.py:450
  4.8 0.1 collective-permute-start.1
  4.9 0.7 %collective-permute-start.2 = (bf16[8,2048]{1,0:T(8,128)(2,1)S(1)}, bf16[8,2048]{1,0:T(8,128)(2,1)S(1)}, u32[]{:S(2)}, u32[]{:S(2)}) collective-permute-start(bf16[8,2048]{1,0:T(8,128)(2,1)S(1)} %get-tuple-element.20), channel_id=1, source_target_pairs={{1,2},{3,4},{5,6},{2,1},{4,3},{6,5},{9,10},{11,12},{13,14},{10,9},... | collective-permute-start | bytes 98312 | tf_op jit(solution)/shard_map/ppermute | solution.py:450
  5.6 1.2 %shard_map.101 = (bf16[128,256]{1,0:T(8,128)(2,1)S(1)}, f32[2,4,128,128]{3,2,1,0:T(8,128)S(1)}, bf16[2048,256]{1,0:T(8,128)(2,1)S(1)}, f32[2,128]{1,0:T(2,128)S(1)}) custom-call(s32[1,64]{1,0:T(1,128)S(1)} %get-tuple-element.21.owners, f32[24,128]{1,0:T(8,128)S(1)} %get-tuple-element.22.columns, bf16[2048,256]{1,0:T(8,128)(2,1)} %constant.6.clone.table_hbm, ...), custom_call_target="tpu_custom_call" | custom-call | tf_op jit(solution)/shard_map/pallas_call | solution.py:489
  6.8 0.9 %shard_map.102 = (f32[2,5,16,2048]{3,2,1,0:T(8,128)S(1)}, f32[120,128]{1,0:T(8,128)S(1)}) custom-call(bf16[3,16,2048]{2,1,0:T(8,128)(2,1)S(1)} %get-tuple-element.17.own_one.other, bf16[3,16,2048]{2,1,0:T(8,128)(2,1)S(1)} %get-tuple-element.18.own_two.other, bf16[2048,256]{1,0:T(8,128)(2,1)S(1)} %get-tuple-element.23.table, ...), custom_call_target="tpu_custom_call" | custom-call | tf_op jit(solution)/shard_map/pallas_call | solution.py:503
  7.7 0.0 collective-permute-done.1.row_one
  7.7 0.0 collective-permute-done.2.row_two
  7.7 1.3 %collective-permute-done.3.plane = bf16[3,16,2048]{2,1,0:T(8,128)(2,1)S(1)} collective-permute-done((bf16[3,16,2048]{2,1,0:T(8,128)(2,1)S(1)}, bf16[3,16,2048]{2,1,0:T(8,128)(2,1)S(1)}, u32[]{:S(2)}, u32[]{:S(2)}) %collective-permute-start.3) | collective-permute-done | bytes 196640 | tf_op jit(solution)/shard_map/ppermute | solution.py:450
  9.0 0.6 %shard_map.103.earlier = f32[112,128]{1,0:T(8,128)S(1)} custom-call(bf16[3,16,2048]{2,1,0:T(8,128)(2,1)S(1)} %get-tuple-element.18.own_two.other, bf16[3,16,2048]{2,1,0:T(8,128)(2,1)S(1)} %collective-permute-done.3.plane, bf16[8,2048]{1,0:T(8,128)(2,1)S(1)} %collective-permute-done.1.row_one, bf16[8,2048]{1,0:T(8,128)(2,1)S(1)} %collective-permute-done.2.row_two, ...), custom_call_target="tpu_custom_call" | custom-call | tf_op jit(solution)/shard_map/pallas_call | solution.py:517
  9.6 0.0 collective-permute-done.plane
  9.6 0.0 copy-start
  9.6 1.0 %shard_map.104 = s16[640,128]{1,0:T(8,128)(2,1)S(1)} custom-call(bf16[3,16,2048]{2,1,0:T(8,128)(2,1)S(1)} %get-tuple-element.17.own_one.other, bf16[3,16,2048]{2,1,0:T(8,128)(2,1)S(1)} %collective-permute-done.plane, bf16[8,2048]{1,0:T(8,128)(2,1)S(1)} %collective-permute-done.1.row_one, bf16[8,2048]{1,0:T(8,128)(2,1)S(1)} %collective-permute-done.2.row_two, ...), custom_call_target="tpu_custom_call" | custom-call | tf_op jit(solution)/shard_map/pallas_call | solution.py:525
  10.6 18.0 %all_to_all.5 = s16[32,10,2,128]{3,2,1,0:T(2,128)(2,1)S(1)} all-to-all(s16[32,10,2,128]{3,2,1,0:T(2,128)(2,1)S(1)} %bitcast.4), channel_id=1, replica_groups=mesh['gz'=4,'gy'=8] {'gz','gy'}, dimensions={0} | all-to-all | bytes 327680 | tf_op jit(solution)/shard_map/all_to_all | solution.py:534
  28.6 0.0 copy-done
  28.6 1.4 %shard_map.105 = f32[32,2,128]{2,1,0:T(2,128)} custom-call(s16[640,128]{1,0:T(8,128)(2,1)S(1)} %bitcast.5, bf16[512,160]{1,0:T(8,128)(2,1)S(1)} %copy-done, f32[2,4,128,128]{3,2,1,0:T(8,128)S(1)} %get-tuple-element.28.green), custom_call_target="tpu_custom_call" | custom-call | tf_op jit(solution)/shard_map/pallas_call | solution.py:538
Async XLA Ops:
  1.1 7.9 %collective-permute-start.3 = (bf16[3,16,2048]{2,1,0:T(8,128)(2,1)S(1)}, bf16[3,16,2048]{2,1,0:T(8,128)(2,1)S(1)}, u32[]{:S(2)}, u32[]{:S(2)}) collective-permute-start(bf16[3,16,2048]{2,1,0:T(8,128)(2,1)S(1)} %get-tuple-element.17.own_one.other), channel_id=1, source_target_pairs={{0,8},{16,24},{8,0},{24,16},{1,9},{17,25},{9,1},{25,17},{2,10},{18... | collective-permute-start | bytes 589832 | tf_op jit(solution)/shard_map/ppermute | solution.py:450
  4.1 5.5 %collective-permute-start = (bf16[3,16,2048]{2,1,0:T(8,128)(2,1)S(1)}, bf16[3,16,2048]{2,1,0:T(8,128)(2,1)S(1)}, u32[]{:S(2)}, u32[]{:S(2)}) collective-permute-start(bf16[3,16,2048]{2,1,0:T(8,128)(2,1)S(1)} %get-tuple-element.18.own_two.other), channel_id=1, source_target_pairs={{8,16},{16,8},{9,17},{17,9},{10,18},{18,10},{11,19},{19,11},{12,20... | collective-permute-start | bytes 589832 | tf_op jit(solution)/shard_map/ppermute | solution.py:450
  4.8 2.9 %collective-permute-start.1 = (bf16[8,2048]{1,0:T(8,128)(2,1)S(1)}, bf16[8,2048]{1,0:T(8,128)(2,1)S(1)}, u32[]{:S(2)}, u32[]{:S(2)}) collective-permute-start(bf16[8,2048]{1,0:T(8,128)(2,1)S(1)} %get-tuple-element.19), channel_id=1, source_target_pairs={{0,1},{2,3},{4,5},{6,7},{1,0},{3,2},{5,4},{7,6},{8,9},{10,11},{12,... | collective-permute-start | bytes 98312 | tf_op jit(solution)/shard_map/ppermute | solution.py:450
  4.9 2.8 %collective-permute-start.2 = (bf16[8,2048]{1,0:T(8,128)(2,1)S(1)}, bf16[8,2048]{1,0:T(8,128)(2,1)S(1)}, u32[]{:S(2)}, u32[]{:S(2)}) collective-permute-start(bf16[8,2048]{1,0:T(8,128)(2,1)S(1)} %get-tuple-element.20), channel_id=1, source_target_pairs={{1,2},{3,4},{5,6},{2,1},{4,3},{6,5},{9,10},{11,12},{13,14},{10,9},... | collective-permute-start | bytes 98312 | tf_op jit(solution)/shard_map/ppermute | solution.py:450
  9.6 19.0 %copy-start = (bf16[512,160]{1,0:T(8,128)(2,1)S(1)}, bf16[512,160]{1,0:T(8,128)(2,1)}, u32[]{:S(2)}) copy-start(bf16[512,160]{1,0:T(8,128)(2,1)} %constant.8.clone.basis) | copy-start | bytes 491524

commit v6 on v5

--- a/solution.py
+++ b/solution.py
@@ -56,7 +56,7 @@
 def y_tables(rows, groups, kyr):
     grid_rows = rows * groups
     nowhere = -grid_rows
-    offset = np.concatenate([np.arange(rows), [-1, rows, nowhere, nowhere]])
+    offset = np.concatenate([[nowhere, -1, rows, nowhere], np.arange(rows)])
     cells = (np.arange(groups)[:, None] * rows + offset[None, :]).reshape(-1)
     ky = np.arange(kyr) - kyr // 2
     phase = (ky[:, None] * cells[None, :] % grid_rows) * (2.0 * np.pi / grid_rows)
@@ -277,7 +277,8 @@
         squared = 0.5 * (ghost[2] * ghost[2])
         squared = squared + 0.25 * (ghost[0] * ghost[0] + ghost[1] * ghost[1])
         viscous = magnitude(squared + STRAIN_FLOOR)
-        put_lines(lines, cells, flat + [viscous * ghost[i] for i in range(3)] + rims)
+        edge = [viscous * ghost[i] for i in range(3)]
+        put_lines(lines, cells, flat + edge + [jnp.concatenate(rims, axis=0)])
 
     total = transformed(lines, table)
     pieces = [padded(total[rows * i : rows * (i + 1)]) for i in range(5)]
@@ -391,11 +392,11 @@
             largest = jnp.max(jnp.abs(block), axis=0, keepdims=True)
             power = jnp.floor(jnp.log2(jnp.maximum(largest, 1e-35)) * STEPS) + 1.0
             block = jnp.floor(block * (CODES * jnp.exp2(power * (-1.0 / STEPS))) + 0.5)
-            rim = pltpu.roll(block[rows:], 1, 0)
-            rim = jnp.where(sub_lanes < 2, rim, jnp.where(sub_lanes == 2, power, 0.0))
+            rim = pltpu.roll(block[rows:], 2, 0)
+            rim = jnp.where(sub_lanes == 0, power, jnp.where(sub_lanes < 3, rim, 0.0))
             base = (half * (128 // share) + place) * (rows + 4)
-            codes[base : base + rows, :] = block[:rows]
-            codes[base + rows : base + rows + 4, :] = rim[:4]
+            codes[base : base + 4, :] = rim[:4]
+            codes[base + 4 : base + 4 + rows, :] = block[:rows]
     packed = codes[...].astype(jnp.int32).astype(jnp.int16)
     for side in range(planes):
         out[side * packed.shape[0] : (side + 1) * packed.shape[0], :] = packed
@@ -405,7 +406,7 @@
     planes = green.shape[1]
     sources = received.shape[0] // reach
     codes[...] = received[...].astype(jnp.int32).astype(jnp.float32)
-    power = codes[pl.ds(reach - 2, sources, stride=reach), :]
+    power = codes[pl.ds(0, sources, stride=reach), :]
     scale = jnp.exp2(power * (1.0 / STEPS)) * (1.0 / CODES)
     row = lax.broadcasted_iota(jnp.int32, (2 * reach, 128), 0)
     values = []
@@ -427,22 +428,17 @@
     lane = lax.broadcasted_iota(jnp.int32, (kyr, 128), 1)
     share = 2 * capacity
 
-    def gathered(field):
-        distance = 64
-        while distance >= share:
-            field = field + pltpu.roll(field, distance, 1)
-            distance //= 2
-        return field
-
-    result = jnp.zeros((kyr, 128), jnp.float32)
-    for k in range(depth):
-        real = gathered(cosine[k])
-        turned = gathered(sine[k])
-        turned = jnp.where(lane % 2 == 0, pltpu.roll(turned, 127, 1), -pltpu.roll(turned, 1, 1))
-        result = jnp.where(lane // share == k, real + turned, result)
+    def gathered(fields):
+        fields = [field + pltpu.roll(field, 64, 1) for field in fields]
+        field = jnp.where(lane < 64, fields[0], fields[1])
+        return field + pltpu.roll(field, share, 1)
+
+    turned = gathered(sine)
+    turned = jnp.where(lane % 2 == 0, pltpu.roll(turned, 127, 1), -pltpu.roll(turned, 1, 1))
+    result = gathered(cosine) + turned
     flipped = result.T
     for k in range(depth):
-        out[:, k, :] = flipped[k * share : (k + 1) * share]
+        out[:, k, :] = flipped[64 * k + share : 64 * k + 2 * share]
 
 
 def exchange(array, axis, size, shifted):

time: 30.3 us -> 30.2 us (level)
  no operation moved by 1% of the time
where the time goes in v6:
time: 30.2 us; the launch traced here: 29.9 us
  blocking collectives  18 us (60%)
  Pallas kernels  6.09 us (20%)
  starting transfers between devices  4.4 us (15%)
  waiting for transfers between devices  1.34 us (4%)
    all_to_all x1, blocking collectives, per_device(): lax.all_to_all(outgoing, ('gz', 'gy'), split_axis=0, concat_axis=0, tiled...  18 us
    ppermute x4, starting transfers between devices, exchange(): return lax.ppermute(array, axis, pairs + [(j, i) for i, j in pairs])  4.4 us
    ppermute x4, waiting for transfers between devices, exchange(): return lax.ppermute(array, axis, pairs + [(j, i) for i, j in pairs])  1.34 us
    pallas_call x1, Pallas kernels, per_device(): pl.pallas_call(functools.partial(solve_kernel, kyr, depth, CAP, reach), o...  1.31 us
    pallas_call x1, Pallas kernels, per_device(): pl.pallas_call(functools.partial(mode_kernel, groups, CAP, kyr, levels, d...  1.25 us
    pallas_call x1, Pallas kernels, per_device(): pl.pallas_call(pack_kernel, out_shape=(plane_shape, plane_shape, row_shap...  1.12 us
    pallas_call x1, Pallas kernels, per_device(): pl.pallas_call(functools.partial(last_kernel, planes, groups, CAP), out_s...  0.98 us
    pallas_call x1, Pallas kernels, per_device(): pl.pallas_call(functools.partial(early_kernel, groups, planes), out_shape...  0.87 us
  transfers between devices with their start and end apart: 4, of which 1 were waited for; matrix products, arithmetic and copies ran while one was open for 0% of the time, Pallas kernels for 9%

profile of v6, /device:TPU:0, one launch (start us, length us, event | category | flops | bytes accessed | tf_op | source)
XLA Modules:
  0.0 29.9 jit_solution(8748156264683562604)
XLA Ops:
  0.0 1.1 %shard_map.100 = (bf16[3,16,2048]{2,1,0:T(8,128)(2,1)S(1)}, bf16[3,16,2048]{2,1,0:T(8,128)(2,1)S(1)}, bf16[8,2048]{1,0:T(8,128)(2,1)S(1)}, bf16[8,2048]{1,0:T(8,...) custom-call(bf16[2,16,2048]{2,1,0:T(8,128)(2,1)} %vx.1, bf16[2,16,2048]{2,1,0:T(8,128)(2,1)} %vy.1, ...), custom_call_target="tpu_custom_call" | custom-call | tf_op jit(solution)/shard_map/pallas_call | solution.py:463
  1.1 3.0 %collective-permute-start.3 = (bf16[3,16,2048]{2,1,0:T(8,128)(2,1)S(1)}, bf16[3,16,2048]{2,1,0:T(8,128)(2,1)S(1)}, u32[]{:S(2)}, u32[]{:S(2)}) collective-permute-start(bf16[3,16,2048]{2,1,0:T(8,128)(2,1)S(1)} %get-tuple-element.17.own_one.other), channel_id=1, source_target_pairs={{0,8},{16,24},{8,0},{24,16},{1,9},{17,25},{9,1},{25,17},{2,10},{18... | collective-permute-start | bytes 589832 | tf_op jit(solution)/shard_map/ppermute | solution.py:446
  4.1 0.7 %collective-permute-start = (bf16[3,16,2048]{2,1,0:T(8,128)(2,1)S(1)}, bf16[3,16,2048]{2,1,0:T(8,128)(2,1)S(1)}, u32[]{:S(2)}, u32[]{:S(2)}) collective-permute-start(bf16[3,16,2048]{2,1,0:T(8,128)(2,1)S(1)} %get-tuple-element.18.own_two.other), channel_id=1, source_target_pairs={{8,16},{16,8},{9,17},{17,9},{10,18},{18,10},{11,19},{19,11},{12,20... | collective-permute-start | bytes 589832 | tf_op jit(solution)/shard_map/ppermute | solution.py:446
  4.8 0.1 collective-permute-start.1
  4.9 0.7 %collective-permute-start.2 = (bf16[8,2048]{1,0:T(8,128)(2,1)S(1)}, bf16[8,2048]{1,0:T(8,128)(2,1)S(1)}, u32[]{:S(2)}, u32[]{:S(2)}) collective-permute-start(bf16[8,2048]{1,0:T(8,128)(2,1)S(1)} %get-tuple-element.20), channel_id=1, source_target_pairs={{1,2},{3,4},{5,6},{2,1},{4,3},{6,5},{9,10},{11,12},{13,14},{10,9},... | collective-permute-start | bytes 98312 | tf_op jit(solution)/shard_map/ppermute | solution.py:446
  5.6 1.2 %shard_map.101 = (bf16[128,256]{1,0:T(8,128)(2,1)S(1)}, f32[2,4,128,128]{3,2,1,0:T(8,128)S(1)}, bf16[2048,256]{1,0:T(8,128)(2,1)S(1)}, f32[2,128]{1,0:T(2,128)S(1)}) custom-call(s32[1,64]{1,0:T(1,128)S(1)} %get-tuple-element.21.owners, f32[24,128]{1,0:T(8,128)S(1)} %get-tuple-element.22.columns, bf16[2048,256]{1,0:T(8,128)(2,1)} %constant.6.clone.table_hbm, ...), custom_call_target="tpu_custom_call" | custom-call | tf_op jit(solution)/shard_map/pallas_call | solution.py:485
  6.8 0.9 %shard_map.102 = (f32[2,5,16,2048]{3,2,1,0:T(8,128)S(1)}, f32[120,128]{1,0:T(8,128)S(1)}) custom-call(bf16[3,16,2048]{2,1,0:T(8,128)(2,1)S(1)} %get-tuple-element.17.own_one.other, bf16[3,16,2048]{2,1,0:T(8,128)(2,1)S(1)} %get-tuple-element.18.own_two.other, bf16[2048,256]{1,0:T(8,128)(2,1)S(1)} %get-tuple-element.23.table, ...), custom_call_target="tpu_custom_call" | custom-call | tf_op jit(solution)/shard_map/pallas_call | solution.py:499
  7.7 0.0 collective-permute-done.1.row_one
  7.7 0.0 collective-permute-done.2.row_two
  7.7 1.3 %collective-permute-done.3.plane = bf16[3,16,2048]{2,1,0:T(8,128)(2,1)S(1)} collective-permute-done((bf16[3,16,2048]{2,1,0:T(8,128)(2,1)S(1)}, bf16[3,16,2048]{2,1,0:T(8,128)(2,1)S(1)}, u32[]{:S(2)}, u32[]{:S(2)}) %collective-permute-start.3) | collective-permute-done | bytes 196640 | tf_op jit(solution)/shard_map/ppermute | solution.py:446
  9.0 0.6 %shard_map.103.earlier = f32[112,128]{1,0:T(8,128)S(1)} custom-call(bf16[3,16,2048]{2,1,0:T(8,128)(2,1)S(1)} %get-tuple-element.18.own_two.other, bf16[3,16,2048]{2,1,0:T(8,128)(2,1)S(1)} %collective-permute-done.3.plane, bf16[8,2048]{1,0:T(8,128)(2,1)S(1)} %collective-permute-done.1.row_one, bf16[8,2048]{1,0:T(8,128)(2,1)S(1)} %collective-permute-done.2.row_two, ...), custom_call_target="tpu_custom_call" | custom-call | tf_op jit(solution)/shard_map/pallas_call | solution.py:513
  9.6 0.0 collective-permute-done.plane
  9.6 0.0 copy-start
  9.6 1.0 %shard_map.104 = s16[640,128]{1,0:T(8,128)(2,1)S(1)} custom-call(bf16[3,16,2048]{2,1,0:T(8,128)(2,1)S(1)} %get-tuple-element.17.own_one.other, bf16[3,16,2048]{2,1,0:T(8,128)(2,1)S(1)} %collective-permute-done.plane, bf16[8,2048]{1,0:T(8,128)(2,1)S(1)} %collective-permute-done.1.row_one, bf16[8,2048]{1,0:T(8,128)(2,1)S(1)} %collective-permute-done.2.row_two, ...), custom_call_target="tpu_custom_call" | custom-call | tf_op jit(solution)/shard_map/pallas_call | solution.py:521
  10.6 18.0 %all_to_all.5 = s16[32,10,2,128]{3,2,1,0:T(2,128)(2,1)S(1)} all-to-all(s16[32,10,2,128]{3,2,1,0:T(2,128)(2,1)S(1)} %bitcast.4), channel_id=1, replica_groups=mesh['gz'=4,'gy'=8] {'gz','gy'}, dimensions={0} | all-to-all | bytes 327680 | tf_op jit(solution)/shard_map/all_to_all | solution.py:530
  28.6 0.0 copy-done
  28.6 1.3 %shard_map.105 = f32[32,2,128]{2,1,0:T(2,128)} custom-call(s16[640,128]{1,0:T(8,128)(2,1)S(1)} %bitcast.5, bf16[512,160]{1,0:T(8,128)(2,1)S(1)} %copy-done, f32[2,4,128,128]{3,2,1,0:T(8,128)S(1)} %get-tuple-element.28.green), custom_call_target="tpu_custom_call" | custom-call | tf_op jit(solution)/shard_map/pallas_call | solution.py:534
Async XLA Ops:
  1.1 7.9 %collective-permute-start.3 = (bf16[3,16,2048]{2,1,0:T(8,128)(2,1)S(1)}, bf16[3,16,2048]{2,1,0:T(8,128)(2,1)S(1)}, u32[]{:S(2)}, u32[]{:S(2)}) collective-permute-start(bf16[3,16,2048]{2,1,0:T(8,128)(2,1)S(1)} %get-tuple-element.17.own_one.other), channel_id=1, source_target_pairs={{0,8},{16,24},{8,0},{24,16},{1,9},{17,25},{9,1},{25,17},{2,10},{18... | collective-permute-start | bytes 589832 | tf_op jit(solution)/shard_map/ppermute | solution.py:446
  4.1 5.5 %collective-permute-start = (bf16[3,16,2048]{2,1,0:T(8,128)(2,1)S(1)}, bf16[3,16,2048]{2,1,0:T(8,128)(2,1)S(1)}, u32[]{:S(2)}, u32[]{:S(2)}) collective-permute-start(bf16[3,16,2048]{2,1,0:T(8,128)(2,1)S(1)} %get-tuple-element.18.own_two.other), channel_id=1, source_target_pairs={{8,16},{16,8},{9,17},{17,9},{10,18},{18,10},{11,19},{19,11},{12,20... | collective-permute-start | bytes 589832 | tf_op jit(solution)/shard_map/ppermute | solution.py:446
  4.8 2.9 %collective-permute-start.1 = (bf16[8,2048]{1,0:T(8,128)(2,1)S(1)}, bf16[8,2048]{1,0:T(8,128)(2,1)S(1)}, u32[]{:S(2)}, u32[]{:S(2)}) collective-permute-start(bf16[8,2048]{1,0:T(8,128)(2,1)S(1)} %get-tuple-element.19), channel_id=1, source_target_pairs={{0,1},{2,3},{4,5},{6,7},{1,0},{3,2},{5,4},{7,6},{8,9},{10,11},{12,... | collective-permute-start | bytes 98312 | tf_op jit(solution)/shard_map/ppermute | solution.py:446
  4.9 2.8 %collective-permute-start.2 = (bf16[8,2048]{1,0:T(8,128)(2,1)S(1)}, bf16[8,2048]{1,0:T(8,128)(2,1)S(1)}, u32[]{:S(2)}, u32[]{:S(2)}) collective-permute-start(bf16[8,2048]{1,0:T(8,128)(2,1)S(1)} %get-tuple-element.20), channel_id=1, source_target_pairs={{1,2},{3,4},{5,6},{2,1},{4,3},{6,5},{9,10},{11,12},{13,14},{10,9},... | collective-permute-start | bytes 98312 | tf_op jit(solution)/shard_map/ppermute | solution.py:446
  9.6 19.0 %copy-start = (bf16[512,160]{1,0:T(8,128)(2,1)S(1)}, bf16[512,160]{1,0:T(8,128)(2,1)}, u32[]{:S(2)}) copy-start(bf16[512,160]{1,0:T(8,128)(2,1)} %constant.8.clone.basis) | copy-start | bytes 491524

commit v7 on v6

--- a/solution.py
+++ b/solution.py
@@ -19,6 +19,7 @@
 PAD_ROWS = 24
 CODES = 32000.0
 STEPS = 32.0
+PIECES = 3
 VMEM = pl.BlockSpec(memory_space=pltpu.VMEM)
 HBM = pl.BlockSpec(memory_space=pltpu.HBM)
 SMEM = pl.BlockSpec(memory_space=pltpu.SMEM)
@@ -42,14 +43,20 @@
     return jnp.dot(left, right, preferred_element_type=jnp.float32)
 
 
+def mode_order(place, kxr):
+    return 2 * place - (2 * place // kxr) * (kxr - 1)
+
+
 def x_tables(width, kxr, grid_rows):
     norm = 1.0 / math.sqrt(width * grid_rows)
-    phase = (np.arange(width)[:, None] * np.arange(kxr)[None, :] % width) * (2.0 * np.pi / width)
+    modes = mode_order(np.arange(kxr), kxr)
+    phase = (np.arange(width // 2)[:, None] * modes[None, :] % width) * (2.0 * np.pi / width)
     table = np.stack([np.cos(phase) * norm, -np.sin(phase) * norm], axis=2)
-    pieces = split_table(table.reshape(width, 2 * kxr), 2)
-    angle = np.arange(kxr) * (2.0 * np.pi / width)
+    table = table.reshape(width // 2, 2, kxr).transpose(1, 0, 2).reshape(width, kxr)
+    angle = modes * (2.0 * np.pi / width)
     turn = np.stack([-np.sin(angle), np.sin(angle)], axis=1).reshape(2 * kxr) * 0.5
     second = np.repeat(-4.0 * np.sin(angle * 0.5) ** 2, 2)
+    pieces = split_table(table, PIECES) + [np.zeros(table.shape, jnp.bfloat16)]
     return np.concatenate(pieces, axis=1), np.stack([turn, second]).astype(np.float32)
 
 
@@ -83,7 +90,7 @@
     ]
     places, gy = lax.axis_index("gz"), lax.axis_index("gy")
     shape = (2 * kxr, kxr)
-    mode = lax.broadcasted_iota(jnp.int32, shape, 0) // 2
+    mode = mode_order(lax.broadcasted_iota(jnp.int32, shape, 0) // 2, kxr)
     other = lax.broadcasted_iota(jnp.int32, shape, 1)
     named = owners[...].astype(jnp.float32)
     owner = jnp.sum(jnp.where(mode == other, named, 0.0), axis=1, keepdims=True)
@@ -98,7 +105,8 @@
     lane = lax.broadcasted_iota(jnp.int32, (2 * kxr, 128), 1)
     here = gy * capacity + lane % (2 * capacity) // 2
     owned = (slot == here) & (part == 0)
-    mode_id = (lax.broadcasted_iota(jnp.int32, (2 * kxr, 128), 0) // 2).astype(jnp.float32)
+    mode_id = mode_order(lax.broadcasted_iota(jnp.int32, (2 * kxr, 128), 0) // 2, kxr)
+    mode_id = mode_id.astype(jnp.float32)
     kx = jnp.sum(jnp.where(owned, mode_id, 0.0), axis=0, keepdims=True)
     filled = jnp.sum(jnp.where(owned, 1.0, 0.0), axis=0, keepdims=True)
 
@@ -200,22 +208,33 @@
     return SMAG_COEF * (squared * lax.rsqrt(squared))
 
 
-def put_lines(lines, cells, fields):
-    count = lines.shape[0] // 2
+def put_lines(lines, step, near, far):
+    cells = pl.ds(step * CHUNK, CHUNK)
+    count = lines.shape[1] // PIECES
     start = 0
-    for field in fields:
-        high, low = split(field)
-        size = field.shape[0]
-        lines[start : start + size, cells] = high
-        lines[count + start : count + start + size, cells] = low
+    for one, other in zip(near, far):
+        size = one.shape[0]
+        for parity, field in enumerate((one + other, one - other)):
+            for piece in range(PIECES):
+                at = piece * count + start
+                part = field.astype(jnp.bfloat16)
+                lines[parity, at : at + size, cells] = part
+                field = field - part.astype(jnp.float32)
         start += size
 
 
 def transformed(lines, table):
-    count, modes = lines.shape[0] // 2, table.shape[1] // 2
-    product = matmul(lines[...], table[...])
-    product = product[:count] + product[count:]
-    return product[:, :modes] + product[:, modes:]
+    count, half = lines.shape[1] // PIECES, lines.shape[2]
+    modes = table.shape[1] // (PIECES + 1)
+    totals = []
+    for parity in range(2):
+        product = matmul(lines[parity], table[parity * half : (parity + 1) * half, :])
+        total = product[:count, : 2 * modes] + product[:count, 2 * modes :]
+        for piece in range(1, PIECES):
+            total = total + product[piece * count : (piece + 1) * count, : 2 * modes]
+        totals.append(total + pltpu.roll(total, modes, 1))
+    lane = lax.broadcasted_iota(jnp.int32, (1, 2 * modes), 1)
+    return jnp.where(lane < modes, *totals)
 
 
 def slope_of(factors, field):
@@ -238,7 +257,7 @@
     sub = lax.broadcasted_iota(jnp.int32, (8, CHUNK), 0)
     ghost_rows = jnp.where((sub == 0) & (gy == groups - 1) | (sub == 7) & (gy == 0), 1.0, 0.0)
 
-    for step in range(width // CHUNK):
+    def fields_at(step):
         here = step * CHUNK
         before, after = (here - 128) % width, (here + CHUNK) % width
         cells = pl.ds(here, CHUNK)
@@ -278,7 +297,11 @@
         squared = squared + 0.25 * (ghost[0] * ghost[0] + ghost[1] * ghost[1])
         viscous = magnitude(squared + STRAIN_FLOOR)
         edge = [viscous * ghost[i] for i in range(3)]
-        put_lines(lines, cells, flat + edge + [jnp.concatenate(rims, axis=0)])
+        return flat + edge + [jnp.concatenate(rims, axis=0)]
+
+    steps = width // CHUNK // 2
+    for step in range(steps):
+        put_lines(lines, step, fields_at(step), fields_at(step + steps))
 
     total = transformed(lines, table)
     pieces = [padded(total[rows * i : rows * (i + 1)]) for i in range(5)]
@@ -289,48 +312,62 @@
         spectra[PAD_ROWS * i : PAD_ROWS * i + piece.shape[0], :] = piece
 
 
-def stress_lines(k, other, plane, row_one, row_two, strain, table, lines):
-    rows, width = other.shape[1:]
+def corrected(k, cells, row_one, row_two, strain):
+    rows = strain.shape[2]
     odd_row = lax.axis_index("gy") % 2
     sign = jnp.where(lax.axis_index("gz") % 2 == k, 1.0, -1.0)
     row = lax.broadcasted_iota(jnp.int32, (rows, CHUNK), 0)
-    for step in range(width // CHUNK):
+    ones = row_one[:, cells].astype(jnp.float32)
+    twos = row_two[:, cells].astype(jnp.float32)
+    lows = jnp.where(odd_row == 0, twos, ones)
+    highs = jnp.where(odd_row == 0, ones, twos)
+
+    def beyond(i):
+        at = 2 * i + k
+        inner = jnp.where(row == 0, -lows[at : at + 1], 0.0)
+        return jnp.where(row == rows - 1, highs[at : at + 1], inner)
+
+    x0, sx2 = strain[k, 0, :, cells], strain[k, 3, :, cells]
+    edge = beyond(1)
+    y1 = strain[k, 1, :, cells] + edge
+    e01 = strain[k, 2, :, cells] + beyond(0)
+    sy2 = strain[k, 4, :, cells] + sign * beyond(2)
+    flat = 0.5 * (x0 * x0 + y1 * y1) + 0.25 * (e01 * e01) + STRAIN_FLOOR
+    return x0, y1, e01, sx2, sy2, flat, sign * edge
+
+
+def stress_lines(slopes_at, other, plane, table, lines):
+    def fields_at(step):
         cells = pl.ds(step * CHUNK, CHUNK)
-        ones = row_one[:, cells].astype(jnp.float32)
-        twos = row_two[:, cells].astype(jnp.float32)
-        lows = jnp.where(odd_row == 0, twos, ones)
-        highs = jnp.where(odd_row == 0, ones, twos)
-        z, beyond = [], []
-        for i in range(3):
-            at = 2 * i + k
-            z.append(plane[i, :, cells].astype(jnp.float32) - other[i, :, cells].astype(jnp.float32))
-            beyond.append(
-                jnp.where(
-                    row == rows - 1,
-                    highs[at : at + 1],
-                    jnp.where(row == 0, -lows[at : at + 1], 0.0),
-                )
-            )
-        x0 = strain[k, 0, :, cells]
-        y1 = strain[k, 1, :, cells] + beyond[1]
-        e01 = strain[k, 2, :, cells] + beyond[0]
-        e02 = z[0] + strain[k, 3, :, cells]
-        e12 = z[1] + strain[k, 4, :, cells] + sign * beyond[2]
-        squared = 0.5 * (x0 * x0 + y1 * y1 + z[2] * z[2]) + STRAIN_FLOOR
-        squared = squared + 0.25 * (e01 * e01 + e02 * e02 + e12 * e12)
+        x0, y1, e01, sx2, sy2, flat, edge = slopes_at(cells)
+        z = [
+            plane[i, :, cells].astype(jnp.float32) - other[i, :, cells].astype(jnp.float32)
+            for i in range(3)
+        ]
+        e02, e12 = z[0] + sx2, z[1] + sy2
+        squared = flat + 0.5 * (z[2] * z[2]) + 0.25 * (e02 * e02 + e12 * e12)
         viscous = magnitude(squared)
         fields = [viscous * field for field in (e01, y1, e12, z[2], e02, x0)]
-        put_lines(lines, cells, fields + [z[2] + sign * beyond[1]])
+        return fields + [z[2] + edge]
+
+    steps = plane.shape[2] // CHUNK // 2
+    for step in range(steps):
+        put_lines(lines, step, fields_at(step), fields_at(step + steps))
     return transformed(lines, table)
 
 
-def late_kernel(other, plane, row_one, row_two, strain, table, out, lines):
-    out[...] = stress_lines(0, other, plane, row_one, row_two, strain, table, lines)
+def late_kernel(other, plane, row_one, row_two, strain, table, out, ready, lines):
+    slopes_at = lambda cells: corrected(0, cells, row_one, row_two, strain)
+    out[...] = stress_lines(slopes_at, other, plane, table, lines)
+    for step in range(plane.shape[2] // CHUNK):
+        cells = pl.ds(step * CHUNK, CHUNK)
+        for i, field in enumerate(corrected(1, cells, row_one, row_two, strain)):
+            ready[i, :, cells] = field
 
 
 def last_kernel(
     planes, groups, capacity,
-    other, plane, row_one, row_two, strain, table, earlier, spectra, factors, pick,
+    other, plane, ready, table, earlier, spectra, factors, pick,
     out, lines, codes,
 ):
     rows = other.shape[1]
@@ -338,7 +375,8 @@
     first = jnp.where(gz == 0, 1.0, 0.0)
     last = jnp.where(gz == planes - 1, 1.0, 0.0)
     odd = gz % 2
-    totals = (earlier, stress_lines(1, other, plane, row_one, row_two, strain, table, lines))
+    slopes_at = lambda cells: [ready[i, :, cells] for i in range(7)]
+    totals = (earlier, stress_lines(slopes_at, other, plane, table, lines))
     parts = []
     for k in range(2):
         sign = jnp.where(odd == k, 1.0, -1.0)
@@ -390,7 +428,7 @@
                 moved = pltpu.roll(pieces[j], distance, 1) if distance else pieces[j]
                 block = jnp.where(lane // share == j, moved, block)
             largest = jnp.max(jnp.abs(block), axis=0, keepdims=True)
-            power = jnp.floor(jnp.log2(jnp.maximum(largest, 1e-35)) * STEPS) + 1.0
+            power = jnp.floor(jnp.log2(jnp.maximum(largest, 1e-30)) * STEPS) + 1.0
             block = jnp.floor(block * (CODES * jnp.exp2(power * (-1.0 / STEPS))) + 0.5)
             rim = pltpu.roll(block[rows:], 2, 0)
             rim = jnp.where(sub_lanes == 0, power, jnp.where(sub_lanes < 3, rim, 0.0))
@@ -504,28 +542,31 @@
         ),
         in_specs=[VMEM] * 4,
         out_specs=(VMEM,) * 2,
-        scratch_shapes=[pltpu.VMEM((2 * (5 * rows + 6 * 8), width), jnp.bfloat16)],
+        scratch_shapes=[pltpu.VMEM((2, PIECES * (5 * rows + 6 * 8), width // 2), jnp.bfloat16)],
         compiler_params=limit,
     )(own_one, own_two, table, factors)
 
     reach = rows + 4
-    held = pltpu.VMEM((2 * 7 * rows, width), jnp.bfloat16)
-    earlier = pl.pallas_call(
+    held = pltpu.VMEM((2, PIECES * 7 * rows, width // 2), jnp.bfloat16)
+    earlier, ready = pl.pallas_call(
         late_kernel,
-        out_shape=jax.ShapeDtypeStruct((7 * rows, 2 * kxr), jnp.float32),
+        out_shape=(
+            jax.ShapeDtypeStruct((7 * rows, 2 * kxr), jnp.float32),
+            jax.ShapeDtypeStruct((7, rows, width), jnp.float32),
+        ),
         in_specs=[VMEM] * 6,
-        out_specs=VMEM,
+        out_specs=(VMEM,) * 2,
         scratch_shapes=[held],
         compiler_params=limit,
     )(own_two, plane_one, row_one, row_two, strain, table)
     outgoing = pl.pallas_call(
         functools.partial(last_kernel, planes, groups, CAP),
         out_shape=jax.ShapeDtypeStruct((planes * groups * reach, 128), jnp.int16),
-        in_specs=[VMEM] * 10,
+        in_specs=[VMEM] * 8,
         out_specs=VMEM,
         scratch_shapes=[held, pltpu.VMEM((groups * reach, 128), jnp.float32)],
         compiler_params=limit,
-    )(own_one, plane_two, row_one, row_two, strain, table, earlier, spectra, factors, pick)
+    )(own_one, plane_two, ready, table, earlier, spectra, factors, pick)
     outgoing = outgoing.reshape(planes * groups, reach // 2, 2, 128)
     received = lax.all_to_all(outgoing, ("gz", "gy"), split_axis=0, concat_axis=0, tiled=True)
     received = received.reshape(planes * groups * reach, 128)

time: 30.2 us -> 30.3 us (level)
  Pallas kernels: 6.09 us -> 6.87 us
  blocking collectives: 18 us -> 17.6 us
  waiting for transfers between devices: 1.34 us -> 1.01 us
    all_to_all x1, blocking collectives: 18 us -> 17.6 us  [per_device(): lax.all_to_all(outgoing, ('gz', 'gy'), split_axis=0, concat_axis=0, tiled...]
    pallas_call x1, Pallas kernels: 0.56 us -> 0.91 us  [per_device(): pl.pallas_call(late_kernel, out_shape=(jax.ShapeDtypeStruct((7 * rows, 2...]
    ppermute x4, waiting for transfers between devices: 1.34 us -> 1.01 us  [exchange(): return lax.ppermute(array, axis, pairs + [(j, i) for i, j in pairs])]
    pallas_call x1, Pallas kernels: 0.87 us -> 1.2 us  [per_device(): pl.pallas_call(functools.partial(early_kernel, groups, planes), out_shape...]
  transfers between devices with their start and end apart: 4 -> 4, of which waited for: 1 -> 1; matrix products, arithmetic and copies ran while one was open for 0% -> 0% of each run, Pallas kernels for 9% -> 11%
where the time goes in v7:
time: 30.3 us; the launch traced here: 30 us
  blocking collectives  17.6 us (58%)
  Pallas kernels  6.87 us (23%)
  starting transfers between devices  4.4 us (15%)
  waiting for transfers between devices  1.01 us (3%)
    all_to_all x1, blocking collectives, per_device(): lax.all_to_all(outgoing, ('gz', 'gy'), split_axis=0, concat_axis=0, tiled...  17.6 us
    ppermute x4, starting transfers between devices, exchange(): return lax.ppermute(array, axis, pairs + [(j, i) for i, j in pairs])  4.4 us
    pallas_call x1, Pallas kernels, per_device(): pl.pallas_call(functools.partial(solve_kernel, kyr, depth, CAP, reach), o...  1.31 us
    pallas_call x1, Pallas kernels, per_device(): pl.pallas_call(functools.partial(mode_kernel, groups, CAP, kyr, levels, d...  1.25 us
    pallas_call x1, Pallas kernels, per_device(): pl.pallas_call(functools.partial(early_kernel, groups, planes), out_shape...  1.2 us
    pallas_call x1, Pallas kernels, per_device(): pl.pallas_call(pack_kernel, out_shape=(plane_shape, plane_shape, row_shap...  1.12 us
    pallas_call x1, Pallas kernels, per_device(): pl.pallas_call(functools.partial(last_kernel, planes, groups, CAP), out_s...  1.08 us
    ppermute x4, waiting for transfers between devices, exchange(): return lax.ppermute(array, axis, pairs + [(j, i) for i, j in pairs])  1.01 us
  transfers between devices with their start and end apart: 4, of which 1 were waited for; matrix products, arithmetic and copies ran while one was open for 0% of the time, Pallas kernels for 11%

profile of v7, /device:TPU:0, one launch (start us, length us, event | category | flops | bytes accessed | tf_op | source)
XLA Modules:
  0.0 30.0 jit_solution(9153930322920880671)
XLA Ops:
  0.0 1.1 %shard_map.100 = (bf16[3,16,2048]{2,1,0:T(8,128)(2,1)S(1)}, bf16[3,16,2048]{2,1,0:T(8,128)(2,1)S(1)}, bf16[8,2048]{1,0:T(8,128)(2,1)S(1)}, bf16[8,2048]{1,0:T(8,...) custom-call(bf16[2,16,2048]{2,1,0:T(8,128)(2,1)} %vx.1, bf16[2,16,2048]{2,1,0:T(8,128)(2,1)} %vy.1, ...), custom_call_target="tpu_custom_call" | custom-call | tf_op jit(solution)/shard_map/pallas_call | solution.py:501
  1.1 3.0 %collective-permute-start.1 = (bf16[3,16,2048]{2,1,0:T(8,128)(2,1)S(1)}, bf16[3,16,2048]{2,1,0:T(8,128)(2,1)S(1)}, u32[]{:S(2)}, u32[]{:S(2)}) collective-permute-start(bf16[3,16,2048]{2,1,0:T(8,128)(2,1)S(1)} %get-tuple-element.19.own_one.other), channel_id=1, source_target_pairs={{0,8},{16,24},{8,0},{24,16},{1,9},{17,25},{9,1},{25,17},{2,10},{18... | collective-permute-start | bytes 589832 | tf_op jit(solution)/shard_map/ppermute | solution.py:484
  4.1 0.7 %collective-permute-start = (bf16[3,16,2048]{2,1,0:T(8,128)(2,1)S(1)}, bf16[3,16,2048]{2,1,0:T(8,128)(2,1)S(1)}, u32[]{:S(2)}, u32[]{:S(2)}) collective-permute-start(bf16[3,16,2048]{2,1,0:T(8,128)(2,1)S(1)} %get-tuple-element.20.own_two.other), channel_id=1, source_target_pairs={{8,16},{16,8},{9,17},{17,9},{10,18},{18,10},{11,19},{19,11},{12,20... | collective-permute-start | bytes 589832 | tf_op jit(solution)/shard_map/ppermute | solution.py:484
  4.8 0.1 collective-permute-start.2
  4.9 0.7 %collective-permute-start.3 = (bf16[8,2048]{1,0:T(8,128)(2,1)S(1)}, bf16[8,2048]{1,0:T(8,128)(2,1)S(1)}, u32[]{:S(2)}, u32[]{:S(2)}) collective-permute-start(bf16[8,2048]{1,0:T(8,128)(2,1)S(1)} %get-tuple-element.22), channel_id=1, source_target_pairs={{1,2},{3,4},{5,6},{2,1},{4,3},{6,5},{9,10},{11,12},{13,14},{10,9},... | collective-permute-start | bytes 98312 | tf_op jit(solution)/shard_map/ppermute | solution.py:484
  5.6 1.2 %shard_map.101 = (bf16[128,256]{1,0:T(8,128)(2,1)S(1)}, f32[2,4,128,128]{3,2,1,0:T(8,128)S(1)}, bf16[2048,256]{1,0:T(8,128)(2,1)S(1)}, f32[2,128]{1,0:T(2,128)S(1)}) custom-call(s32[1,64]{1,0:T(1,128)S(1)} %get-tuple-element.23.owners, f32[24,128]{1,0:T(8,128)S(1)} %get-tuple-element.24.columns, bf16[2048,256]{1,0:T(8,128)(2,1)} %constant.6.clone.table_hbm, ...), custom_call_target="tpu_custom_call" | custom-call | tf_op jit(solution)/shard_map/pallas_call | solution.py:523
  6.8 1.2 %shard_map.102 = (f32[2,5,16,2048]{3,2,1,0:T(8,128)S(1)}, f32[120,128]{1,0:T(8,128)S(1)}) custom-call(bf16[3,16,2048]{2,1,0:T(8,128)(2,1)S(1)} %get-tuple-element.19.own_one.other, bf16[3,16,2048]{2,1,0:T(8,128)(2,1)S(1)} %get-tuple-element.20.own_two.other, bf16[2048,256]{1,0:T(8,128)(2,1)S(1)} %get-tuple-element.25.table, ...), custom_call_target="tpu_custom_call" | custom-call | tf_op jit(solution)/shard_map/pallas_call | solution.py:537
  8.0 0.0 collective-permute-done.2.row_one
  8.0 0.0 collective-permute-done.3.row_two
  8.0 1.0 %collective-permute-done.1.plane = bf16[3,16,2048]{2,1,0:T(8,128)(2,1)S(1)} collective-permute-done((bf16[3,16,2048]{2,1,0:T(8,128)(2,1)S(1)}, bf16[3,16,2048]{2,1,0:T(8,128)(2,1)S(1)}, u32[]{:S(2)}, u32[]{:S(2)}) %collective-permute-start.1) | collective-permute-done | bytes 196640 | tf_op jit(solution)/shard_map/ppermute | solution.py:484
  9.0 0.9 %shard_map.103 = (f32[112,128]{1,0:T(8,128)S(1)}, f32[7,16,2048]{2,1,0:T(8,128)S(1)}) custom-call(bf16[3,16,2048]{2,1,0:T(8,128)(2,1)S(1)} %get-tuple-element.20.own_two.other, bf16[3,16,2048]{2,1,0:T(8,128)(2,1)S(1)} %collective-permute-done.1.plane, bf16[8,2048]{1,0:T(8,128)(2,1)S(1)} %collective-permute-done.2.row_one, ...), custom_call_target="tpu_custom_call" | custom-call | tf_op jit(solution)/shard_map/pallas_call | solution.py:551
  10.0 0.0 collective-permute-done.plane
  10.0 0.0 copy-start
  10.0 1.1 %shard_map.104 = s16[640,128]{1,0:T(8,128)(2,1)S(1)} custom-call(bf16[3,16,2048]{2,1,0:T(8,128)(2,1)S(1)} %get-tuple-element.19.own_one.other, bf16[3,16,2048]{2,1,0:T(8,128)(2,1)S(1)} %collective-permute-done.plane, f32[7,16,2048]{2,1,0:T(8,128)S(1)} %get-tuple-element.28.ready, bf16[2048,256]{1,0:T(8,128)(2,1)S(1)} %get-tuple-element.25.table, ...), custom_call_target="tpu_custom_call" | custom-call | tf_op jit(solution)/shard_map/pallas_call | solution.py:562
  11.1 17.6 %all_to_all.5 = s16[32,10,2,128]{3,2,1,0:T(2,128)(2,1)S(1)} all-to-all(s16[32,10,2,128]{3,2,1,0:T(2,128)(2,1)S(1)} %bitcast.4), channel_id=1, replica_groups=mesh['gz'=4,'gy'=8] {'gz','gy'}, dimensions={0} | all-to-all | bytes 327680 | tf_op jit(solution)/shard_map/all_to_all | solution.py:571
  28.7 0.0 copy-done
  28.7 1.3 %shard_map.105 = f32[32,2,128]{2,1,0:T(2,128)} custom-call(s16[640,128]{1,0:T(8,128)(2,1)S(1)} %bitcast.5, bf16[512,160]{1,0:T(8,128)(2,1)S(1)} %copy-done, f32[2,4,128,128]{3,2,1,0:T(8,128)S(1)} %get-tuple-element.32.green), custom_call_target="tpu_custom_call" | custom-call | tf_op jit(solution)/shard_map/pallas_call | solution.py:575
Async XLA Ops:
  1.1 7.9 %collective-permute-start.1 = (bf16[3,16,2048]{2,1,0:T(8,128)(2,1)S(1)}, bf16[3,16,2048]{2,1,0:T(8,128)(2,1)S(1)}, u32[]{:S(2)}, u32[]{:S(2)}) collective-permute-start(bf16[3,16,2048]{2,1,0:T(8,128)(2,1)S(1)} %get-tuple-element.19.own_one.other), channel_id=1, source_target_pairs={{0,8},{16,24},{8,0},{24,16},{1,9},{17,25},{9,1},{25,17},{2,10},{18... | collective-permute-start | bytes 589832 | tf_op jit(solution)/shard_map/ppermute | solution.py:484
  4.1 5.8 %collective-permute-start = (bf16[3,16,2048]{2,1,0:T(8,128)(2,1)S(1)}, bf16[3,16,2048]{2,1,0:T(8,128)(2,1)S(1)}, u32[]{:S(2)}, u32[]{:S(2)}) collective-permute-start(bf16[3,16,2048]{2,1,0:T(8,128)(2,1)S(1)} %get-tuple-element.20.own_two.other), channel_id=1, source_target_pairs={{8,16},{16,8},{9,17},{17,9},{10,18},{18,10},{11,19},{19,11},{12,20... | collective-permute-start | bytes 589832 | tf_op jit(solution)/shard_map/ppermute | solution.py:484
  4.8 3.2 %collective-permute-start.2 = (bf16[8,2048]{1,0:T(8,128)(2,1)S(1)}, bf16[8,2048]{1,0:T(8,128)(2,1)S(1)}, u32[]{:S(2)}, u32[]{:S(2)}) collective-permute-start(bf16[8,2048]{1,0:T(8,128)(2,1)S(1)} %get-tuple-element.21), channel_id=1, source_target_pairs={{0,1},{2,3},{4,5},{6,7},{1,0},{3,2},{5,4},{7,6},{8,9},{10,11},{12,... | collective-permute-start | bytes 98312 | tf_op jit(solution)/shard_map/ppermute | solution.py:484
  4.9 3.1 %collective-permute-start.3 = (bf16[8,2048]{1,0:T(8,128)(2,1)S(1)}, bf16[8,2048]{1,0:T(8,128)(2,1)S(1)}, u32[]{:S(2)}, u32[]{:S(2)}) collective-permute-start(bf16[8,2048]{1,0:T(8,128)(2,1)S(1)} %get-tuple-element.22), channel_id=1, source_target_pairs={{1,2},{3,4},{5,6},{2,1},{4,3},{6,5},{9,10},{11,12},{13,14},{10,9},... | collective-permute-start | bytes 98312 | tf_op jit(solution)/shard_map/ppermute | solution.py:484
  10.0 18.7 %copy-start = (bf16[512,160]{1,0:T(8,128)(2,1)S(1)}, bf16[512,160]{1,0:T(8,128)(2,1)}, u32[]{:S(2)}) copy-start(bf16[512,160]{1,0:T(8,128)(2,1)} %constant.8.clone.basis) | copy-start | bytes 491524

commit v8 on v7

--- a/solution.py
+++ b/solution.py
@@ -100,7 +100,14 @@
     slot = (owner * capacity + rank).astype(jnp.int32)
     part = lax.broadcasted_iota(jnp.int32, (2 * kxr, 1), 0) % 2
     column = lax.broadcasted_iota(jnp.int32, (2 * kxr, groups * capacity * 2), 1)
-    pick[...] = jnp.where(slot * 2 + part == column, 1.0, 0.0).astype(jnp.bfloat16)
+    chosen = jnp.where(slot * 2 + part == column, 1.0, 0.0)
+    if pick.dtype == jnp.bfloat16:
+        pick[...] = chosen.astype(jnp.bfloat16)
+    else:
+        place = lax.broadcasted_iota(jnp.int32, chosen.shape, 0).astype(jnp.float32)
+        source = jnp.sum(chosen * place, axis=0, keepdims=True).astype(jnp.int32)
+        filled = jnp.sum(chosen, axis=0, keepdims=True).astype(jnp.int32)
+        pick[...] = jnp.concatenate([source, filled] + [source * 0] * 6, axis=0)
 
     lane = lax.broadcasted_iota(jnp.int32, (2 * kxr, 128), 1)
     here = gy * capacity + lane % (2 * capacity) // 2
@@ -408,9 +415,17 @@
     count = len(spectrum)
 
     stacked = jnp.concatenate(spectrum, axis=0)
-    selected = matmul(jnp.concatenate(split(stacked), axis=0), pick[...])
-    size = count * PAD_ROWS
-    selected = selected[:size] + selected[size:]
+    if pick.dtype == jnp.bfloat16:
+        selected = matmul(jnp.concatenate(split(stacked), axis=0), pick[...])
+        size = count * PAD_ROWS
+        selected = selected[:size] + selected[size:]
+    else:
+        halves = []
+        for start in range(0, pick.shape[1], 128):
+            source = jnp.broadcast_to(pick[0:1, start : start + 128], stacked.shape)
+            taken = jnp.take_along_axis(stacked, source, axis=1)
+            halves.append(jnp.where(pick[1:2, start : start + 128] > 0, taken, 0.0))
+        selected = jnp.concatenate(halves, axis=1)
 
     lane = lax.broadcasted_iota(jnp.int32, (PAD_ROWS, 128), 1)
     empty_block = jnp.zeros((PAD_ROWS, 128), jnp.float32)
@@ -520,10 +535,14 @@
     row_two = exchange(row_two, "gy", groups, 1)
 
     table, factors = [jnp.asarray(array) for array in x_tables(width, kxr, rows * groups)]
+    if 2 * kxr == 128:
+        pick_shape = jax.ShapeDtypeStruct((8, groups * CAP * 2), jnp.int32)
+    else:
+        pick_shape = jax.ShapeDtypeStruct((2 * kxr, groups * CAP * 2), jnp.bfloat16)
     pick, green, table, factors = pl.pallas_call(
         functools.partial(mode_kernel, groups, CAP, kyr, levels, depth),
         out_shape=(
-            jax.ShapeDtypeStruct((2 * kxr, groups * CAP * 2), jnp.bfloat16),
+            pick_shape,
             jax.ShapeDtypeStruct((depth, planes, kyr, 128), jnp.float32),
             jax.ShapeDtypeStruct(table.shape, table.dtype),
             jax.ShapeDtypeStruct(factors.shape, factors.dtype),

time: 30.3 us -> 30.3 us (level)
  no operation moved by 1% of the time
where the time goes in v8:
time: 30.3 us; the launch traced here: 30 us
  blocking collectives  17.6 us (58%)
  Pallas kernels  6.82 us (23%)
  starting transfers between devices  4.4 us (15%)
  waiting for transfers between devices  1.02 us (3%)
    all_to_all x1, blocking collectives, per_device(): lax.all_to_all(outgoing, ('gz', 'gy'), split_axis=0, concat_axis=0, tiled...  17.6 us
    ppermute x4, starting transfers between devices, exchange(): return lax.ppermute(array, axis, pairs + [(j, i) for i, j in pairs])  4.4 us
    pallas_call x1, Pallas kernels, per_device(): pl.pallas_call(functools.partial(solve_kernel, kyr, depth, CAP, reach), o...  1.32 us
    pallas_call x1, Pallas kernels, per_device(): pl.pallas_call(functools.partial(mode_kernel, groups, CAP, kyr, levels, d...  1.25 us
    pallas_call x1, Pallas kernels, per_device(): pl.pallas_call(functools.partial(early_kernel, groups, planes), out_shape...  1.2 us
    pallas_call x1, Pallas kernels, per_device(): pl.pallas_call(pack_kernel, out_shape=(plane_shape, plane_shape, row_shap...  1.12 us
    pallas_call x1, Pallas kernels, per_device(): pl.pallas_call(functools.partial(last_kernel, planes, groups, CAP), out_s...  1.02 us
    ppermute x4, waiting for transfers between devices, exchange(): return lax.ppermute(array, axis, pairs + [(j, i) for i, j in pairs])  1.02 us
  transfers between devices with their start and end apart: 4, of which 1 were waited for; matrix products, arithmetic and copies ran while one was open for 0% of the time, Pallas kernels for 11%

profile of v8, /device:TPU:0, one launch (start us, length us, event | category | flops | bytes accessed | tf_op | source)
XLA Modules:
  0.0 30.0 jit_solution(15666589699053794429)
XLA Ops:
  0.0 1.1 %shard_map.100 = (bf16[3,16,2048]{2,1,0:T(8,128)(2,1)S(1)}, bf16[3,16,2048]{2,1,0:T(8,128)(2,1)S(1)}, bf16[8,2048]{1,0:T(8,128)(2,1)S(1)}, bf16[8,2048]{1,0:T(8,...) custom-call(bf16[2,16,2048]{2,1,0:T(8,128)(2,1)} %vx.1, bf16[2,16,2048]{2,1,0:T(8,128)(2,1)} %vy.1, ...), custom_call_target="tpu_custom_call" | custom-call | tf_op jit(solution)/shard_map/pallas_call | solution.py:516
  1.1 3.0 %collective-permute-start.1 = (bf16[3,16,2048]{2,1,0:T(8,128)(2,1)S(1)}, bf16[3,16,2048]{2,1,0:T(8,128)(2,1)S(1)}, u32[]{:S(2)}, u32[]{:S(2)}) collective-permute-start(bf16[3,16,2048]{2,1,0:T(8,128)(2,1)S(1)} %get-tuple-element.19.own_one.other), channel_id=1, source_target_pairs={{0,8},{16,24},{8,0},{24,16},{1,9},{17,25},{9,1},{25,17},{2,10},{18... | collective-permute-start | bytes 589832 | tf_op jit(solution)/shard_map/ppermute | solution.py:499
  4.1 0.7 %collective-permute-start = (bf16[3,16,2048]{2,1,0:T(8,128)(2,1)S(1)}, bf16[3,16,2048]{2,1,0:T(8,128)(2,1)S(1)}, u32[]{:S(2)}, u32[]{:S(2)}) collective-permute-start(bf16[3,16,2048]{2,1,0:T(8,128)(2,1)S(1)} %get-tuple-element.20.own_two.other), channel_id=1, source_target_pairs={{8,16},{16,8},{9,17},{17,9},{10,18},{18,10},{11,19},{19,11},{12,20... | collective-permute-start | bytes 589832 | tf_op jit(solution)/shard_map/ppermute | solution.py:499
  4.8 0.1 collective-permute-start.2
  4.9 0.7 %collective-permute-start.3 = (bf16[8,2048]{1,0:T(8,128)(2,1)S(1)}, bf16[8,2048]{1,0:T(8,128)(2,1)S(1)}, u32[]{:S(2)}, u32[]{:S(2)}) collective-permute-start(bf16[8,2048]{1,0:T(8,128)(2,1)S(1)} %get-tuple-element.22), channel_id=1, source_target_pairs={{1,2},{3,4},{5,6},{2,1},{4,3},{6,5},{9,10},{11,12},{13,14},{10,9},... | collective-permute-start | bytes 98312 | tf_op jit(solution)/shard_map/ppermute | solution.py:499
  5.6 1.2 %shard_map.101 = (s32[8,256]{1,0:T(8,128)S(1)}, f32[2,4,128,128]{3,2,1,0:T(8,128)S(1)}, bf16[2048,256]{1,0:T(8,128)(2,1)S(1)}, f32[2,128]{1,0:T(2,128)S(1)}) custom-call(s32[1,64]{1,0:T(1,128)S(1)} %get-tuple-element.23.owners, f32[24,128]{1,0:T(8,128)S(1)} %get-tuple-element.24.columns, bf16[2048,256]{1,0:T(8,128)(2,1)} %constant.6.clone.table_hbm, ...), custom_call_target="tpu_custom_call" | custom-call | tf_op jit(solution)/shard_map/pallas_call | solution.py:542
  6.8 1.2 %shard_map.102 = (f32[2,5,16,2048]{3,2,1,0:T(8,128)S(1)}, f32[120,128]{1,0:T(8,128)S(1)}) custom-call(bf16[3,16,2048]{2,1,0:T(8,128)(2,1)S(1)} %get-tuple-element.19.own_one.other, bf16[3,16,2048]{2,1,0:T(8,128)(2,1)S(1)} %get-tuple-element.20.own_two.other, bf16[2048,256]{1,0:T(8,128)(2,1)S(1)} %get-tuple-element.25.table, ...), custom_call_target="tpu_custom_call" | custom-call | tf_op jit(solution)/shard_map/pallas_call | solution.py:556
  8.0 0.0 collective-permute-done.2.row_one
  8.0 0.0 collective-permute-done.3.row_two
  8.0 1.0 %collective-permute-done.1.plane = bf16[3,16,2048]{2,1,0:T(8,128)(2,1)S(1)} collective-permute-done((bf16[3,16,2048]{2,1,0:T(8,128)(2,1)S(1)}, bf16[3,16,2048]{2,1,0:T(8,128)(2,1)S(1)}, u32[]{:S(2)}, u32[]{:S(2)}) %collective-permute-start.1) | collective-permute-done | bytes 196640 | tf_op jit(solution)/shard_map/ppermute | solution.py:499
  9.0 0.9 %shard_map.103 = (f32[112,128]{1,0:T(8,128)S(1)}, f32[7,16,2048]{2,1,0:T(8,128)S(1)}) custom-call(bf16[3,16,2048]{2,1,0:T(8,128)(2,1)S(1)} %get-tuple-element.20.own_two.other, bf16[3,16,2048]{2,1,0:T(8,128)(2,1)S(1)} %collective-permute-done.1.plane, bf16[8,2048]{1,0:T(8,128)(2,1)S(1)} %collective-permute-done.2.row_one, ...), custom_call_target="tpu_custom_call" | custom-call | tf_op jit(solution)/shard_map/pallas_call | solution.py:570
  10.0 0.0 collective-permute-done.plane
  10.0 0.0 copy-start
  10.0 1.0 %shard_map.104 = s16[640,128]{1,0:T(8,128)(2,1)S(1)} custom-call(bf16[3,16,2048]{2,1,0:T(8,128)(2,1)S(1)} %get-tuple-element.19.own_one.other, bf16[3,16,2048]{2,1,0:T(8,128)(2,1)S(1)} %collective-permute-done.plane, f32[7,16,2048]{2,1,0:T(8,128)S(1)} %get-tuple-element.28.ready, bf16[2048,256]{1,0:T(8,128)(2,1)S(1)} %get-tuple-element.25.table, ...), custom_call_target="tpu_custom_call" | custom-call | tf_op jit(solution)/shard_map/pallas_call | solution.py:581
  11.0 17.6 %all_to_all.5 = s16[32,10,2,128]{3,2,1,0:T(2,128)(2,1)S(1)} all-to-all(s16[32,10,2,128]{3,2,1,0:T(2,128)(2,1)S(1)} %bitcast.4), channel_id=1, replica_groups=mesh['gz'=4,'gy'=8] {'gz','gy'}, dimensions={0} | all-to-all | bytes 327680 | tf_op jit(solution)/shard_map/all_to_all | solution.py:590
  28.6 0.0 copy-done
  28.6 1.3 %shard_map.105 = f32[32,2,128]{2,1,0:T(2,128)} custom-call(s16[640,128]{1,0:T(8,128)(2,1)S(1)} %bitcast.5, bf16[512,160]{1,0:T(8,128)(2,1)S(1)} %copy-done, f32[2,4,128,128]{3,2,1,0:T(8,128)S(1)} %get-tuple-element.32.green), custom_call_target="tpu_custom_call" | custom-call | tf_op jit(solution)/shard_map/pallas_call | solution.py:594
Async XLA Ops:
  1.1 7.9 %collective-permute-start.1 = (bf16[3,16,2048]{2,1,0:T(8,128)(2,1)S(1)}, bf16[3,16,2048]{2,1,0:T(8,128)(2,1)S(1)}, u32[]{:S(2)}, u32[]{:S(2)}) collective-permute-start(bf16[3,16,2048]{2,1,0:T(8,128)(2,1)S(1)} %get-tuple-element.19.own_one.other), channel_id=1, source_target_pairs={{0,8},{16,24},{8,0},{24,16},{1,9},{17,25},{9,1},{25,17},{2,10},{18... | collective-permute-start | bytes 589832 | tf_op jit(solution)/shard_map/ppermute | solution.py:499
  4.1 5.8 %collective-permute-start = (bf16[3,16,2048]{2,1,0:T(8,128)(2,1)S(1)}, bf16[3,16,2048]{2,1,0:T(8,128)(2,1)S(1)}, u32[]{:S(2)}, u32[]{:S(2)}) collective-permute-start(bf16[3,16,2048]{2,1,0:T(8,128)(2,1)S(1)} %get-tuple-element.20.own_two.other), channel_id=1, source_target_pairs={{8,16},{16,8},{9,17},{17,9},{10,18},{18,10},{11,19},{19,11},{12,20... | collective-permute-start | bytes 589832 | tf_op jit(solution)/shard_map/ppermute | solution.py:499
  4.8 3.2 %collective-permute-start.2 = (bf16[8,2048]{1,0:T(8,128)(2,1)S(1)}, bf16[8,2048]{1,0:T(8,128)(2,1)S(1)}, u32[]{:S(2)}, u32[]{:S(2)}) collective-permute-start(bf16[8,2048]{1,0:T(8,128)(2,1)S(1)} %get-tuple-element.21), channel_id=1, source_target_pairs={{0,1},{2,3},{4,5},{6,7},{1,0},{3,2},{5,4},{7,6},{8,9},{10,11},{12,... | collective-permute-start | bytes 98312 | tf_op jit(solution)/shard_map/ppermute | solution.py:499
  4.9 3.1 %collective-permute-start.3 = (bf16[8,2048]{1,0:T(8,128)(2,1)S(1)}, bf16[8,2048]{1,0:T(8,128)(2,1)S(1)}, u32[]{:S(2)}, u32[]{:S(2)}) collective-permute-start(bf16[8,2048]{1,0:T(8,128)(2,1)S(1)} %get-tuple-element.22), channel_id=1, source_target_pairs={{1,2},{3,4},{5,6},{2,1},{4,3},{6,5},{9,10},{11,12},{13,14},{10,9},... | collective-permute-start | bytes 98312 | tf_op jit(solution)/shard_map/ppermute | solution.py:499
  10.0 18.7 %copy-start = (bf16[512,160]{1,0:T(8,128)(2,1)S(1)}, bf16[512,160]{1,0:T(8,128)(2,1)}, u32[]{:S(2)}) copy-start(bf16[512,160]{1,0:T(8,128)(2,1)} %constant.8.clone.basis) | copy-start | bytes 491524

commit v9 on v8

--- a/solution.py
+++ b/solution.py
@@ -74,20 +74,23 @@
 
 def mode_kernel(
     groups, capacity, kyr, levels, depth,
-    owners, columns, table_hbm, factors_hbm,
-    pick, green, table, factors, arrived,
+    owners_hbm, below_hbm, above_hbm, metric_hbm, table_hbm, factors_hbm,
+    pick, green, table, factors, owners, scalars, arrived, small,
 ):
     copies = [pltpu.make_async_copy(factors_hbm, factors, arrived.at[0])]
     share = table.shape[0] // (arrived.shape[0] - 1)
     for i in range(1, arrived.shape[0]):
         at = pl.ds((i - 1) * share, share)
         copies.append(pltpu.make_async_copy(table_hbm.at[at], table.at[at], arrived.at[i]))
-    for copy in copies:
+    others = [pltpu.make_async_copy(owners_hbm, owners, small.at[3])]
+    for i, array in enumerate((below_hbm, above_hbm, metric_hbm)):
+        others.append(pltpu.make_async_copy(array, scalars.at[i], small.at[i]))
+    for copy in others + copies:
         copy.start()
+    for copy in others:
+        copy.wait()
     kxr = owners.shape[1]
-    below, above, metric = [
-        [columns[i * levels + k : i * levels + k + 1, :] for k in range(levels)] for i in range(3)
-    ]
+    below, above, metric = [[scalars[i, k] for k in range(levels)] for i in range(3)]
     places, gy = lax.axis_index("gz"), lax.axis_index("gy")
     shape = (2 * kxr, kxr)
     mode = mode_order(lax.broadcasted_iota(jnp.int32, shape, 0) // 2, kxr)
@@ -162,35 +165,27 @@
         copy.wait()
 
 
-def pack_kernel(
-    vx, vy, vz, owners_hbm, below_hbm, above_hbm, metric_hbm,
-    own_one, own_two, row_one, row_two, owners, columns, scalars, arrived, small,
-):
-    rows = vx.shape[1]
-    odd, odd_row = lax.axis_index("gz") % 2, lax.axis_index("gy") % 2
+def pack_kernel(vx, vy, vz, own_one, own_two, arrived):
+    odd = lax.axis_index("gz") % 2
     copies = []
-    for i, field in enumerate((vx, vy, vz)):
-        for k, plane in enumerate((own_one, own_two)):
+    for k, plane in enumerate((own_one, own_two)):
+        for i, field in enumerate((vx, vy, vz)):
             level = odd if k else 1 - odd
             copies.append(pltpu.make_async_copy(field.at[level], plane.at[i], arrived.at[i, k]))
-    others = [pltpu.make_async_copy(owners_hbm, owners, small.at[3])]
-    for i, array in enumerate((below_hbm, above_hbm, metric_hbm)):
-        others.append(pltpu.make_async_copy(array, scalars.at[i], small.at[i]))
-    for copy in copies + others:
+    for copy in copies:
         copy.start()
-    sub = lax.broadcasted_iota(jnp.int32, (8, vx.shape[2]), 0)
-    bottom = jnp.zeros((8, vx.shape[2]), jnp.float32)
+    for copy in copies:
+        copy.wait()
+
+
+def row_kernel(own_one, own_two, row_one, row_two):
+    rows, width = own_one.shape[1:]
+    odd_row = lax.axis_index("gy") % 2
+    sub = lax.broadcasted_iota(jnp.int32, (8, width), 0)
+    bottom = jnp.zeros((8, width), jnp.float32)
     top = bottom
-    for copy in others:
-        copy.wait()
-    levels = scalars.shape[1]
-    for i in range(3):
-        for k in range(levels):
-            at = i * levels + k
-            columns[at : at + 1, :] = jnp.full((1, 128), scalars[i, k], jnp.float32)
     for i in range(3):
         for k, plane in enumerate((own_one, own_two)):
-            copies[2 * i + k].wait()
             field = plane[i].astype(jnp.float32)
             bottom = jnp.where(sub == 2 * i + k, field[0:1], bottom)
             top = jnp.where(sub == 2 * i + k, field[rows - 1 : rows], top)
@@ -513,24 +508,23 @@
 
     plane_shape = jax.ShapeDtypeStruct((3, rows, width), jnp.bfloat16)
     row_shape = jax.ShapeDtypeStruct((8, width), jnp.bfloat16)
-    own_one, own_two, row_one, row_two, owners, columns = pl.pallas_call(
+    own_one, own_two = pl.pallas_call(
         pack_kernel,
-        out_shape=(plane_shape, plane_shape, row_shape, row_shape)
-        + (
-            jax.ShapeDtypeStruct((1, kxr), jnp.int32),
-            jax.ShapeDtypeStruct((3 * levels, 128), jnp.float32),
-        ),
-        in_specs=[HBM] * 7,
-        out_specs=(VMEM,) * 6,
-        scratch_shapes=[
-            pltpu.SMEM((3, levels), jnp.float32),
-            pltpu.SemaphoreType.DMA((3, 2)),
-            pltpu.SemaphoreType.DMA((4,)),
-        ],
+        out_shape=(plane_shape, plane_shape),
+        in_specs=[HBM] * 3,
+        out_specs=(VMEM,) * 2,
+        scratch_shapes=[pltpu.SemaphoreType.DMA((3, 2))],
         compiler_params=limit,
-    )(*[in_hbm(array) for array in (*fields, owners.reshape(1, kxr), below, above, metric)])
+    )(*[in_hbm(field) for field in fields])
     plane_one = exchange(own_one, "gz", planes, 0)
     plane_two = exchange(own_two, "gz", planes, 1)
+    row_one, row_two = pl.pallas_call(
+        row_kernel,
+        out_shape=(row_shape, row_shape),
+        in_specs=[VMEM] * 2,
+        out_specs=(VMEM,) * 2,
+        compiler_params=limit,
+    )(own_one, own_two)
     row_one = exchange(row_one, "gy", groups, 0)
     row_two = exchange(row_two, "gy", groups, 1)
 
@@ -547,11 +541,16 @@
             jax.ShapeDtypeStruct(table.shape, table.dtype),
             jax.ShapeDtypeStruct(factors.shape, factors.dtype),
         ),
-        in_specs=[VMEM, VMEM, HBM, HBM],
+        in_specs=[HBM] * 6,
         out_specs=(VMEM,) * 4,
-        scratch_shapes=[pltpu.SemaphoreType.DMA((5,))],
+        scratch_shapes=[
+            pltpu.VMEM((1, kxr), jnp.int32),
+            pltpu.SMEM((3, levels), jnp.float32),
+            pltpu.SemaphoreType.DMA((5,)),
+            pltpu.SemaphoreType.DMA((4,)),
+        ],
         compiler_params=limit,
-    )(owners, columns, in_hbm(table), in_hbm(factors))
+    )(*map(in_hbm, (owners.reshape(1, kxr), below, above, metric, table, factors)))
 
     strain, spectra = pl.pallas_call(
         functools.partial(early_kernel, groups, planes),

time: 30.3 us -> 30.2 us (level)
  waiting for transfers between devices: 1.02 us -> 0.61 us
  Pallas kernels: 6.82 us -> 7.14 us
    ppermute x4, waiting for transfers between devices: 1.02 us -> 0.61 us  [exchange(): return lax.ppermute(array, axis, pairs + [(j, i) for i, j in pairs])]
    pallas_call x1, Pallas kernels: 1.25 us -> 1.58 us  [per_device(): pl.pallas_call(functools.partial(mode_kernel, groups, CAP, kyr, levels, d...]
    pallas_call x1 -> x2, Pallas kernels: 1.12 us -> 1.14 us  [the longest x1 1.05 us: per_device(): pl.pallas_call(pack_kernel, out_shape=(plane_shape, plane_shape), in_spec...]
  transfers between devices with their start and end apart: 4 -> 4, of which waited for: 1 -> 1; matrix products, arithmetic and copies ran while one was open for 0% -> 0% of each run, Pallas kernels for 11% -> 13%
where the time goes in v9:
time: 30.2 us; the launch traced here: 29.9 us
  blocking collectives  17.7 us (59%)
  Pallas kernels  7.14 us (24%)
  starting transfers between devices  4.4 us (15%)
  waiting for transfers between devices  0.61 us (2%)
    all_to_all x1, blocking collectives, per_device(): lax.all_to_all(outgoing, ('gz', 'gy'), split_axis=0, concat_axis=0, tiled...  17.7 us
    ppermute x4, starting transfers between devices, exchange(): return lax.ppermute(array, axis, pairs + [(j, i) for i, j in pairs])  4.4 us
    pallas_call x1, Pallas kernels, per_device(): pl.pallas_call(functools.partial(mode_kernel, groups, CAP, kyr, levels, d...  1.58 us
    pallas_call x1, Pallas kernels, per_device(): pl.pallas_call(functools.partial(solve_kernel, kyr, depth, CAP, reach), o...  1.32 us
    pallas_call x1, Pallas kernels, per_device(): pl.pallas_call(functools.partial(early_kernel, groups, planes), out_shape...  1.17 us
    pallas_call x1, Pallas kernels, per_device(): pl.pallas_call(pack_kernel, out_shape=(plane_shape, plane_shape), in_spec...  1.05 us
    pallas_call x1, Pallas kernels, per_device(): pl.pallas_call(functools.partial(last_kernel, planes, groups, CAP), out_s...  1.01 us
    pallas_call x1, Pallas kernels, per_device(): pl.pallas_call(late_kernel, out_shape=(jax.ShapeDtypeStruct((7 * rows, 2...  0.91 us
  transfers between devices with their start and end apart: 4, of which 1 were waited for; matrix products, arithmetic and copies ran while one was open for 0% of the time, Pallas kernels for 13%

profile of v9, /device:TPU:0, one launch (start us, length us, event | category | flops | bytes accessed | tf_op | source)
XLA Modules:
  0.0 29.9 jit_solution(6820123345897796980)
XLA Ops:
  0.0 1.0 %shard_map.100 = (bf16[3,16,2048]{2,1,0:T(8,128)(2,1)S(1)}, bf16[3,16,2048]{2,1,0:T(8,128)(2,1)S(1)}) custom-call(bf16[2,16,2048]{2,1,0:T(8,128)(2,1)} %vx.1, bf16[2,16,2048]{2,1,0:T(8,128)(2,1)} %vy.1, bf16[2,16,2048]{2,1,0:T(8,128)(2,1)} %vz.1), custom_call_target="tpu_custom_call" | custom-call | tf_op jit(solution)/shard_map/pallas_call | solution.py:511
  1.1 3.0 %collective-permute-start.1 = (bf16[3,16,2048]{2,1,0:T(8,128)(2,1)S(1)}, bf16[3,16,2048]{2,1,0:T(8,128)(2,1)S(1)}, u32[]{:S(2)}, u32[]{:S(2)}) collective-permute-start(bf16[3,16,2048]{2,1,0:T(8,128)(2,1)S(1)} %get-tuple-element.17.own_one.other), channel_id=1, source_target_pairs={{0,8},{16,24},{8,0},{24,16},{1,9},{17,25},{9,1},{25,17},{2,10},{18... | collective-permute-start | bytes 589832 | tf_op jit(solution)/shard_map/ppermute | solution.py:494
  4.1 0.7 %collective-permute-start = (bf16[3,16,2048]{2,1,0:T(8,128)(2,1)S(1)}, bf16[3,16,2048]{2,1,0:T(8,128)(2,1)S(1)}, u32[]{:S(2)}, u32[]{:S(2)}) collective-permute-start(bf16[3,16,2048]{2,1,0:T(8,128)(2,1)S(1)} %get-tuple-element.18.own_two.other), channel_id=1, source_target_pairs={{8,16},{16,8},{9,17},{17,9},{10,18},{18,10},{11,19},{19,11},{12,20... | collective-permute-start | bytes 589832 | tf_op jit(solution)/shard_map/ppermute | solution.py:494
  4.7 0.1 shard_map.101
  4.8 0.1 collective-permute-start.2
  4.9 0.7 %collective-permute-start.3 = (bf16[8,2048]{1,0:T(8,128)(2,1)S(1)}, bf16[8,2048]{1,0:T(8,128)(2,1)S(1)}, u32[]{:S(2)}, u32[]{:S(2)}) collective-permute-start(bf16[8,2048]{1,0:T(8,128)(2,1)S(1)} %get-tuple-element.20), channel_id=1, source_target_pairs={{1,2},{3,4},{5,6},{2,1},{4,3},{6,5},{9,10},{11,12},{13,14},{10,9},... | collective-permute-start | bytes 98312 | tf_op jit(solution)/shard_map/ppermute | solution.py:494
  5.6 1.6 %shard_map.102 = (s32[8,256]{1,0:T(8,128)S(1)}, f32[2,4,128,128]{3,2,1,0:T(8,128)S(1)}, bf16[2048,256]{1,0:T(8,128)(2,1)S(1)}, f32[2,128]{1,0:T(2,128)S(1)}) custom-call(s32[1,64]{1,0:T(1,128)} %bitcast.6, f32[8]{0:T(128)} %below_hbm.1, f32[8]{0:T(128)} %above_hbm.1, f32[8]{0:T(128)} %metric_hbm.1, bf16[2048,256]{1,0:T(8,128)(2,1)} %constant.6.clone.table_hbm, ...), custom_call_target="tpu_custom_call" | custom-call | tf_op jit(solution)/shard_map/pallas_call | solution.py:536
  7.2 1.2 %shard_map.103 = (f32[2,5,16,2048]{3,2,1,0:T(8,128)S(1)}, f32[120,128]{1,0:T(8,128)S(1)}) custom-call(bf16[3,16,2048]{2,1,0:T(8,128)(2,1)S(1)} %get-tuple-element.17.own_one.other, bf16[3,16,2048]{2,1,0:T(8,128)(2,1)S(1)} %get-tuple-element.18.own_two.other, bf16[2048,256]{1,0:T(8,128)(2,1)S(1)} %get-tuple-element.21.table, ...), custom_call_target="tpu_custom_call" | custom-call | tf_op jit(solution)/shard_map/pallas_call | solution.py:555
  8.3 0.0 collective-permute-done.2.row_one
  8.4 0.0 collective-permute-done.3.row_two
  8.4 0.6 %collective-permute-done.1.plane = bf16[3,16,2048]{2,1,0:T(8,128)(2,1)S(1)} collective-permute-done((bf16[3,16,2048]{2,1,0:T(8,128)(2,1)S(1)}, bf16[3,16,2048]{2,1,0:T(8,128)(2,1)S(1)}, u32[]{:S(2)}, u32[]{:S(2)}) %collective-permute-start.1) | collective-permute-done | bytes 196640 | tf_op jit(solution)/shard_map/ppermute | solution.py:494
  9.0 0.9 %shard_map.104 = (f32[112,128]{1,0:T(8,128)S(1)}, f32[7,16,2048]{2,1,0:T(8,128)S(1)}) custom-call(bf16[3,16,2048]{2,1,0:T(8,128)(2,1)S(1)} %get-tuple-element.18.own_two.other, bf16[3,16,2048]{2,1,0:T(8,128)(2,1)S(1)} %collective-permute-done.1.plane, bf16[8,2048]{1,0:T(8,128)(2,1)S(1)} %collective-permute-done.2.row_one, ...), custom_call_target="tpu_custom_call" | custom-call | tf_op jit(solution)/shard_map/pallas_call | solution.py:569
  9.9 0.0 collective-permute-done.plane
  9.9 0.0 copy-start
  9.9 1.0 %shard_map.105 = s16[640,128]{1,0:T(8,128)(2,1)S(1)} custom-call(bf16[3,16,2048]{2,1,0:T(8,128)(2,1)S(1)} %get-tuple-element.17.own_one.other, bf16[3,16,2048]{2,1,0:T(8,128)(2,1)S(1)} %collective-permute-done.plane, f32[7,16,2048]{2,1,0:T(8,128)S(1)} %get-tuple-element.24.ready, bf16[2048,256]{1,0:T(8,128)(2,1)S(1)} %get-tuple-element.21.table, ...), custom_call_target="tpu_custom_call" | custom-call | tf_op jit(solution)/shard_map/pallas_call | solution.py:580
  10.9 17.7 %all_to_all.5 = s16[32,10,2,128]{3,2,1,0:T(2,128)(2,1)S(1)} all-to-all(s16[32,10,2,128]{3,2,1,0:T(2,128)(2,1)S(1)} %bitcast.4), channel_id=1, replica_groups=mesh['gz'=4,'gy'=8] {'gz','gy'}, dimensions={0} | all-to-all | bytes 327680 | tf_op jit(solution)/shard_map/all_to_all | solution.py:589
  28.6 0.0 copy-done
  28.6 1.3 %shard_map.106 = f32[32,2,128]{2,1,0:T(2,128)} custom-call(s16[640,128]{1,0:T(8,128)(2,1)S(1)} %bitcast.5, bf16[512,160]{1,0:T(8,128)(2,1)S(1)} %copy-done, f32[2,4,128,128]{3,2,1,0:T(8,128)S(1)} %get-tuple-element.28.green), custom_call_target="tpu_custom_call" | custom-call | tf_op jit(solution)/shard_map/pallas_call | solution.py:593
Async XLA Ops:
  1.1 7.9 %collective-permute-start.1 = (bf16[3,16,2048]{2,1,0:T(8,128)(2,1)S(1)}, bf16[3,16,2048]{2,1,0:T(8,128)(2,1)S(1)}, u32[]{:S(2)}, u32[]{:S(2)}) collective-permute-start(bf16[3,16,2048]{2,1,0:T(8,128)(2,1)S(1)} %get-tuple-element.17.own_one.other), channel_id=1, source_target_pairs={{0,8},{16,24},{8,0},{24,16},{1,9},{17,25},{9,1},{25,17},{2,10},{18... | collective-permute-start | bytes 589832 | tf_op jit(solution)/shard_map/ppermute | solution.py:494
  4.1 5.8 %collective-permute-start = (bf16[3,16,2048]{2,1,0:T(8,128)(2,1)S(1)}, bf16[3,16,2048]{2,1,0:T(8,128)(2,1)S(1)}, u32[]{:S(2)}, u32[]{:S(2)}) collective-permute-start(bf16[3,16,2048]{2,1,0:T(8,128)(2,1)S(1)} %get-tuple-element.18.own_two.other), channel_id=1, source_target_pairs={{8,16},{16,8},{9,17},{17,9},{10,18},{18,10},{11,19},{19,11},{12,20... | collective-permute-start | bytes 589832 | tf_op jit(solution)/shard_map/ppermute | solution.py:494
  4.8 3.5 %collective-permute-start.2 = (bf16[8,2048]{1,0:T(8,128)(2,1)S(1)}, bf16[8,2048]{1,0:T(8,128)(2,1)S(1)}, u32[]{:S(2)}, u32[]{:S(2)}) collective-permute-start(bf16[8,2048]{1,0:T(8,128)(2,1)S(1)} %get-tuple-element.19), channel_id=1, source_target_pairs={{0,1},{2,3},{4,5},{6,7},{1,0},{3,2},{5,4},{7,6},{8,9},{10,11},{12,... | collective-permute-start | bytes 98312 | tf_op jit(solution)/shard_map/ppermute | solution.py:494
  4.9 3.5 %collective-permute-start.3 = (bf16[8,2048]{1,0:T(8,128)(2,1)S(1)}, bf16[8,2048]{1,0:T(8,128)(2,1)S(1)}, u32[]{:S(2)}, u32[]{:S(2)}) collective-permute-start(bf16[8,2048]{1,0:T(8,128)(2,1)S(1)} %get-tuple-element.20), channel_id=1, source_target_pairs={{1,2},{3,4},{5,6},{2,1},{4,3},{6,5},{9,10},{11,12},{13,14},{10,9},... | collective-permute-start | bytes 98312 | tf_op jit(solution)/shard_map/ppermute | solution.py:494
  9.9 18.7 %copy-start = (bf16[512,160]{1,0:T(8,128)(2,1)S(1)}, bf16[512,160]{1,0:T(8,128)(2,1)}, u32[]{:S(2)}) copy-start(bf16[512,160]{1,0:T(8,128)(2,1)} %constant.8.clone.basis) | copy-start | bytes 491524

commit v10 on v9

--- a/solution.py
+++ b/solution.py
@@ -16,7 +16,7 @@
 MODE_SHIFT = 0.02
 
 CHUNK = 256
-PAD_ROWS = 24
+MARGIN = 8
 CODES = 32000.0
 STEPS = 32.0
 PIECES = 3
@@ -194,7 +194,7 @@
 
 
 def up(field):
-    return pltpu.roll(field, PAD_ROWS - 1, 0)
+    return pltpu.roll(field, field.shape[0] - 1, 0)
 
 
 def down(field):
@@ -202,7 +202,7 @@
 
 
 def padded(field):
-    empty = jnp.zeros((PAD_ROWS - field.shape[0], field.shape[1]), field.dtype)
+    empty = jnp.zeros((MARGIN, field.shape[1]), field.dtype)
     return jnp.concatenate([field, empty], axis=0)
 
 
@@ -311,7 +311,8 @@
     cross = 0.25 * (up(t12) - down(t12)) + slope_of(factors, t02)
     pieces = pieces[:2] + [s22 + (last - first) * cross]
     for i, piece in enumerate(pieces + [total[5 * rows :]]):
-        spectra[PAD_ROWS * i : PAD_ROWS * i + piece.shape[0], :] = piece
+        start = (rows + MARGIN) * i
+        spectra[start : start + piece.shape[0], :] = piece
 
 
 def corrected(k, cells, row_one, row_two, strain):
@@ -373,6 +374,7 @@
     out, lines, codes,
 ):
     rows = other.shape[1]
+    padded_rows = rows + MARGIN
     gz = lax.axis_index("gz")
     first = jnp.where(gz == 0, 1.0, 0.0)
     last = jnp.where(gz == planes - 1, 1.0, 0.0)
@@ -384,21 +386,21 @@
         sign = jnp.where(odd == k, 1.0, -1.0)
         pieces = [totals[k][rows * i : rows * (i + 1)] for i in range(7)]
         for i in range(3):
-            start = 3 * PAD_ROWS + 8 * (3 * k + i)
-            pieces[i] = jnp.concatenate([pieces[i], spectra[start : start + 8, :]], axis=0)
+            start = 3 * padded_rows + MARGIN * (3 * k + i)
+            pieces[i] = jnp.concatenate([pieces[i], spectra[start : start + MARGIN, :]], axis=0)
         t01, p11, t12 = pieces[:3]
         s22, t02, s00, rise = [padded(piece) for piece in pieces[3:]]
         p11 = up(p11) + down(p11) - 2.0 * p11
         t01 = up(t01) - down(t01)
         t12 = 0.25 * (up(t12) - down(t12))
-        flat = spectra[k * PAD_ROWS : (k + 1) * PAD_ROWS, :]
+        flat = spectra[k * padded_rows : (k + 1) * padded_rows, :]
         s22, rise = sign * s22, sign * rise
         middle = p11 - 2.0 * s22 + 0.5 * (flat + rise)
         middle = middle + slope_of(factors, t01) + factors[1:2] * s00
         cross = sign * (t12 + slope_of(factors, t02))
         parts.append([s22 + cross, middle, s22 - cross])
 
-    ghost = spectra[2 * PAD_ROWS : 3 * PAD_ROWS, :]
+    ghost = spectra[2 * padded_rows : 3 * padded_rows, :]
     lower = [jnp.where(odd == 1, p, q) for p, q in zip(*parts)]
     upper = [jnp.where(odd == 1, q, p) for p, q in zip(*parts)]
     spectrum = [
@@ -412,7 +414,7 @@
     stacked = jnp.concatenate(spectrum, axis=0)
     if pick.dtype == jnp.bfloat16:
         selected = matmul(jnp.concatenate(split(stacked), axis=0), pick[...])
-        size = count * PAD_ROWS
+        size = count * padded_rows
         selected = selected[:size] + selected[size:]
     else:
         halves = []
@@ -422,13 +424,13 @@
             halves.append(jnp.where(pick[1:2, start : start + 128] > 0, taken, 0.0))
         selected = jnp.concatenate(halves, axis=1)
 
-    lane = lax.broadcasted_iota(jnp.int32, (PAD_ROWS, 128), 1)
-    empty_block = jnp.zeros((PAD_ROWS, 128), jnp.float32)
+    lane = lax.broadcasted_iota(jnp.int32, (padded_rows, 128), 1)
+    empty_block = jnp.zeros((padded_rows, 128), jnp.float32)
     sub_lanes = lax.broadcasted_iota(jnp.int32, (8, 128), 0)
     share = 2 * capacity
     for half in range(groups * share // 128):
         pieces = [
-            selected[PAD_ROWS * j : PAD_ROWS * (j + 1), 128 * half : 128 * (half + 1)]
+            selected[padded_rows * j : padded_rows * (j + 1), 128 * half : 128 * (half + 1)]
             for j in range(count)
         ]
         for place in range(128 // share):
@@ -556,11 +558,11 @@
         functools.partial(early_kernel, groups, planes),
         out_shape=(
             jax.ShapeDtypeStruct((depth, 5, rows, width), jnp.float32),
-            jax.ShapeDtypeStruct((3 * PAD_ROWS + 6 * 8, 2 * kxr), jnp.float32),
+            jax.ShapeDtypeStruct((3 * (rows + MARGIN) + 6 * MARGIN, 2 * kxr), jnp.float32),
         ),
         in_specs=[VMEM] * 4,
         out_specs=(VMEM,) * 2,
-        scratch_shapes=[pltpu.VMEM((2, PIECES * (5 * rows + 6 * 8), width // 2), jnp.bfloat16)],
+        scratch_shapes=[pltpu.VMEM((2, PIECES * (5 * rows + 6 * MARGIN), width // 2), jnp.bfloat16)],
         compiler_params=limit,
     )(own_one, own_two, table, factors)
 

time: 30.2 us -> 30.2 us (level)
  no operation moved by 1% of the time
where the time goes in v10:
time: 30.2 us; the launch traced here: 29.9 us
  blocking collectives  17.7 us (59%)
  Pallas kernels  7.14 us (24%)
  starting transfers between devices  4.4 us (15%)
  waiting for transfers between devices  0.61 us (2%)
    all_to_all x1, blocking collectives, per_device(): lax.all_to_all(outgoing, ('gz', 'gy'), split_axis=0, concat_axis=0, tiled...  17.7 us
    ppermute x4, starting transfers between devices, exchange(): return lax.ppermute(array, axis, pairs + [(j, i) for i, j in pairs])  4.4 us
    pallas_call x1, Pallas kernels, per_device(): pl.pallas_call(functools.partial(mode_kernel, groups, CAP, kyr, levels, d...  1.58 us
    pallas_call x1, Pallas kernels, per_device(): pl.pallas_call(functools.partial(solve_kernel, kyr, depth, CAP, reach), o...  1.32 us
    pallas_call x1, Pallas kernels, per_device(): pl.pallas_call(functools.partial(early_kernel, groups, planes), out_shape...  1.17 us
    pallas_call x1, Pallas kernels, per_device(): pl.pallas_call(pack_kernel, out_shape=(plane_shape, plane_shape), in_spec...  1.05 us
    pallas_call x1, Pallas kernels, per_device(): pl.pallas_call(functools.partial(last_kernel, planes, groups, CAP), out_s...  1.01 us
    pallas_call x1, Pallas kernels, per_device(): pl.pallas_call(late_kernel, out_shape=(jax.ShapeDtypeStruct((7 * rows, 2...  0.91 us
  transfers between devices with their start and end apart: 4, of which 1 were waited for; matrix products, arithmetic and copies ran while one was open for 0% of the time, Pallas kernels for 13%

profile of v10, /device:TPU:0, one launch (start us, length us, event | category | flops | bytes accessed | tf_op | source)
XLA Modules:
  0.0 29.9 jit_solution(6820123345897796980)
XLA Ops:
  0.0 1.0 %shard_map.100 = (bf16[3,16,2048]{2,1,0:T(8,128)(2,1)S(1)}, bf16[3,16,2048]{2,1,0:T(8,128)(2,1)S(1)}) custom-call(bf16[2,16,2048]{2,1,0:T(8,128)(2,1)} %vx.1, bf16[2,16,2048]{2,1,0:T(8,128)(2,1)} %vy.1, bf16[2,16,2048]{2,1,0:T(8,128)(2,1)} %vz.1), custom_call_target="tpu_custom_call" | custom-call | tf_op jit(solution)/shard_map/pallas_call | solution.py:513
  1.1 3.0 %collective-permute-start.1 = (bf16[3,16,2048]{2,1,0:T(8,128)(2,1)S(1)}, bf16[3,16,2048]{2,1,0:T(8,128)(2,1)S(1)}, u32[]{:S(2)}, u32[]{:S(2)}) collective-permute-start(bf16[3,16,2048]{2,1,0:T(8,128)(2,1)S(1)} %get-tuple-element.17.own_one.other), channel_id=1, source_target_pairs={{0,8},{16,24},{8,0},{24,16},{1,9},{17,25},{9,1},{25,17},{2,10},{18... | collective-permute-start | bytes 589832 | tf_op jit(solution)/shard_map/ppermute | solution.py:496
  4.1 0.7 %collective-permute-start = (bf16[3,16,2048]{2,1,0:T(8,128)(2,1)S(1)}, bf16[3,16,2048]{2,1,0:T(8,128)(2,1)S(1)}, u32[]{:S(2)}, u32[]{:S(2)}) collective-permute-start(bf16[3,16,2048]{2,1,0:T(8,128)(2,1)S(1)} %get-tuple-element.18.own_two.other), channel_id=1, source_target_pairs={{8,16},{16,8},{9,17},{17,9},{10,18},{18,10},{11,19},{19,11},{12,20... | collective-permute-start | bytes 589832 | tf_op jit(solution)/shard_map/ppermute | solution.py:496
  4.7 0.1 shard_map.101
  4.8 0.1 collective-permute-start.2
  4.9 0.7 %collective-permute-start.3 = (bf16[8,2048]{1,0:T(8,128)(2,1)S(1)}, bf16[8,2048]{1,0:T(8,128)(2,1)S(1)}, u32[]{:S(2)}, u32[]{:S(2)}) collective-permute-start(bf16[8,2048]{1,0:T(8,128)(2,1)S(1)} %get-tuple-element.20), channel_id=1, source_target_pairs={{1,2},{3,4},{5,6},{2,1},{4,3},{6,5},{9,10},{11,12},{13,14},{10,9},... | collective-permute-start | bytes 98312 | tf_op jit(solution)/shard_map/ppermute | solution.py:496
  5.6 1.6 %shard_map.102 = (s32[8,256]{1,0:T(8,128)S(1)}, f32[2,4,128,128]{3,2,1,0:T(8,128)S(1)}, bf16[2048,256]{1,0:T(8,128)(2,1)S(1)}, f32[2,128]{1,0:T(2,128)S(1)}) custom-call(s32[1,64]{1,0:T(1,128)} %bitcast.6, f32[8]{0:T(128)} %below_hbm.1, f32[8]{0:T(128)} %above_hbm.1, f32[8]{0:T(128)} %metric_hbm.1, bf16[2048,256]{1,0:T(8,128)(2,1)} %constant.6.clone.table_hbm, ...), custom_call_target="tpu_custom_call" | custom-call | tf_op jit(solution)/shard_map/pallas_call | solution.py:538
  7.2 1.2 %shard_map.103 = (f32[2,5,16,2048]{3,2,1,0:T(8,128)S(1)}, f32[120,128]{1,0:T(8,128)S(1)}) custom-call(bf16[3,16,2048]{2,1,0:T(8,128)(2,1)S(1)} %get-tuple-element.17.own_one.other, bf16[3,16,2048]{2,1,0:T(8,128)(2,1)S(1)} %get-tuple-element.18.own_two.other, bf16[2048,256]{1,0:T(8,128)(2,1)S(1)} %get-tuple-element.21.table, ...), custom_call_target="tpu_custom_call" | custom-call | tf_op jit(solution)/shard_map/pallas_call | solution.py:557
  8.3 0.0 collective-permute-done.2.row_one
  8.4 0.0 collective-permute-done.3.row_two
  8.4 0.6 %collective-permute-done.1.plane = bf16[3,16,2048]{2,1,0:T(8,128)(2,1)S(1)} collective-permute-done((bf16[3,16,2048]{2,1,0:T(8,128)(2,1)S(1)}, bf16[3,16,2048]{2,1,0:T(8,128)(2,1)S(1)}, u32[]{:S(2)}, u32[]{:S(2)}) %collective-permute-start.1) | collective-permute-done | bytes 196640 | tf_op jit(solution)/shard_map/ppermute | solution.py:496
  9.0 0.9 %shard_map.104 = (f32[112,128]{1,0:T(8,128)S(1)}, f32[7,16,2048]{2,1,0:T(8,128)S(1)}) custom-call(bf16[3,16,2048]{2,1,0:T(8,128)(2,1)S(1)} %get-tuple-element.18.own_two.other, bf16[3,16,2048]{2,1,0:T(8,128)(2,1)S(1)} %collective-permute-done.1.plane, bf16[8,2048]{1,0:T(8,128)(2,1)S(1)} %collective-permute-done.2.row_one, ...), custom_call_target="tpu_custom_call" | custom-call | tf_op jit(solution)/shard_map/pallas_call | solution.py:571
  9.9 0.0 collective-permute-done.plane
  9.9 0.0 copy-start
  9.9 1.0 %shard_map.105 = s16[640,128]{1,0:T(8,128)(2,1)S(1)} custom-call(bf16[3,16,2048]{2,1,0:T(8,128)(2,1)S(1)} %get-tuple-element.17.own_one.other, bf16[3,16,2048]{2,1,0:T(8,128)(2,1)S(1)} %collective-permute-done.plane, f32[7,16,2048]{2,1,0:T(8,128)S(1)} %get-tuple-element.24.ready, bf16[2048,256]{1,0:T(8,128)(2,1)S(1)} %get-tuple-element.21.table, ...), custom_call_target="tpu_custom_call" | custom-call | tf_op jit(solution)/shard_map/pallas_call | solution.py:582
  10.9 17.7 %all_to_all.5 = s16[32,10,2,128]{3,2,1,0:T(2,128)(2,1)S(1)} all-to-all(s16[32,10,2,128]{3,2,1,0:T(2,128)(2,1)S(1)} %bitcast.4), channel_id=1, replica_groups=mesh['gz'=4,'gy'=8] {'gz','gy'}, dimensions={0} | all-to-all | bytes 327680 | tf_op jit(solution)/shard_map/all_to_all | solution.py:591
  28.6 0.0 copy-done
  28.6 1.3 %shard_map.106 = f32[32,2,128]{2,1,0:T(2,128)} custom-call(s16[640,128]{1,0:T(8,128)(2,1)S(1)} %bitcast.5, bf16[512,160]{1,0:T(8,128)(2,1)S(1)} %copy-done, f32[2,4,128,128]{3,2,1,0:T(8,128)S(1)} %get-tuple-element.28.green), custom_call_target="tpu_custom_call" | custom-call | tf_op jit(solution)/shard_map/pallas_call | solution.py:595
Async XLA Ops:
  1.1 7.9 %collective-permute-start.1 = (bf16[3,16,2048]{2,1,0:T(8,128)(2,1)S(1)}, bf16[3,16,2048]{2,1,0:T(8,128)(2,1)S(1)}, u32[]{:S(2)}, u32[]{:S(2)}) collective-permute-start(bf16[3,16,2048]{2,1,0:T(8,128)(2,1)S(1)} %get-tuple-element.17.own_one.other), channel_id=1, source_target_pairs={{0,8},{16,24},{8,0},{24,16},{1,9},{17,25},{9,1},{25,17},{2,10},{18... | collective-permute-start | bytes 589832 | tf_op jit(solution)/shard_map/ppermute | solution.py:496
  4.1 5.8 %collective-permute-start = (bf16[3,16,2048]{2,1,0:T(8,128)(2,1)S(1)}, bf16[3,16,2048]{2,1,0:T(8,128)(2,1)S(1)}, u32[]{:S(2)}, u32[]{:S(2)}) collective-permute-start(bf16[3,16,2048]{2,1,0:T(8,128)(2,1)S(1)} %get-tuple-element.18.own_two.other), channel_id=1, source_target_pairs={{8,16},{16,8},{9,17},{17,9},{10,18},{18,10},{11,19},{19,11},{12,20... | collective-permute-start | bytes 589832 | tf_op jit(solution)/shard_map/ppermute | solution.py:496
  4.8 3.5 %collective-permute-start.2 = (bf16[8,2048]{1,0:T(8,128)(2,1)S(1)}, bf16[8,2048]{1,0:T(8,128)(2,1)S(1)}, u32[]{:S(2)}, u32[]{:S(2)}) collective-permute-start(bf16[8,2048]{1,0:T(8,128)(2,1)S(1)} %get-tuple-element.19), channel_id=1, source_target_pairs={{0,1},{2,3},{4,5},{6,7},{1,0},{3,2},{5,4},{7,6},{8,9},{10,11},{12,... | collective-permute-start | bytes 98312 | tf_op jit(solution)/shard_map/ppermute | solution.py:496
  4.9 3.5 %collective-permute-start.3 = (bf16[8,2048]{1,0:T(8,128)(2,1)S(1)}, bf16[8,2048]{1,0:T(8,128)(2,1)S(1)}, u32[]{:S(2)}, u32[]{:S(2)}) collective-permute-start(bf16[8,2048]{1,0:T(8,128)(2,1)S(1)} %get-tuple-element.20), channel_id=1, source_target_pairs={{1,2},{3,4},{5,6},{2,1},{4,3},{6,5},{9,10},{11,12},{13,14},{10,9},... | collective-permute-start | bytes 98312 | tf_op jit(solution)/shard_map/ppermute | solution.py:496
  9.9 18.7 %copy-start = (bf16[512,160]{1,0:T(8,128)(2,1)S(1)}, bf16[512,160]{1,0:T(8,128)(2,1)}, u32[]{:S(2)}) copy-start(bf16[512,160]{1,0:T(8,128)(2,1)} %constant.8.clone.basis) | copy-start | bytes 491524

commit v11 on v10

--- a/solution.py
+++ b/solution.py
@@ -359,9 +359,35 @@
     return transformed(lines, table)
 
 
-def late_kernel(other, plane, row_one, row_two, strain, table, out, ready, lines):
+def level_parts(k, total, spectra, factors):
+    rows = total.shape[0] // 7
+    padded_rows = rows + MARGIN
+    odd = lax.axis_index("gz") % 2
+    sign = jnp.where(odd == k, 1.0, -1.0)
+    pieces = [total[rows * i : rows * (i + 1)] for i in range(7)]
+    for i in range(3):
+        start = 3 * padded_rows + MARGIN * (3 * k + i)
+        pieces[i] = jnp.concatenate([pieces[i], spectra[start : start + MARGIN, :]], axis=0)
+    t01, p11, t12 = pieces[:3]
+    s22, t02, s00, rise = [padded(piece) for piece in pieces[3:]]
+    p11 = up(p11) + down(p11) - 2.0 * p11
+    t01 = up(t01) - down(t01)
+    t12 = 0.25 * (up(t12) - down(t12))
+    flat = spectra[k * padded_rows : (k + 1) * padded_rows, :]
+    s22, rise = sign * s22, sign * rise
+    middle = p11 - 2.0 * s22 + 0.5 * (flat + rise)
+    middle = middle + slope_of(factors, t01) + factors[1:2] * s00
+    cross = sign * (t12 + slope_of(factors, t02))
+    return [s22 + cross, middle, s22 - cross]
+
+
+def late_kernel(
+    other, plane, row_one, row_two, strain, table, spectra, factors,
+    out, ready, lines,
+):
     slopes_at = lambda cells: corrected(0, cells, row_one, row_two, strain)
-    out[...] = stress_lines(slopes_at, other, plane, table, lines)
+    total = stress_lines(slopes_at, other, plane, table, lines)
+    out[...] = jnp.concatenate(level_parts(0, total, spectra, factors), axis=0)
     for step in range(plane.shape[2] // CHUNK):
         cells = pl.ds(step * CHUNK, CHUNK)
         for i, field in enumerate(corrected(1, cells, row_one, row_two, strain)):
@@ -380,26 +406,10 @@
     last = jnp.where(gz == planes - 1, 1.0, 0.0)
     odd = gz % 2
     slopes_at = lambda cells: [ready[i, :, cells] for i in range(7)]
-    totals = (earlier, stress_lines(slopes_at, other, plane, table, lines))
-    parts = []
-    for k in range(2):
-        sign = jnp.where(odd == k, 1.0, -1.0)
-        pieces = [totals[k][rows * i : rows * (i + 1)] for i in range(7)]
-        for i in range(3):
-            start = 3 * padded_rows + MARGIN * (3 * k + i)
-            pieces[i] = jnp.concatenate([pieces[i], spectra[start : start + MARGIN, :]], axis=0)
-        t01, p11, t12 = pieces[:3]
-        s22, t02, s00, rise = [padded(piece) for piece in pieces[3:]]
-        p11 = up(p11) + down(p11) - 2.0 * p11
-        t01 = up(t01) - down(t01)
-        t12 = 0.25 * (up(t12) - down(t12))
-        flat = spectra[k * padded_rows : (k + 1) * padded_rows, :]
-        s22, rise = sign * s22, sign * rise
-        middle = p11 - 2.0 * s22 + 0.5 * (flat + rise)
-        middle = middle + slope_of(factors, t01) + factors[1:2] * s00
-        cross = sign * (t12 + slope_of(factors, t02))
-        parts.append([s22 + cross, middle, s22 - cross])
-
+    parts = [
+        [earlier[padded_rows * i : padded_rows * (i + 1), :] for i in range(3)],
+        level_parts(1, stress_lines(slopes_at, other, plane, table, lines), spectra, factors),
+    ]
     ghost = spectra[2 * padded_rows : 3 * padded_rows, :]
     lower = [jnp.where(odd == 1, p, q) for p, q in zip(*parts)]
     upper = [jnp.where(odd == 1, q, p) for p, q in zip(*parts)]
@@ -571,14 +581,14 @@
     earlier, ready = pl.pallas_call(
         late_kernel,
         out_shape=(
-            jax.ShapeDtypeStruct((7 * rows, 2 * kxr), jnp.float32),
+            jax.ShapeDtypeStruct((3 * (rows + MARGIN), 2 * kxr), jnp.float32),
             jax.ShapeDtypeStruct((7, rows, width), jnp.float32),
         ),
-        in_specs=[VMEM] * 6,
+        in_specs=[VMEM] * 8,
         out_specs=(VMEM,) * 2,
         scratch_shapes=[held],
         compiler_params=limit,
-    )(own_two, plane_one, row_one, row_two, strain, table)
+    )(own_two, plane_one, row_one, row_two, strain, table, spectra, factors)
     outgoing = pl.pallas_call(
         functools.partial(last_kernel, planes, groups, CAP),
         out_shape=jax.ShapeDtypeStruct((planes * groups * reach, 128), jnp.int16),

time: 30.2 us -> 30.2 us (level)
  no operation moved by 1% of the time
where the time goes in v11:
time: 30.2 us; the launch traced here: 29.9 us
  blocking collectives  17.6 us (58%)
  Pallas kernels  7.23 us (24%)
  starting transfers between devices  4.4 us (15%)
  waiting for transfers between devices  0.58 us (2%)
    all_to_all x1, blocking collectives, per_device(): lax.all_to_all(outgoing, ('gz', 'gy'), split_axis=0, concat_axis=0, tiled...  17.6 us
    ppermute x4, starting transfers between devices, exchange(): return lax.ppermute(array, axis, pairs + [(j, i) for i, j in pairs])  4.4 us
    pallas_call x1, Pallas kernels, per_device(): pl.pallas_call(functools.partial(mode_kernel, groups, CAP, kyr, levels, d...  1.58 us
    pallas_call x1, Pallas kernels, per_device(): pl.pallas_call(functools.partial(solve_kernel, kyr, depth, CAP, reach), o...  1.32 us
    pallas_call x1, Pallas kernels, per_device(): pl.pallas_call(functools.partial(early_kernel, groups, planes), out_shape...  1.2 us
    pallas_call x1, Pallas kernels, per_device(): pl.pallas_call(pack_kernel, out_shape=(plane_shape, plane_shape), in_spec...  1.05 us
    pallas_call x1, Pallas kernels, per_device(): pl.pallas_call(functools.partial(last_kernel, planes, groups, CAP), out_s...  1.02 us
    pallas_call x1, Pallas kernels, per_device(): pl.pallas_call(late_kernel, out_shape=(jax.ShapeDtypeStruct((3 * (rows +...  0.96 us
  transfers between devices with their start and end apart: 4, of which 1 were waited for; matrix products, arithmetic and copies ran while one was open for 0% of the time, Pallas kernels for 13%

profile of v11, /device:TPU:0, one launch (start us, length us, event | category | flops | bytes accessed | tf_op | source)
XLA Modules:
  0.0 29.9 jit_solution(12383447058398355780)
XLA Ops:
  0.0 1.0 %shard_map.100 = (bf16[3,16,2048]{2,1,0:T(8,128)(2,1)S(1)}, bf16[3,16,2048]{2,1,0:T(8,128)(2,1)S(1)}) custom-call(bf16[2,16,2048]{2,1,0:T(8,128)(2,1)} %vx.1, bf16[2,16,2048]{2,1,0:T(8,128)(2,1)} %vy.1, bf16[2,16,2048]{2,1,0:T(8,128)(2,1)} %vz.1), custom_call_target="tpu_custom_call" | custom-call | tf_op jit(solution)/shard_map/pallas_call | solution.py:523
  1.1 3.0 %collective-permute-start.1 = (bf16[3,16,2048]{2,1,0:T(8,128)(2,1)S(1)}, bf16[3,16,2048]{2,1,0:T(8,128)(2,1)S(1)}, u32[]{:S(2)}, u32[]{:S(2)}) collective-permute-start(bf16[3,16,2048]{2,1,0:T(8,128)(2,1)S(1)} %get-tuple-element.17.own_one.other), channel_id=1, source_target_pairs={{0,8},{16,24},{8,0},{24,16},{1,9},{17,25},{9,1},{25,17},{2,10},{18... | collective-permute-start | bytes 589832 | tf_op jit(solution)/shard_map/ppermute | solution.py:506
  4.1 0.7 %collective-permute-start = (bf16[3,16,2048]{2,1,0:T(8,128)(2,1)S(1)}, bf16[3,16,2048]{2,1,0:T(8,128)(2,1)S(1)}, u32[]{:S(2)}, u32[]{:S(2)}) collective-permute-start(bf16[3,16,2048]{2,1,0:T(8,128)(2,1)S(1)} %get-tuple-element.18.own_two.other), channel_id=1, source_target_pairs={{8,16},{16,8},{9,17},{17,9},{10,18},{18,10},{11,19},{19,11},{12,20... | collective-permute-start | bytes 589832 | tf_op jit(solution)/shard_map/ppermute | solution.py:506
  4.7 0.1 shard_map.101
  4.8 0.1 collective-permute-start.2
  4.9 0.7 %collective-permute-start.3 = (bf16[8,2048]{1,0:T(8,128)(2,1)S(1)}, bf16[8,2048]{1,0:T(8,128)(2,1)S(1)}, u32[]{:S(2)}, u32[]{:S(2)}) collective-permute-start(bf16[8,2048]{1,0:T(8,128)(2,1)S(1)} %get-tuple-element.20), channel_id=1, source_target_pairs={{1,2},{3,4},{5,6},{2,1},{4,3},{6,5},{9,10},{11,12},{13,14},{10,9},... | collective-permute-start | bytes 98312 | tf_op jit(solution)/shard_map/ppermute | solution.py:506
  5.6 1.6 %shard_map.102 = (s32[8,256]{1,0:T(8,128)S(1)}, f32[2,4,128,128]{3,2,1,0:T(8,128)S(1)}, bf16[2048,256]{1,0:T(8,128)(2,1)S(1)}, f32[2,128]{1,0:T(2,128)S(1)}) custom-call(s32[1,64]{1,0:T(1,128)} %bitcast.6, f32[8]{0:T(128)} %below_hbm.1, f32[8]{0:T(128)} %above_hbm.1, f32[8]{0:T(128)} %metric_hbm.1, bf16[2048,256]{1,0:T(8,128)(2,1)} %constant.6.clone.table_hbm, ...), custom_call_target="tpu_custom_call" | custom-call | tf_op jit(solution)/shard_map/pallas_call | solution.py:548
  7.2 1.2 %shard_map.103 = (f32[2,5,16,2048]{3,2,1,0:T(8,128)S(1)}, f32[120,128]{1,0:T(8,128)S(1)}) custom-call(bf16[3,16,2048]{2,1,0:T(8,128)(2,1)S(1)} %get-tuple-element.17.own_one.other, bf16[3,16,2048]{2,1,0:T(8,128)(2,1)S(1)} %get-tuple-element.18.own_two.other, bf16[2048,256]{1,0:T(8,128)(2,1)S(1)} %get-tuple-element.21.table, ...), custom_call_target="tpu_custom_call" | custom-call | tf_op jit(solution)/shard_map/pallas_call | solution.py:567
  8.4 0.0 collective-permute-done.2.row_one
  8.4 0.0 collective-permute-done.3.row_two
  8.4 0.6 %collective-permute-done.1.plane = bf16[3,16,2048]{2,1,0:T(8,128)(2,1)S(1)} collective-permute-done((bf16[3,16,2048]{2,1,0:T(8,128)(2,1)S(1)}, bf16[3,16,2048]{2,1,0:T(8,128)(2,1)S(1)}, u32[]{:S(2)}, u32[]{:S(2)}) %collective-permute-start.1) | collective-permute-done | bytes 196640 | tf_op jit(solution)/shard_map/ppermute | solution.py:506
  9.0 1.0 %shard_map.104 = (f32[72,128]{1,0:T(8,128)S(1)}, f32[7,16,2048]{2,1,0:T(8,128)S(1)}) custom-call(bf16[3,16,2048]{2,1,0:T(8,128)(2,1)S(1)} %get-tuple-element.18.own_two.other, bf16[3,16,2048]{2,1,0:T(8,128)(2,1)S(1)} %collective-permute-done.1.plane, bf16[8,2048]{1,0:T(8,128)(2,1)S(1)} %collective-permute-done.2.row_one, ...), custom_call_target="tpu_custom_call" | custom-call | tf_op jit(solution)/shard_map/pallas_call | solution.py:581
  9.9 0.0 collective-permute-done.plane
  9.9 0.0 copy-start
  9.9 1.0 %shard_map.105 = s16[640,128]{1,0:T(8,128)(2,1)S(1)} custom-call(bf16[3,16,2048]{2,1,0:T(8,128)(2,1)S(1)} %get-tuple-element.17.own_one.other, bf16[3,16,2048]{2,1,0:T(8,128)(2,1)S(1)} %collective-permute-done.plane, f32[7,16,2048]{2,1,0:T(8,128)S(1)} %get-tuple-element.25.ready, bf16[2048,256]{1,0:T(8,128)(2,1)S(1)} %get-tuple-element.21.table, ...), custom_call_target="tpu_custom_call" | custom-call | tf_op jit(solution)/shard_map/pallas_call | solution.py:592
  11.0 17.6 %all_to_all.5 = s16[32,10,2,128]{3,2,1,0:T(2,128)(2,1)S(1)} all-to-all(s16[32,10,2,128]{3,2,1,0:T(2,128)(2,1)S(1)} %bitcast.4), channel_id=1, replica_groups=mesh['gz'=4,'gy'=8] {'gz','gy'}, dimensions={0} | all-to-all | bytes 327680 | tf_op jit(solution)/shard_map/all_to_all | solution.py:601
  28.6 0.0 copy-done
  28.6 1.3 %shard_map.106 = f32[32,2,128]{2,1,0:T(2,128)} custom-call(s16[640,128]{1,0:T(8,128)(2,1)S(1)} %bitcast.5, bf16[512,160]{1,0:T(8,128)(2,1)S(1)} %copy-done, f32[2,4,128,128]{3,2,1,0:T(8,128)S(1)} %get-tuple-element.28.green), custom_call_target="tpu_custom_call" | custom-call | tf_op jit(solution)/shard_map/pallas_call | solution.py:605
Async XLA Ops:
  1.1 7.9 %collective-permute-start.1 = (bf16[3,16,2048]{2,1,0:T(8,128)(2,1)S(1)}, bf16[3,16,2048]{2,1,0:T(8,128)(2,1)S(1)}, u32[]{:S(2)}, u32[]{:S(2)}) collective-permute-start(bf16[3,16,2048]{2,1,0:T(8,128)(2,1)S(1)} %get-tuple-element.17.own_one.other), channel_id=1, source_target_pairs={{0,8},{16,24},{8,0},{24,16},{1,9},{17,25},{9,1},{25,17},{2,10},{18... | collective-permute-start | bytes 589832 | tf_op jit(solution)/shard_map/ppermute | solution.py:506
  4.1 5.9 %collective-permute-start = (bf16[3,16,2048]{2,1,0:T(8,128)(2,1)S(1)}, bf16[3,16,2048]{2,1,0:T(8,128)(2,1)S(1)}, u32[]{:S(2)}, u32[]{:S(2)}) collective-permute-start(bf16[3,16,2048]{2,1,0:T(8,128)(2,1)S(1)} %get-tuple-element.18.own_two.other), channel_id=1, source_target_pairs={{8,16},{16,8},{9,17},{17,9},{10,18},{18,10},{11,19},{19,11},{12,20... | collective-permute-start | bytes 589832 | tf_op jit(solution)/shard_map/ppermute | solution.py:506
  4.8 3.6 %collective-permute-start.2 = (bf16[8,2048]{1,0:T(8,128)(2,1)S(1)}, bf16[8,2048]{1,0:T(8,128)(2,1)S(1)}, u32[]{:S(2)}, u32[]{:S(2)}) collective-permute-start(bf16[8,2048]{1,0:T(8,128)(2,1)S(1)} %get-tuple-element.19), channel_id=1, source_target_pairs={{0,1},{2,3},{4,5},{6,7},{1,0},{3,2},{5,4},{7,6},{8,9},{10,11},{12,... | collective-permute-start | bytes 98312 | tf_op jit(solution)/shard_map/ppermute | solution.py:506
  4.9 3.5 %collective-permute-start.3 = (bf16[8,2048]{1,0:T(8,128)(2,1)S(1)}, bf16[8,2048]{1,0:T(8,128)(2,1)S(1)}, u32[]{:S(2)}, u32[]{:S(2)}) collective-permute-start(bf16[8,2048]{1,0:T(8,128)(2,1)S(1)} %get-tuple-element.20), channel_id=1, source_target_pairs={{1,2},{3,4},{5,6},{2,1},{4,3},{6,5},{9,10},{11,12},{13,14},{10,9},... | collective-permute-start | bytes 98312 | tf_op jit(solution)/shard_map/ppermute | solution.py:506
  9.9 18.6 %copy-start = (bf16[512,160]{1,0:T(8,128)(2,1)S(1)}, bf16[512,160]{1,0:T(8,128)(2,1)}, u32[]{:S(2)}) copy-start(bf16[512,160]{1,0:T(8,128)(2,1)} %constant.8.clone.basis) | copy-start | bytes 491524

commit v12 on v11

--- a/solution.py
+++ b/solution.py
@@ -315,7 +315,7 @@
         spectra[start : start + piece.shape[0], :] = piece
 
 
-def corrected(k, cells, row_one, row_two, strain):
+def corrected(k, cells, other, row_one, row_two, strain):
     rows = strain.shape[2]
     odd_row = lax.axis_index("gy") % 2
     sign = jnp.where(lax.axis_index("gz") % 2 == k, 1.0, -1.0)
@@ -336,22 +336,20 @@
     e01 = strain[k, 2, :, cells] + beyond(0)
     sy2 = strain[k, 4, :, cells] + sign * beyond(2)
     flat = 0.5 * (x0 * x0 + y1 * y1) + 0.25 * (e01 * e01) + STRAIN_FLOOR
-    return x0, y1, e01, sx2, sy2, flat, sign * edge
-
-
-def stress_lines(slopes_at, other, plane, table, lines):
+    across = [other[i, :, cells].astype(jnp.float32) for i in range(3)]
+    return x0, y1, e01, sx2 - across[0], sy2 - across[1], flat, sign * edge, across[2]
+
+
+def stress_lines(slopes_at, plane, table, lines):
     def fields_at(step):
         cells = pl.ds(step * CHUNK, CHUNK)
-        x0, y1, e01, sx2, sy2, flat, edge = slopes_at(cells)
-        z = [
-            plane[i, :, cells].astype(jnp.float32) - other[i, :, cells].astype(jnp.float32)
-            for i in range(3)
-        ]
-        e02, e12 = z[0] + sx2, z[1] + sy2
-        squared = flat + 0.5 * (z[2] * z[2]) + 0.25 * (e02 * e02 + e12 * e12)
+        x0, y1, e01, sx2, sy2, flat, edge, across = slopes_at(cells)
+        near = [plane[i, :, cells].astype(jnp.float32) for i in range(3)]
+        e02, e12, rise = near[0] + sx2, near[1] + sy2, near[2] - across
+        squared = flat + 0.5 * (rise * rise) + 0.25 * (e02 * e02 + e12 * e12)
         viscous = magnitude(squared)
-        fields = [viscous * field for field in (e01, y1, e12, z[2], e02, x0)]
-        return fields + [z[2] + edge]
+        fields = [viscous * field for field in (e01, y1, e12, rise, e02, x0)]
+        return fields + [rise + edge]
 
     steps = plane.shape[2] // CHUNK // 2
     for step in range(steps):
@@ -382,33 +380,33 @@
 
 
 def late_kernel(
-    other, plane, row_one, row_two, strain, table, spectra, factors,
+    own_one, own_two, plane, row_one, row_two, strain, table, spectra, factors,
     out, ready, lines,
 ):
-    slopes_at = lambda cells: corrected(0, cells, row_one, row_two, strain)
-    total = stress_lines(slopes_at, other, plane, table, lines)
+    slopes_at = lambda cells: corrected(0, cells, own_two, row_one, row_two, strain)
+    total = stress_lines(slopes_at, plane, table, lines)
     out[...] = jnp.concatenate(level_parts(0, total, spectra, factors), axis=0)
     for step in range(plane.shape[2] // CHUNK):
         cells = pl.ds(step * CHUNK, CHUNK)
-        for i, field in enumerate(corrected(1, cells, row_one, row_two, strain)):
+        for i, field in enumerate(corrected(1, cells, own_one, row_one, row_two, strain)):
             ready[i, :, cells] = field
 
 
 def last_kernel(
     planes, groups, capacity,
-    other, plane, ready, table, earlier, spectra, factors, pick,
+    plane, ready, table, earlier, spectra, factors, pick,
     out, lines, codes,
 ):
-    rows = other.shape[1]
+    rows = plane.shape[1]
     padded_rows = rows + MARGIN
     gz = lax.axis_index("gz")
     first = jnp.where(gz == 0, 1.0, 0.0)
     last = jnp.where(gz == planes - 1, 1.0, 0.0)
     odd = gz % 2
-    slopes_at = lambda cells: [ready[i, :, cells] for i in range(7)]
+    slopes_at = lambda cells: [ready[i, :, cells] for i in range(8)]
     parts = [
         [earlier[padded_rows * i : padded_rows * (i + 1), :] for i in range(3)],
-        level_parts(1, stress_lines(slopes_at, other, plane, table, lines), spectra, factors),
+        level_parts(1, stress_lines(slopes_at, plane, table, lines), spectra, factors),
     ]
     ghost = spectra[2 * padded_rows : 3 * padded_rows, :]
     lower = [jnp.where(odd == 1, p, q) for p, q in zip(*parts)]
@@ -582,21 +580,21 @@
         late_kernel,
         out_shape=(
             jax.ShapeDtypeStruct((3 * (rows + MARGIN), 2 * kxr), jnp.float32),
-            jax.ShapeDtypeStruct((7, rows, width), jnp.float32),
+            jax.ShapeDtypeStruct((8, rows, width), jnp.float32),
         ),
-        in_specs=[VMEM] * 8,
+        in_specs=[VMEM] * 9,
         out_specs=(VMEM,) * 2,
         scratch_shapes=[held],
         compiler_params=limit,
-    )(own_two, plane_one, row_one, row_two, strain, table, spectra, factors)
+    )(own_one, own_two, plane_one, row_one, row_two, strain, table, spectra, factors)
     outgoing = pl.pallas_call(
         functools.partial(last_kernel, planes, groups, CAP),
         out_shape=jax.ShapeDtypeStruct((planes * groups * reach, 128), jnp.int16),
-        in_specs=[VMEM] * 8,
+        in_specs=[VMEM] * 7,
         out_specs=VMEM,
         scratch_shapes=[held, pltpu.VMEM((groups * reach, 128), jnp.float32)],
         compiler_params=limit,
-    )(own_one, plane_two, ready, table, earlier, spectra, factors, pick)
+    )(plane_two, ready, table, earlier, spectra, factors, pick)
     outgoing = outgoing.reshape(planes * groups, reach // 2, 2, 128)
     received = lax.all_to_all(outgoing, ("gz", "gy"), split_axis=0, concat_axis=0, tiled=True)
     received = received.reshape(planes * groups * reach, 128)

time: 30.2 us -> 30.2 us (level)
  no operation moved by 1% of the time
where the time goes in v12:
time: 30.2 us; the launch traced here: 29.9 us
  blocking collectives  17.6 us (58%)
  Pallas kernels  7.23 us (24%)
  starting transfers between devices  4.4 us (15%)
  waiting for transfers between devices  0.58 us (2%)
    all_to_all x1, blocking collectives, per_device(): lax.all_to_all(outgoing, ('gz', 'gy'), split_axis=0, concat_axis=0, tiled...  17.6 us
    ppermute x4, starting transfers between devices, exchange(): return lax.ppermute(array, axis, pairs + [(j, i) for i, j in pairs])  4.4 us
    pallas_call x1, Pallas kernels, per_device(): pl.pallas_call(functools.partial(mode_kernel, groups, CAP, kyr, levels, d...  1.58 us
    pallas_call x1, Pallas kernels, per_device(): pl.pallas_call(functools.partial(solve_kernel, kyr, depth, CAP, reach), o...  1.31 us
    pallas_call x1, Pallas kernels, per_device(): pl.pallas_call(functools.partial(early_kernel, groups, planes), out_shape...  1.2 us
    pallas_call x1, Pallas kernels, per_device(): pl.pallas_call(pack_kernel, out_shape=(plane_shape, plane_shape), in_spec...  1.05 us
    pallas_call x1, Pallas kernels, per_device(): pl.pallas_call(late_kernel, out_shape=(jax.ShapeDtypeStruct((3 * (rows +...  1.02 us
    pallas_call x1, Pallas kernels, per_device(): pl.pallas_call(functools.partial(last_kernel, planes, groups, CAP), out_s...  0.98 us
  transfers between devices with their start and end apart: 4, of which 1 were waited for; matrix products, arithmetic and copies ran while one was open for 0% of the time, Pallas kernels for 13%

profile of v12, /device:TPU:0, one launch (start us, length us, event | category | flops | bytes accessed | tf_op | source)
XLA Modules:
  0.0 29.9 jit_solution(1184164924519999386)
XLA Ops:
  0.0 1.0 %shard_map.100 = (bf16[3,16,2048]{2,1,0:T(8,128)(2,1)S(1)}, bf16[3,16,2048]{2,1,0:T(8,128)(2,1)S(1)}) custom-call(bf16[2,16,2048]{2,1,0:T(8,128)(2,1)} %vx.1, bf16[2,16,2048]{2,1,0:T(8,128)(2,1)} %vy.1, bf16[2,16,2048]{2,1,0:T(8,128)(2,1)} %vz.1), custom_call_target="tpu_custom_call" | custom-call | tf_op jit(solution)/shard_map/pallas_call | solution.py:521
  1.1 3.0 %collective-permute-start.1 = (bf16[3,16,2048]{2,1,0:T(8,128)(2,1)S(1)}, bf16[3,16,2048]{2,1,0:T(8,128)(2,1)S(1)}, u32[]{:S(2)}, u32[]{:S(2)}) collective-permute-start(bf16[3,16,2048]{2,1,0:T(8,128)(2,1)S(1)} %get-tuple-element.18.own_one), channel_id=1, source_target_pairs={{0,8},{16,24},{8,0},{24,16},{1,9},{17,25},{9,1},{25,17},{2,10},{18... | collective-permute-start | bytes 589832 | tf_op jit(solution)/shard_map/ppermute | solution.py:504
  4.1 0.7 %collective-permute-start = (bf16[3,16,2048]{2,1,0:T(8,128)(2,1)S(1)}, bf16[3,16,2048]{2,1,0:T(8,128)(2,1)S(1)}, u32[]{:S(2)}, u32[]{:S(2)}) collective-permute-start(bf16[3,16,2048]{2,1,0:T(8,128)(2,1)S(1)} %get-tuple-element.17.own_two), channel_id=1, source_target_pairs={{8,16},{16,8},{9,17},{17,9},{10,18},{18,10},{11,19},{19,11},{12,20... | collective-permute-start | bytes 589832 | tf_op jit(solution)/shard_map/ppermute | solution.py:504
  4.7 0.1 shard_map.101
  4.8 0.1 collective-permute-start.2
  4.9 0.7 %collective-permute-start.3 = (bf16[8,2048]{1,0:T(8,128)(2,1)S(1)}, bf16[8,2048]{1,0:T(8,128)(2,1)S(1)}, u32[]{:S(2)}, u32[]{:S(2)}) collective-permute-start(bf16[8,2048]{1,0:T(8,128)(2,1)S(1)} %get-tuple-element.20), channel_id=1, source_target_pairs={{1,2},{3,4},{5,6},{2,1},{4,3},{6,5},{9,10},{11,12},{13,14},{10,9},... | collective-permute-start | bytes 98312 | tf_op jit(solution)/shard_map/ppermute | solution.py:504
  5.6 1.6 %shard_map.102 = (s32[8,256]{1,0:T(8,128)S(1)}, f32[2,4,128,128]{3,2,1,0:T(8,128)S(1)}, bf16[2048,256]{1,0:T(8,128)(2,1)S(1)}, f32[2,128]{1,0:T(2,128)S(1)}) custom-call(s32[1,64]{1,0:T(1,128)} %bitcast.6, f32[8]{0:T(128)} %below_hbm.1, f32[8]{0:T(128)} %above_hbm.1, f32[8]{0:T(128)} %metric_hbm.1, bf16[2048,256]{1,0:T(8,128)(2,1)} %constant.6.clone.table_hbm, ...), custom_call_target="tpu_custom_call" | custom-call | tf_op jit(solution)/shard_map/pallas_call | solution.py:546
  7.2 1.2 %shard_map.103 = (f32[2,5,16,2048]{3,2,1,0:T(8,128)S(1)}, f32[120,128]{1,0:T(8,128)S(1)}) custom-call(bf16[3,16,2048]{2,1,0:T(8,128)(2,1)S(1)} %get-tuple-element.18.own_one, bf16[3,16,2048]{2,1,0:T(8,128)(2,1)S(1)} %get-tuple-element.17.own_two, bf16[2048,256]{1,0:T(8,128)(2,1)S(1)} %get-tuple-element.21.table, f32[2,128]{1,0:T(2,128)S(1)} %get-tuple-element.22.factors), custom_call_target="tpu_custom_call" | custom-call | tf_op jit(solution)/shard_map/pallas_call | solution.py:565
  8.4 0.0 collective-permute-done.2.row_one
  8.4 0.0 collective-permute-done.3.row_two
  8.4 0.6 %collective-permute-done.1.plane = bf16[3,16,2048]{2,1,0:T(8,128)(2,1)S(1)} collective-permute-done((bf16[3,16,2048]{2,1,0:T(8,128)(2,1)S(1)}, bf16[3,16,2048]{2,1,0:T(8,128)(2,1)S(1)}, u32[]{:S(2)}, u32[]{:S(2)}) %collective-permute-start.1) | collective-permute-done | bytes 196640 | tf_op jit(solution)/shard_map/ppermute | solution.py:504
  9.0 1.0 %shard_map.104 = (f32[72,128]{1,0:T(8,128)S(1)}, f32[8,16,2048]{2,1,0:T(8,128)S(1)}) custom-call(bf16[3,16,2048]{2,1,0:T(8,128)(2,1)S(1)} %get-tuple-element.18.own_one, bf16[3,16,2048]{2,1,0:T(8,128)(2,1)S(1)} %get-tuple-element.17.own_two, bf16[3,16,2048]{2,1,0:T(8,128)(2,1)S(1)} %collective-permute-done.1.plane, ...), custom_call_target="tpu_custom_call" | custom-call | tf_op jit(solution)/shard_map/pallas_call | solution.py:579
  10.0 0.0 collective-permute-done.plane
  10.0 0.0 copy-start
  10.0 1.0 %shard_map.105 = s16[640,128]{1,0:T(8,128)(2,1)S(1)} custom-call(bf16[3,16,2048]{2,1,0:T(8,128)(2,1)S(1)} %collective-permute-done.plane, f32[8,16,2048]{2,1,0:T(8,128)S(1)} %get-tuple-element.25.ready, bf16[2048,256]{1,0:T(8,128)(2,1)S(1)} %get-tuple-element.21.table, f32[72,128]{1,0:T(8,128)S(1)} %get-tuple-element.26.earlier, ...), custom_call_target="tpu_custom_call" | custom-call | tf_op jit(solution)/shard_map/pallas_call | solution.py:590
  11.0 17.6 %all_to_all.5 = s16[32,10,2,128]{3,2,1,0:T(2,128)(2,1)S(1)} all-to-all(s16[32,10,2,128]{3,2,1,0:T(2,128)(2,1)S(1)} %bitcast.4), channel_id=1, replica_groups=mesh['gz'=4,'gy'=8] {'gz','gy'}, dimensions={0} | all-to-all | bytes 327680 | tf_op jit(solution)/shard_map/all_to_all | solution.py:599
  28.5 0.0 copy-done
  28.5 1.3 %shard_map.106 = f32[32,2,128]{2,1,0:T(2,128)} custom-call(s16[640,128]{1,0:T(8,128)(2,1)S(1)} %bitcast.5, bf16[512,160]{1,0:T(8,128)(2,1)S(1)} %copy-done, f32[2,4,128,128]{3,2,1,0:T(8,128)S(1)} %get-tuple-element.28.green), custom_call_target="tpu_custom_call" | custom-call | tf_op jit(solution)/shard_map/pallas_call | solution.py:603
Async XLA Ops:
  1.1 7.9 %collective-permute-start.1 = (bf16[3,16,2048]{2,1,0:T(8,128)(2,1)S(1)}, bf16[3,16,2048]{2,1,0:T(8,128)(2,1)S(1)}, u32[]{:S(2)}, u32[]{:S(2)}) collective-permute-start(bf16[3,16,2048]{2,1,0:T(8,128)(2,1)S(1)} %get-tuple-element.18.own_one), channel_id=1, source_target_pairs={{0,8},{16,24},{8,0},{24,16},{1,9},{17,25},{9,1},{25,17},{2,10},{18... | collective-permute-start | bytes 589832 | tf_op jit(solution)/shard_map/ppermute | solution.py:504
  4.1 5.9 %collective-permute-start = (bf16[3,16,2048]{2,1,0:T(8,128)(2,1)S(1)}, bf16[3,16,2048]{2,1,0:T(8,128)(2,1)S(1)}, u32[]{:S(2)}, u32[]{:S(2)}) collective-permute-start(bf16[3,16,2048]{2,1,0:T(8,128)(2,1)S(1)} %get-tuple-element.17.own_two), channel_id=1, source_target_pairs={{8,16},{16,8},{9,17},{17,9},{10,18},{18,10},{11,19},{19,11},{12,20... | collective-permute-start | bytes 589832 | tf_op jit(solution)/shard_map/ppermute | solution.py:504
  4.8 3.6 %collective-permute-start.2 = (bf16[8,2048]{1,0:T(8,128)(2,1)S(1)}, bf16[8,2048]{1,0:T(8,128)(2,1)S(1)}, u32[]{:S(2)}, u32[]{:S(2)}) collective-permute-start(bf16[8,2048]{1,0:T(8,128)(2,1)S(1)} %get-tuple-element.19), channel_id=1, source_target_pairs={{0,1},{2,3},{4,5},{6,7},{1,0},{3,2},{5,4},{7,6},{8,9},{10,11},{12,... | collective-permute-start | bytes 98312 | tf_op jit(solution)/shard_map/ppermute | solution.py:504
  4.9 3.5 %collective-permute-start.3 = (bf16[8,2048]{1,0:T(8,128)(2,1)S(1)}, bf16[8,2048]{1,0:T(8,128)(2,1)S(1)}, u32[]{:S(2)}, u32[]{:S(2)}) collective-permute-start(bf16[8,2048]{1,0:T(8,128)(2,1)S(1)} %get-tuple-element.20), channel_id=1, source_target_pairs={{1,2},{3,4},{5,6},{2,1},{4,3},{6,5},{9,10},{11,12},{13,14},{10,9},... | collective-permute-start | bytes 98312 | tf_op jit(solution)/shard_map/ppermute | solution.py:504
  10.0 18.6 %copy-start = (bf16[512,160]{1,0:T(8,128)(2,1)S(1)}, bf16[512,160]{1,0:T(8,128)(2,1)}, u32[]{:S(2)}) copy-start(bf16[512,160]{1,0:T(8,128)(2,1)} %constant.8.clone.basis) | copy-start | bytes 491524
